TPU v7x, 32 devices: a whole 2x2x4 slice. The times are simulated.
32 devices in a mesh: seq: 8 (over z, core), dp: 4 (over y, x).
Axes of the slice: x: 2, y: 2, z: 4, core: 2. Of those that a mesh axis runs over, the one named last changes fastest.
Arguments:
- skip_input: bfloat16 [8, 2048, 768], P('dp', 'seq'), may hold values from -6 to 6
- upstream: bfloat16 [8, 2048, 1280], P('dp', 'seq'), may hold values from -6 to 6
- proj_weight: bfloat16 [768, 1280], replicated, may hold values from -0.21875 to 0.21875
- depth_kernel: float32 [3, 1280], replicated, may hold values from -3 to 3
Outputs:
- input_grad: bfloat16 [8, 2048, 768], P('dp', 'seq')
- weight_grad: float32 [768, 1280], P('dp', 'seq')
All inputs are finite; a program needn't handle non-finite values.
Results may differ from a plain program's by a relative error of at most 0.0053.
Values may be sent and summed in bfloat16 or wider, within the bound.
No kernel may reach another device: no remote copies, remote signals or barrier semaphores. Data moves between devices by JAX's collectives and lax.ppermute only.
A program may use at most 64 MiB of HBM per device.

v0:
```python
import jax
import jax.numpy as jnp
from jax import lax
from jax.sharding import PartitionSpec as P


def padded_2(block, sides, width):
    for axis, dim in sides:
        count = lax.axis_size(axis)
        forward = [(i, i + 1) for i in range(count - 1)]
        backward = [(target, source) for source, target in forward]
        low = lax.ppermute(
            lax.slice_in_dim(block, block.shape[dim] - width, None, axis=dim), axis, forward
        )
        high = lax.ppermute(lax.slice_in_dim(block, 0, width, axis=dim), axis, backward)
        block = jnp.concatenate([low, block, high], axis=dim)
    return block


def gelu_slope(pre, scaled):
    return jax.vjp(jax.nn.gelu, pre)[1](scaled)[0]


def on_device(skip_input, upstream, proj_weight, depth_kernel):
    batch = skip_input.shape[0]
    k_left = depth_kernel[0]
    k_mid = depth_kernel[1]
    k_right = depth_kernel[2]
    proj = jnp.einsum(
        "bpc,cf->bpf", skip_input, proj_weight, preferred_element_type=jnp.float32
    ).astype(jnp.bfloat16)
    padded = padded_2(proj, (("seq", 1),), 1)
    proj_wide = padded.astype(jnp.float32)
    before = proj_wide[:, :-2]
    centre = proj_wide[:, 1:-1]
    after = proj_wide[:, 2:]
    halved = 0.5 * upstream.astype(jnp.float32)
    slope_fwd = gelu_slope(k_left * before + k_mid * centre + k_right * after, halved)
    slope_rev = gelu_slope(k_right * before + k_mid * centre + k_left * after, halved)
    slopes = padded_2(jnp.stack([slope_fwd, slope_rev]), (("seq", 2),), 1)
    fwd_wide = slopes[0]
    rev_wide = slopes[1]
    grad_proj = (
        k_left * (fwd_wide[:, 2:] + rev_wide[:, :-2])
        + k_mid * (fwd_wide[:, 1:-1] + rev_wide[:, 1:-1])
        + k_right * (fwd_wide[:, :-2] + rev_wide[:, 2:])
    ).astype(jnp.bfloat16)
    input_grad = jnp.einsum(
        "bpf,cf->bpc", grad_proj, proj_weight, preferred_element_type=jnp.float32
    ).astype(jnp.bfloat16)
    partial_value = lax.dot_general(
        skip_input, grad_proj, (((0, 1), (0, 1)), ((), ())), preferred_element_type=jnp.float32
    )
    samples = batch * lax.axis_size("dp")
    section_one = lax.psum_scatter(partial_value, "seq", scatter_dimension=1, tiled=True)
    reduced = lax.psum_scatter(section_one, "dp", scatter_dimension=0, tiled=True)
    return (input_grad, reduced / samples)


def solution(mesh):
    return jax.shard_map(
        on_device,
        mesh=mesh,
        in_specs=(P("dp", "seq", None), P("dp", "seq", None), P(), P()),
        out_specs=(P("dp", "seq", None), P("dp", "seq")),
        check_vma=False,
    )
```

profile of v0, /device:TPU:0, one launch (start us, length us, event | category | flops | bytes accessed | tf_op | source)
XLA Modules:
  0.0 122.1 jit_solution(14599971307436669772)
XLA Ops:
  7.2 0.0 copy-start
  7.2 0.0 copy-start.2
  7.2 0.0 reduce-scatter.5.cloned.1.call-start
  7.2 1.5 %copy-done = bf16[768,1280]{1,0:T(8,128)(2,1)S(1)} copy-done((bf16[768,1280]{1,0:T(8,128)(2,1)S(1)}, bf16[768,1280]{1,0:T(8,128)(2,1)}, u32[]{:S(2)}) %copy-start) | copy-done | bytes 1966104
  8.7 2.3 %convolution_convert_fusion = bf16[2,256,1280]{2,1,0:T(8,128)(2,1)S(1)} fusion(bf16[2,256,768]{2,1,0:T(8,128)(2,1)} %param.4, bf16[768,1280]{1,0:T(8,128)(2,1)S(1)} %copy-done), kind=kOutput, calls=%fused_computation.6 | convolution fusion | flops 1007288320 | bytes 4063232 | tf_op jit(solution)/shard_map/bpc,cf->bpf/dot_general | solution.py:29
  11.0 0.0 copy-start.1
  11.1 2.5 %collective-permute-start = (bf16[2,1,1280]{2,1,0:T(2,128)(2,1)S(1)}, bf16[2,1,1280]{2,1,0:T(2,128)(2,1)S(1)}, u32[]{:S(2)}, u32[]{:S(2)}) collective-permute-start(bf16[2,1,1280]{2,1,0:T(2,128)(2,1)S(1)} %get-tuple-element.11), channel_id=1, source_target_pairs={{0,4},{4,8},{8,12},{12,16},{16,20},{20,24},{24,28},{1,5},{5,9},{9,... | collective-permute-start | bytes 15368 | tf_op jit(solution)/shard_map/ppermute | solution.py:12
  13.6 1.3 %collective-permute-start.1 = (bf16[2,1,1280]{2,1,0:T(2,128)(2,1)S(1)}, bf16[2,1,1280]{2,1,0:T(2,128)(2,1)S(1)}, u32[]{:S(2)}, u32[]{:S(2)}) collective-permute-start(bf16[2,1,1280]{2,1,0:T(2,128)(2,1)S(1)} %get-tuple-element.12), channel_id=1, source_target_pairs={{4,0},{8,4},{12,8},{16,12},{20,16},{24,20},{28,24},{5,1},{9,5},{13... | collective-permute-start | bytes 15368 | tf_op jit(solution)/shard_map/ppermute | solution.py:15
  14.9 0.0 copy-done.2
  14.9 0.0 collective-permute-done
  14.9 3.9 %collective-permute-done.1 = bf16[2,1,1280]{2,1,0:T(2,128)(2,1)S(1)} collective-permute-done((bf16[2,1,1280]{2,1,0:T(2,128)(2,1)S(1)}, bf16[2,1,1280]{2,1,0:T(2,128)(2,1)S(1)}, u32[]{:S(2)}, u32[]{:S(2)}) %collective-permute-start.1) | collective-permute-done | bytes 5152 | tf_op jit(solution)/shard_map/ppermute | solution.py:15
  18.8 0.3 maximum_convert_fusion
  19.1 0.0 copy-done.1
  19.1 4.7 %fusion.6 = (f32[1,2,256,1280]{3,2,1,0:T(8,128)S(1)}, f32[1,2,256,1280]{3,2,1,0:T(8,128)S(1)}) fusion(bf16[2,256,1280]{2,1,0:T(8,128)(2,1)S(1)} %copy-done.1, f32[2,258,1280]{2,1,0:T(8,128)S(1)} %maximum_convert_fusion, f32[1280]{0:T(1024)S(1)} %get-tuple-element.3, f32[1280]{0:T(1024)S(1)} %get-tuple-element.4, f32[1280]{0:T(1024)S(1)} %get-tuple-element.2), kind=kLoop, calls=%fused_computation.15 | loop fusion | flops 32112640 | bytes 14433280 | tf_op jit(solution)/shard_map/stack | solution.py:40
  23.9 4.3 %collective-permute-start.2 = (f32[2,2,1,1280]{3,2,1,0:T(1,128)S(1)}, f32[2,2,1,1280]{3,2,1,0:T(1,128)S(1)}, u32[]{:S(2)}, u32[]{:S(2)}) collective-permute-start(f32[2,2,1,1280]{3,2,1,0:T(1,128)S(1)} %get-tuple-element.7), channel_id=1, source_target_pairs={{0,4},{4,8},{8,12},{12,16},{16,20},{20,24},{24,28},{1,5},{5,9},{9,... | collective-permute-start | bytes 61448 | tf_op jit(solution)/shard_map/ppermute | solution.py:12
  28.3 1.3 %collective-permute-start.3 = (f32[2,2,1,1280]{3,2,1,0:T(1,128)S(1)}, f32[2,2,1,1280]{3,2,1,0:T(1,128)S(1)}, u32[]{:S(2)}, u32[]{:S(2)}) collective-permute-start(f32[2,2,1,1280]{3,2,1,0:T(1,128)S(1)} %get-tuple-element.8), channel_id=1, source_target_pairs={{4,0},{8,4},{12,8},{16,12},{20,16},{24,20},{28,24},{5,1},{9,5},{13... | collective-permute-start | bytes 61448 | tf_op jit(solution)/shard_map/ppermute | solution.py:15
  29.6 0.0 collective-permute-done.2
  29.6 1.8 %collective-permute-done.3 = f32[2,2,1,1280]{3,2,1,0:T(1,128)S(1)} collective-permute-done((f32[2,2,1,1280]{3,2,1,0:T(1,128)S(1)}, f32[2,2,1,1280]{3,2,1,0:T(1,128)S(1)}, u32[]{:S(2)}, u32[]{:S(2)}) %collective-permute-start.3) | collective-permute-done | bytes 20512 | tf_op jit(solution)/shard_map/ppermute | solution.py:15
  31.3 0.5 pad_maximum_fusion
  31.9 0.3 slice_bitcast_fusion.1
  32.2 0.0 copy-start.3
  32.2 1.4 %fusion.16 = bf16[2,256,1280]{2,1,0:T(8,128)(2,1)S(1)} fusion(f32[2,258,1280]{2,1,0:T(8,128)S(1)} %get-tuple-element.6, f32[2,258,1280]{2,1,0:T(8,128)S(1)} %get-tuple-element.5, f32[1280]{0:T(1024)S(1)} %get-tuple-element.3, f32[1280]{0:T(1024)S(1)} %get-tuple-element.4, f32[1280]{0:T(1024)S(1)} %get-tuple-element.2), kind=kLoop, calls=%fused_computation.26 | loop fusion | flops 5898240 | bytes 17054720 | tf_op jit(solution)/shard_map/convert_element_type | solution.py:47
  33.7 0.0 copy-done.3
  33.7 3.1 %convolution_bitcast_fusion = f32[768,1280]{0,1:T(8,128)} fusion(bf16[2,256,1280]{2,1,0:T(8,128)(2,1)S(1)} %fusion.16, bf16[2,256,768]{2,1,0:T(8,128)(2,1)S(1)} %copy-done.3), kind=kOutput, calls=%fused_computation.1 | convolution fusion | flops 1006632960 | bytes 6029312 | tf_op jit(solution)/shard_map/dot_general | solution.py:51
  36.7 0.0 reduce-scatter.5.cloned.1.call-update
  36.8 0.0 reduce-scatter.7.cloned.1.call-start
  36.8 49.6 %reduce-scatter.5.cloned.1.call-done = f32[768,160]{0,1:T(8,128)} async-done(((f32[768,1280]{0,1:T(8,128)}), f32[768,160]{0,1:T(8,128)}) %reduce-scatter.5.cloned.1.call-update) | async-done | bytes 491536 | tf_op jit(solution)/shard_map/reduce_scatter | solution.py:55
  86.4 2.2 %copy.9 = f32[768,160]{1,0:T(8,128)} copy(f32[768,160]{0,1:T(8,128)} %reduce-scatter.5.cloned.1.call-done) | data formatting | bytes 983040
  88.6 0.0 reduce-scatter.7.cloned.1.call-update
  88.6 2.1 %fusion.23 = bf16[2,256,768]{2,1,0:T(8,128)(2,1)} fusion(bf16[2,256,1280]{2,1,0:T(8,128)(2,1)S(1)} %fusion.16, bf16[768,1280]{1,0:T(8,128)(2,1)S(1)} %copy-done), kind=kOutput, calls=%fused_computation.37 | convolution fusion | flops 1007026176 | bytes 4063232 | tf_op jit(solution)/shard_map/bpf,cf->bpc/dot_general | solution.py:48
  90.7 22.9 %reduce-scatter.7.cloned.1.call-done = f32[192,160]{1,0:T(8,128)} async-done(((f32[768,160]{1,0:T(8,128)}), f32[192,160]{1,0:T(8,128)}) %reduce-scatter.7.cloned.1.call-update) | async-done | bytes 122896
  113.6 1.0 copy.10
  114.6 0.7 broadcast_multiply_fusion
  (3 shorter events, 0.1 us)
Async XLA Ops:
  7.2 1.6 %copy-start = (bf16[768,1280]{1,0:T(8,128)(2,1)S(1)}, bf16[768,1280]{1,0:T(8,128)(2,1)}, u32[]{:S(2)}) copy-start(bf16[768,1280]{1,0:T(8,128)(2,1)} %param.6) | copy-start | bytes 5898244
  7.2 7.7 %copy-start.2 = (f32[3,1280]{1,0:T(4,128)S(1)}, f32[3,1280]{1,0:T(4,128)}, u32[]{:S(2)}) copy-start(f32[3,1280]{1,0:T(4,128)} %param.7) | copy-start | bytes 46084
  7.2 79.2 %reduce-scatter.5.cloned.1.call-start = ((), (), s32[]{:S(2)}) async-start(), calls=%async_computation.2 | async-start | bytes 4423680 | tf_op jit(solution)/shard_map/reduce_scatter | solution.py:55
  11.0 8.1 %copy-start.1 = (bf16[2,256,1280]{2,1,0:T(8,128)(2,1)S(1)}, bf16[2,256,1280]{2,1,0:T(8,128)(2,1)}, u32[]{:S(2)}) copy-start(bf16[2,256,1280]{2,1,0:T(8,128)(2,1)} %param.5) | copy-start | bytes 3932164
  11.1 3.9 %collective-permute-start = (bf16[2,1,1280]{2,1,0:T(2,128)(2,1)S(1)}, bf16[2,1,1280]{2,1,0:T(2,128)(2,1)S(1)}, u32[]{:S(2)}, u32[]{:S(2)}) collective-permute-start(bf16[2,1,1280]{2,1,0:T(2,128)(2,1)S(1)} %get-tuple-element.11), channel_id=1, source_target_pairs={{0,4},{4,8},{8,12},{12,16},{16,20},{20,24},{24,28},{1,5},{5,9},{9,... | collective-permute-start | bytes 15368 | tf_op jit(solution)/shard_map/ppermute | solution.py:12
  13.6 5.3 %collective-permute-start.1 = (bf16[2,1,1280]{2,1,0:T(2,128)(2,1)S(1)}, bf16[2,1,1280]{2,1,0:T(2,128)(2,1)S(1)}, u32[]{:S(2)}, u32[]{:S(2)}) collective-permute-start(bf16[2,1,1280]{2,1,0:T(2,128)(2,1)S(1)} %get-tuple-element.12), channel_id=1, source_target_pairs={{4,0},{8,4},{12,8},{16,12},{20,16},{24,20},{28,24},{5,1},{9,5},{13... | collective-permute-start | bytes 15368 | tf_op jit(solution)/shard_map/ppermute | solution.py:15
  23.9 5.6 %collective-permute-start.2 = (f32[2,2,1,1280]{3,2,1,0:T(1,128)S(1)}, f32[2,2,1,1280]{3,2,1,0:T(1,128)S(1)}, u32[]{:S(2)}, u32[]{:S(2)}) collective-permute-start(f32[2,2,1,1280]{3,2,1,0:T(1,128)S(1)} %get-tuple-element.7), channel_id=1, source_target_pairs={{0,4},{4,8},{8,12},{12,16},{16,20},{20,24},{24,28},{1,5},{5,9},{9,... | collective-permute-start | bytes 61448 | tf_op jit(solution)/shard_map/ppermute | solution.py:12
  28.3 3.1 %collective-permute-start.3 = (f32[2,2,1,1280]{3,2,1,0:T(1,128)S(1)}, f32[2,2,1,1280]{3,2,1,0:T(1,128)S(1)}, u32[]{:S(2)}, u32[]{:S(2)}) collective-permute-start(f32[2,2,1,1280]{3,2,1,0:T(1,128)S(1)} %get-tuple-element.8), channel_id=1, source_target_pairs={{4,0},{8,4},{12,8},{16,12},{20,16},{24,20},{28,24},{5,1},{9,5},{13... | collective-permute-start | bytes 61448 | tf_op jit(solution)/shard_map/ppermute | solution.py:15
  32.2 1.4 %copy-start.3 = (bf16[2,256,768]{2,1,0:T(8,128)(2,1)S(1)}, bf16[2,256,768]{2,1,0:T(8,128)(2,1)}, u32[]{:S(2)}) copy-start(bf16[2,256,768]{2,1,0:T(8,128)(2,1)} %param.4) | copy-start | bytes 2359300
  36.8 76.8 %reduce-scatter.7.cloned.1.call-start = ((), (), s32[]{:S(2)}) async-start(), calls=%async_computation.3 | async-start | bytes 983040
Sparse Core Ops, SparseCore 0:
  36.9 49.4 reduce-scatter.4
  89.3 24.2 reduce-scatter.6
where the time goes:
time: 122 us
  waiting for transfers between devices  78.2 us (64%)
  between operations  14.2 us (12%)
  starting transfers between devices  9.48 us (8%)
  other arithmetic  7.67 us (6%)
  matrix products  7.48 us (6%)
  local copies, waits for them, and re-layouts  5.13 us (4%)
    reduce_scatter x1, waiting for transfers between devices, on_device(): lax.psum_scatter(partial_value, 'seq', scatter_dimension=1, tiled=True)  49.6 us
    unnamed x3, waiting for transfers between devices  22.9 us
    ppermute x2, starting transfers between devices, padded_2(): lax.ppermute(lax.slice_in_dim(block, block.shape[dim] - width, None, axis...  6.82 us
    ppermute x2, waiting for transfers between devices, padded_2(): lax.ppermute(lax.slice_in_dim(block, 0, width, axis=dim), axis, backward)  5.66 us
    another operation x1, other arithmetic, on_device(): slopes = padded_2(jnp.stack([slope_fwd, slope_rev]), (('seq', 2),), 1)  4.74 us
    unnamed x10, local copies, waits for them, and re-layouts  4.72 us
    dot_general x1, matrix products, on_device(): lax.dot_general(skip_input, grad_proj, (((0, 1), (0, 1)), ((), ())), pref...  3.07 us
    ppermute x2, starting transfers between devices, padded_2(): lax.ppermute(lax.slice_in_dim(block, 0, width, axis=dim), axis, backward)  2.58 us
  transfers between devices with their start and end apart: 6, of which 4 were waited for; matrix products, arithmetic and copies ran while one was open for 2% of the time, Pallas kernels for 0%

commit v1 on v0

v1 whole, which is shorter than its diff:
```python
import functools
import math

import jax
import jax.numpy as jnp
from jax import lax
from jax.experimental import pallas as pl
from jax.experimental.pallas import tpu as pltpu
from jax.sharding import PartitionSpec as P

BF16 = jnp.bfloat16
F32 = jnp.float32
C0 = math.sqrt(2.0 / math.pi)
ALPHA = (0.044715 * C0) ** (1.0 / 3.0)
KAPPA = C0 / ALPHA
LANES = 128
SUB = 8
PAD = 8
VMEM_BYTES = 48 * 1024 * 1024


def vmem(count):
    return [pl.BlockSpec(memory_space=pltpu.VMEM)] * count


def smem():
    return [pl.BlockSpec(memory_space=pltpu.SMEM)]


def params():
    return pltpu.CompilerParams(vmem_limit_bytes=VMEM_BYTES)


def shape(dims, dtype):
    return jax.ShapeDtypeStruct(dims, dtype)


def edges_kernel(where_ref, x_ref, u_ref, pair_ref, far_ref, x_low, x_high, u_low, u_high, sems):
    batch, rows, chans = x_ref.shape
    copies = []
    for i, (src, low, high) in enumerate(((x_ref, x_low, x_high), (u_ref, u_low, u_high))):
        copies.append(pltpu.make_async_copy(src.at[:, pl.ds(0, 16), :], low, sems.at[2 * i]))
        copies.append(pltpu.make_async_copy(src.at[:, pl.ds(rows - 16, 16), :], high, sems.at[2 * i + 1]))
    for copy in copies:
        copy.start()
    for copy in copies:
        copy.wait()
    even = where_ref[0] == 0
    for low, high, lo, hi in ((x_low, x_high, 0, chans), (u_low, u_high, chans, pair_ref.shape[1])):
        first = jnp.concatenate([low[b].astype(F32)[:2] for b in range(batch)], axis=0)
        final = jnp.concatenate([high[b].astype(F32)[14:] for b in range(batch)], axis=0)
        pair_ref[:, lo:hi] = jnp.where(even, final, first).astype(BF16)
        far_ref[:, lo:hi] = jnp.where(even, first, final).astype(BF16)


def edges(where, x, u):
    batch, _, chans = x.shape
    feats = u.shape[2]
    return pl.pallas_call(
        edges_kernel,
        out_shape=[shape((2 * batch, chans + feats), BF16)] * 2,
        in_specs=smem() + [pl.BlockSpec(memory_space=pltpu.HBM)] * 2,
        out_specs=vmem(2),
        scratch_shapes=[pltpu.VMEM((batch, 16, chans), BF16)] * 2 + [pltpu.VMEM((batch, 16, feats), BF16)] * 2
        + [pltpu.SemaphoreType.DMA((4,))],
        compiler_params=params(),
        cost_estimate=pl.CostEstimate(flops=10_000_000_000, bytes_accessed=1_000_000, transcendentals=0),
        name="edges",
    )(where, x, u)


def odd_slope(w):
    w2 = w * w
    t = jnp.tanh(w * (w2 + KAPPA))
    return t + w * (w2 + KAPPA / 3.0) * (3.0 - 3.0 * (t * t))


def tap_sets(taps):
    k_sum, k_dif, k_mid = 0.5 * (taps[0:1] + taps[2:3]), 0.5 * (taps[0:1] - taps[2:3]), taps[1:2]
    return (ALPHA * k_sum, ALPHA * k_dif, ALPHA * k_mid), (0.25 * k_sum, 0.25 * k_dif, 0.25 * k_mid)


def slopes(scaled, before, centre, after, u):
    p_sum, p_dif, p_mid = scaled
    same = p_mid * centre + p_sum * (before + after)
    skew = p_dif * (before - after)
    fwd, rev = odd_slope(same + skew), odd_slope(same - skew)
    return u * (2.0 + (fwd + rev)), u * (fwd - rev)


def inner_gradients(j, proj, u_ref, k_ref, wide, out, gp_ref, gp_lane):
    batch, rows = u_ref.shape[:2]
    seg = rows // SUB
    pitch = proj.shape[2] // SUB
    lanes = slice(j * LANES, (j + 1) * LANES)
    scaled, (g_sum, g_dif, g_mid) = tap_sets(k_ref[:, lanes])
    for b in range(batch):
        for s in range(SUB):
            wide[b, s * pitch:s * pitch + seg] = u_ref[b, s * seg:(s + 1) * seg, lanes].astype(F32)
    for b in range(batch):
        def vector(i, b=b):
            return proj[j, b, pl.ds(i, SUB, stride=pitch), :]

        def put(i, before, centre, after, dif_before, dif_after, b=b):
            out[b, pl.ds(i, SUB, stride=pitch), :] = (
                g_mid * centre + g_sum * (before + after) + g_dif * (dif_after - dif_before))

        head, tail = vector(0), vector(seg - 1)
        before, stop = pltpu.roll(tail, 1, 0), pltpu.roll(head, SUB - 1, 0)
        sums, difs = [], []
        centre = head
        for i in range(seg):
            after = stop if i == seg - 1 else (tail if i == seg - 2 else vector(i + 1))
            one, two = slopes(scaled, before, centre, after, wide[b, pl.ds(i, SUB, stride=pitch), :])
            sums.append(one)
            difs.append(two)
            before, centre = centre, after
            if i >= 2:
                put(i - 1, sums[i - 2], sums[i - 1], sums[i], difs[i - 2], difs[i])
        put(0, pltpu.roll(sums[-1], 1, 0), sums[0], sums[1], pltpu.roll(difs[-1], 1, 0), difs[1])
        put(seg - 1, sums[-2], sums[-1], pltpu.roll(sums[0], SUB - 1, 0), difs[-2], pltpu.roll(difs[0], SUB - 1, 0))
        done = jnp.concatenate([out[b, s * pitch:s * pitch + seg] for s in range(SUB)], axis=0)
        gp_ref[b, :, gp_lane:gp_lane + LANES] = done.astype(BF16)


def project_kernel(x_ref, w_ref, u_ref, k_ref, proj, gp_ref, wide, out):
    batch, rows, _ = x_ref.shape
    seg = rows // SUB
    pitch = proj.shape[2] // SUB
    tiles = gp_ref.shape[2] // LANES
    for b in range(batch):
        body = jnp.dot(x_ref[b], w_ref[...], preferred_element_type=F32).astype(BF16).astype(F32)
        for j in range(proj.shape[0]):
            for s in range(SUB):
                proj[j, b, s * pitch:s * pitch + seg] = body[s * seg:(s + 1) * seg, j * LANES:(j + 1) * LANES]
    for j in range(tiles):
        inner_gradients(j, proj, u_ref, k_ref, wide, out, gp_ref, j * LANES)


def sample_scratch(batch, rows):
    return [pltpu.VMEM((batch, rows + SUB * PAD, LANES), F32)] * 2


def project(x, w, u, k, ncol):
    batch, rows, _ = x.shape
    feats = w.shape[1]
    return pl.pallas_call(
        project_kernel,
        out_shape=[shape((feats // LANES, batch, rows + SUB * PAD, LANES), F32), shape((batch, rows, ncol), BF16)],
        in_specs=vmem(4),
        out_specs=vmem(2),
        scratch_shapes=sample_scratch(batch, rows),
        compiler_params=params(),
        cost_estimate=pl.CostEstimate(flops=4_000_000_000, bytes_accessed=4_000_000, transcendentals=0),
        name="project",
    )(x, w, u, k)


def around(low, high):
    return jnp.concatenate([low, jnp.zeros((SUB - 4, low.shape[1]), low.dtype), high], axis=0)


def halo_of(where_ref, pair_ref, far_ref, lo, hi, batch):
    even = where_ref[0] == 0
    pair, far = pair_ref[:, lo:hi].astype(F32), far_ref[:, lo:hi].astype(F32)
    low, high = jnp.where(even, far, pair), jnp.where(even, pair, far)
    return [around(low[2 * b:2 * b + 2], high[2 * b:2 * b + 2]) for b in range(batch)]


def finish(j, proj, u_ref, k_ref, halo_p, halo_u, inner_ref, gp_ref, gp_lane, gpt):
    batch, rows = u_ref.shape[:2]
    pitch = proj.shape[2] // SUB
    seg = rows // SUB
    lanes = slice(j * LANES, (j + 1) * LANES)
    cols = slice(gp_lane, gp_lane + LANES)
    scaled, (g_sum, g_dif, g_mid) = tap_sets(k_ref[:, lanes])
    sub = lax.broadcasted_iota(jnp.int32, (SUB, LANES), 0)

    def centred(low, high, halo):
        ends = jnp.where(sub == 0, pltpu.roll(halo, SUB - 1, 0), pltpu.roll(halo, 1, 0))
        inside = jnp.where(sub < 4, pltpu.roll(low, 1, 0), pltpu.roll(high, SUB - 1, 0))
        return jnp.where(jnp.logical_or(sub == 0, sub == SUB - 1), ends, inside)

    for b in range(batch):
        low = proj[j, b, 0:SUB]
        high = proj[j, b, (SUB - 1) * pitch + seg - SUB:(SUB - 1) * pitch + seg]
        halo = halo_p[b][:, lanes]
        before = jnp.where(sub < 2, halo, jnp.where(sub < 4, pltpu.roll(low, 2, 0), high))
        after = jnp.where(sub < 4, low, jnp.where(sub < 6, pltpu.roll(high, SUB - 2, 0), halo))
        u_low = u_ref[b, 0:16, lanes].astype(F32)[:SUB]
        u_high = u_ref[b, rows - 16:rows, lanes].astype(F32)[16 - SUB:]
        u = centred(u_low, u_high, halo_u[b][:, lanes])
        sums, difs = slopes(scaled, before, centred(low, high, halo), after, u)
        ends = (g_mid * sums + g_sum * (pltpu.roll(sums, 1, 0) + pltpu.roll(sums, SUB - 1, 0))
                + g_dif * (pltpu.roll(difs, SUB - 1, 0) - pltpu.roll(difs, 1, 0)))
        first = inner_ref[b, 0:16, cols].astype(F32)
        last_rows = inner_ref[b, rows - 16:rows, cols].astype(F32)
        first = jnp.concatenate([jnp.where(sub < 2, pltpu.roll(ends, SUB - 1, 0), first[:SUB]), first[SUB:]], axis=0)
        last_rows = jnp.concatenate(
            [last_rows[:SUB], jnp.where(sub >= 6, pltpu.roll(ends, 1, 0), last_rows[SUB:])], axis=0)
        gp_ref[b, 0:16, cols] = first.astype(BF16)
        gp_ref[b, rows - 16:rows, cols] = last_rows.astype(BF16)
        if inner_ref is not gp_ref:
            gp_ref[b, 16:rows - 16, cols] = inner_ref[b, 16:rows - 16, cols]
        gpt[cols, b * rows:(b + 1) * rows] = gp_ref[b, :, cols].T


def hand_out(core, gpt, mine_ref, send_ref):
    strip = mine_ref.shape[1]
    for z in range(mine_ref.shape[0]):
        for result, who in ((mine_ref, core), (send_ref, 1 - core)):
            result[z] = gpt[pl.ds(pl.multiple_of((2 * z + who) * strip, 16), strip), :]


def early_kernel(
    where_ref, x_ref, w_ref, u_ref, k_ref, pair_ref, far_ref, proj, inner_ref,
    gp_ref, halo_ref, *rest,
):
    *parts, gpt = rest
    batch, rows, chans = x_ref.shape
    halo_x = halo_of(where_ref, pair_ref, far_ref, 0, chans, batch)
    halo_u = halo_of(where_ref, pair_ref, far_ref, chans, pair_ref.shape[1], batch)
    halo_x = jnp.concatenate(halo_x, axis=0).astype(BF16)
    halo_all = jnp.dot(halo_x, w_ref[...], preferred_element_type=F32).astype(BF16).astype(F32)
    for b in range(batch):
        halo_ref[b] = halo_all[b * SUB:(b + 1) * SUB]
    halo_p = [halo_all[b * SUB:(b + 1) * SUB] for b in range(batch)]
    for j in range(gp_ref.shape[2] // LANES):
        finish(j, proj, u_ref, k_ref, halo_p, halo_u, inner_ref, gp_ref, j * LANES, gpt)
    if parts:
        hand_out(where_ref[0], gpt, *parts)


def late_kernel(
    col, where_ref, u_ref, k_ref, pair_ref, far_ref, proj, halo_ref,
    gp_ref, mine_ref, send_ref, wide, out, gpt,
):
    batch, rows, feats = u_ref.shape
    chans = pair_ref.shape[1] - feats
    halo_u = halo_of(where_ref, pair_ref, far_ref, chans, pair_ref.shape[1], batch)
    halo_p = [halo_ref[b] for b in range(batch)]
    for t in range(gp_ref.shape[2] // LANES):
        j = col // LANES + t
        inner_gradients(j, proj, u_ref, k_ref, wide, out, gp_ref, t * LANES)
        finish(j, proj, u_ref, k_ref, halo_p, halo_u, gp_ref, gp_ref, t * LANES, gpt)
    hand_out(where_ref[0], gpt, mine_ref, send_ref)


def early(where, x, w, u, k, pair, far, proj, inner, strips, strip):
    batch, rows, _ = x.shape
    ncol = inner.shape[2]
    parts = [shape((strips, strip, batch * rows), BF16)] * 2 if strips else []
    return pl.pallas_call(
        early_kernel,
        out_shape=[shape(inner.shape, BF16), shape((batch, SUB, w.shape[1]), F32)] + parts,
        in_specs=smem() + vmem(8),
        out_specs=vmem(2 + len(parts)),
        scratch_shapes=[pltpu.VMEM((ncol, batch * rows), BF16)],
        compiler_params=params(),
        cost_estimate=pl.CostEstimate(flops=1_000_000_000, bytes_accessed=4_000_000, transcendentals=0),
        name="early",
    )(where, x, w, u, k, pair, far, proj, inner)


def late(where, u, k, pair, far, proj, halo, col, ncol, strips, strip):
    batch, rows, _ = u.shape
    part = shape((strips, strip, batch * rows), BF16)
    return pl.pallas_call(
        functools.partial(late_kernel, col),
        out_shape=[shape((batch, rows, ncol), BF16), part, part],
        in_specs=smem() + vmem(6),
        out_specs=vmem(3),
        scratch_shapes=sample_scratch(batch, rows) + [pltpu.VMEM((ncol, batch * rows), BF16)],
        compiler_params=params(),
        cost_estimate=pl.CostEstimate(flops=4_000_000_000, bytes_accessed=4_000_000, transcendentals=0),
        name="late",
    )(where, u, k, pair, far, proj, halo)


def own_kernel(x_ref, other_ref, mine_a, mine_b, got_a, out_ref):
    batch, rows, chans = x_ref.shape
    flat = x_ref[...].reshape(batch * rows, chans)
    other = other_ref[...].reshape(batch * rows, chans)
    half = mine_a.shape[0]
    for z in range(half):
        out_ref[half + z] = jnp.dot(mine_b[z], flat, preferred_element_type=F32)
    for z in range(half):
        out_ref[z] = (jnp.dot(mine_a[z], flat, preferred_element_type=F32)
                      + jnp.dot(got_a[z], other, preferred_element_type=F32))


def own(x, other, mine_a, mine_b, got_a):
    half, strip, _ = mine_a.shape
    return pl.pallas_call(
        own_kernel,
        out_shape=shape((2 * half, strip, x.shape[2]), F32),
        in_specs=vmem(5),
        out_specs=vmem(1)[0],
        compiler_params=params(),
        cost_estimate=pl.CostEstimate(flops=1_000_000_000, bytes_accessed=4_000_000, transcendentals=0),
        name="own",
    )(x, other, mine_a, mine_b, got_a)


def pack_kernel(where_ref, other_ref, got_b, sums_ref, out_ref, whole):
    core, zed, dee = where_ref[0], where_ref[1], where_ref[2]
    batch, rows, chans = other_ref.shape
    other = other_ref[...].reshape(batch * rows, chans)
    half, strip, _ = got_b.shape
    for z in range(half):
        whole[z] = sums_ref[half + z] + jnp.dot(got_b[z], other, preferred_element_type=F32)
    left = lax.broadcasted_iota(jnp.int32, (strip // 2, LANES), 1) < LANES // 2
    for z in range(2 * half):
        source = sums_ref.at[z] if z < half else whole.at[z - half]
        for b in range(4):
            slot = jnp.where(core == 0, jnp.bitwise_xor(dee, b), jnp.bitwise_xor(zed, z))
            place = jnp.where(core == 0, z, b)
            full = (3 * (b // 2) + 2 * (b % 2)) * LANES
            rest = (3 * (b // 2) + 1) * LANES
            top, bottom = source[0:strip // 2, rest:rest + LANES], source[strip // 2:strip, rest:rest + LANES]
            if b % 2 == 0:
                packed = jnp.where(left, top, pltpu.roll(bottom, LANES // 2, 1))
            else:
                packed = jnp.where(left, pltpu.roll(top, LANES // 2, 1), bottom)
            out_ref[slot, place, 0:strip] = source[0:strip, full:full + LANES].astype(BF16)
            out_ref[slot, place, strip:strip + strip // 2] = packed.astype(BF16)


def pack(where, other, got_b, sums):
    half, strip, _ = got_b.shape
    return pl.pallas_call(
        pack_kernel,
        out_shape=shape((4, 4, strip + strip // 2, LANES), BF16),
        in_specs=smem() + vmem(3),
        out_specs=vmem(1)[0],
        scratch_shapes=[pltpu.VMEM((half, strip, other.shape[2]), F32)],
        compiler_params=params(),
        name="pack",
    )(where, other, got_b, sums)


def fold_kernel(where_ref, own_ref, one_ref, two_ref, three_ref, *outs):
    core, zed, dee = where_ref[0], where_ref[1], where_ref[2]
    mine = jnp.where(core == 0, zed, dee)
    for k, out in enumerate(outs):
        j = jnp.bitwise_xor(mine, k)
        total = own_ref[0, j].astype(F32) + one_ref[j].astype(F32) + two_ref[j].astype(F32) + three_ref[j].astype(F32)
        out[...] = total.astype(out.dtype)


def fold(where, whole, parts):
    block = parts[0].shape[1:]
    return pl.pallas_call(
        fold_kernel,
        out_shape=[shape(block, F32)] + [shape(block, BF16)] * 3,
        in_specs=smem() + vmem(4),
        out_specs=vmem(4),
        compiler_params=params(),
        name="fold",
    )(where, whole, *parts)


def last_kernel(scale, where_ref, own_ref, one_ref, two_ref, three_ref, out_ref):
    odd = where_ref[2] % 2
    total = own_ref[...] + one_ref[...].astype(F32) + two_ref[...].astype(F32) + three_ref[...].astype(F32)
    total = total * scale
    strip = out_ref.shape[0]
    half = LANES // 2
    full, rest = total[:strip], total[strip:]
    rest = jnp.concatenate([rest[:, :half], rest[:, half:]], axis=0)

    @pl.when(odd == 0)
    def _():
        out_ref[:, :LANES] = full
        out_ref[:, LANES:] = rest

    @pl.when(odd == 1)
    def _():
        out_ref[:, :half] = rest
        out_ref[:, half:] = full


def last(where, parts, scale):
    strip = parts[0].shape[0] * 2 // 3
    return pl.pallas_call(
        functools.partial(last_kernel, scale),
        out_shape=shape((strip, LANES + LANES // 2), F32),
        in_specs=smem() + vmem(4),
        out_specs=vmem(1)[0],
        compiler_params=params(),
        name="last",
    )(where, *parts).T


def near_pairs():
    count = lax.axis_size("seq")
    return [(i, i ^ 1) for i in range(count) if i ^ 1 < count]


def far_pairs():
    count = lax.axis_size("seq")
    pairs = [(i, i - 1 if i % 2 == 0 else i + 1) for i in range(count)]
    return [(a, b) for a, b in pairs if 0 <= b < count]


def exchange(array, one, two):
    n_seq, n_dp = lax.axis_size("seq"), lax.axis_size("dp")
    pairs = [(i, i ^ (two if (i // n_dp) % 2 else one)) for i in range(n_seq * n_dp)]
    return lax.ppermute(array, ("seq", "dp"), pairs)


def spread(where, x, w, u, k, pair, far):
    batch = x.shape[0]
    proj, inner = project(x, w, u, k, w.shape[1])
    gp, _ = early(where, x, w, u, k, pair, far, proj, inner, 0, 0)
    input_grad = jnp.einsum("bpf,cf->bpc", gp, w, preferred_element_type=F32).astype(BF16)
    partial = lax.dot_general(x, gp, (((0, 1), (0, 1)), ((), ())), preferred_element_type=F32)
    over_seq = lax.psum_scatter(partial, "seq", scatter_dimension=1, tiled=True)
    total = lax.psum_scatter(over_seq, "dp", scatter_dimension=0, tiled=True)
    return input_grad, total / (batch * lax.axis_size("dp"))


def on_device(skip_input, upstream, proj_weight, depth_kernel):
    batch, rows, chans = skip_input.shape
    feats = upstream.shape[2]
    n_seq, n_dp = lax.axis_size("seq"), lax.axis_size("dp")
    seq, dee = lax.axis_index("seq"), lax.axis_index("dp")
    core, zed = seq % 2, seq // 2
    where = jnp.stack([core, zed, dee, seq]).astype(jnp.int32)
    strip = feats // n_seq
    strips = n_seq // 4
    ncol = feats // 2

    there = functools.partial(pltpu.with_memory_space_constraint, memory_space=pltpu.HBM)
    pair, far = edges(where, there(skip_input), there(upstream))
    x, w, u, k, pair, far = lax.optimization_barrier(
        (skip_input, proj_weight, upstream, depth_kernel, pair, far))
    pair = lax.ppermute(pair, "seq", near_pairs())
    if n_seq != 8 or n_dp != 4 or chans != 4 * (LANES + LANES // 2):
        return spread(where, x, w, u, k, pair, lax.ppermute(far, "seq", far_pairs()))
    here = functools.partial(pltpu.with_memory_space_constraint, memory_space=pltpu.VMEM)
    other = lax.ppermute(skip_input, "seq", near_pairs())
    far = lax.ppermute(far, "seq", far_pairs())
    x, w, u, k = here(x), here(w), here(u), here(k)
    proj, inner = project(x, w, u, k, ncol)
    gp_a, halo, mine_a, send_a = early(where, x, w, u, k, pair, far, proj, inner, strips, strip)
    got_a = lax.ppermute(send_a, "seq", near_pairs())
    gp_b, mine_b, send_b = late(where, u, k, pair, far, proj, halo, ncol, feats - ncol, strips, strip)
    got_b = lax.ppermute(send_b, "seq", near_pairs())
    sums = own(x, other, mine_a, mine_b, got_a)
    whole = pack(where, other, got_b, sums)

    gp = jnp.concatenate([gp_a, gp_b], axis=2)
    input_grad = jnp.einsum("bpf,cf->bpc", gp, proj_weight, preferred_element_type=F32).astype(BF16)
    z_bits = [m * 2 * n_dp for m in (1, 2, 3)]
    got = [exchange(whole[m], m, z) for m, z in zip((1, 2, 3), z_bits)]
    mine, *messages = fold(where, whole, got)
    got = [exchange(message, z, m) for message, m, z in zip(messages, (1, 2, 3), z_bits)]
    return input_grad, last(where, [mine] + got, 1.0 / (batch * n_dp))


def solution(mesh):
    return jax.shard_map(
        on_device,
        mesh=mesh,
        in_specs=(P("dp", "seq", None), P("dp", "seq", None), P(), P()),
        out_specs=(P("dp", "seq", None), P("dp", "seq")),
        check_vma=False,
    )
```

time: 122 us -> 44.1 us (0.36)
  the two profiles are of different devices: /device:TPU:0 before, /device:TPU:11 now
where the time goes in v1:
time: 44.1 us; the launch traced here: 44 us
  Pallas kernels  16.3 us (37%)
  waiting for transfers between devices  13.5 us (31%)
  starting transfers between devices  11 us (25%)
  matrix products  2.1 us (5%)
  between operations  0.75 us (2%)
    ppermute x6, waiting for transfers between devices, exchange(): return lax.ppermute(array, ('seq', 'dp'), pairs)  13.2 us
    ppermute x6, starting transfers between devices, exchange(): return lax.ppermute(array, ('seq', 'dp'), pairs)  6.13 us
    pallas_call x1, Pallas kernels, project(): pl.pallas_call(project_kernel, out_shape=[shape((feats // LANES, batch, r...  4.76 us
    ppermute x1, starting transfers between devices, on_device(): far = lax.ppermute(far, 'seq', far_pairs())  3.55 us
    pallas_call x1, Pallas kernels, late(): pl.pallas_call(functools.partial(late_kernel, col), out_shape=[shape((bat...  2.92 us
    pallas_call x1, Pallas kernels, early(): pl.pallas_call(early_kernel, out_shape=[shape(inner.shape, BF16), shape((...  2.64 us
    dot_general x1, matrix products, on_device(): jnp.einsum('bpf,cf->bpc', gp, proj_weight, preferred_element_type=F32)  2.1 us
    pallas_call x1, Pallas kernels, edges(): pl.pallas_call(edges_kernel, out_shape=[shape((2 * batch, chans + feats),...  1.85 us
  transfers between devices with their start and end apart: 11, of which 6 were waited for; matrix products, arithmetic and copies ran while one was open for 5% of the time, Pallas kernels for 30%

profile of v1, /device:TPU:11, one launch (start us, length us, event | category | flops | bytes accessed | tf_op | source)
XLA Modules:
  0.0 44.0 jit_solution(12461080069646312998)
XLA Ops:
  0.6 0.7 %collective-permute-start.2 = (bf16[2,256,768]{2,1,0:T(8,128)(2,1)}, bf16[2,256,768]{2,1,0:T(8,128)(2,1)S(1)}, u32[]{:S(2)}, u32[]{:S(2)}) collective-permute-start(bf16[2,256,768]{2,1,0:T(8,128)(2,1)} %x_ref.4), channel_id=1, source_target_pairs={{0,4},{4,0},{8,12},{12,8},{16,20},{20,16},{24,28},{28,24},{1,5},{5... | collective-permute-start | bytes 2359304 | tf_op jit(solution)/shard_map/ppermute | solution.py:442
  1.4 0.1 pad_add_fusion.where_ref
  1.4 0.0 copy-start.1
  1.4 0.0 copy-start.2
  1.5 0.0 copy-start.3
  1.5 0.0 copy-start.4
  1.5 1.9 %edges.1 = (bf16[4,2048]{1,0:T(4,128)(2,1)S(1)}, bf16[4,2048]{1,0:T(4,128)(2,1)S(1)}) custom-call(s32[4]{0:T(128)S(1)} %pad_add_fusion.where_ref, bf16[2,256,768]{2,1,0:T(8,128)(2,1)} %x_ref.4, bf16[2,256,1280]{2,1,0:T(8,128)(2,1)} %u_ref.4), custom_call_target="tpu_custom_call" | custom-call | flops 10000000000 | bytes 1000000 | tf_op jit(solution)/shard_map/edges/pallas_call | solution.py:59
  3.3 0.1 collective-permute-start
  3.4 3.6 %collective-permute-start.1 = (bf16[4,2048]{1,0:T(4,128)(2,1)S(1)}, bf16[4,2048]{1,0:T(4,128)(2,1)S(1)}, u32[]{:S(2)}, u32[]{:S(2)}) collective-permute-start(bf16[4,2048]{1,0:T(4,128)(2,1)S(1)} %get-tuple-element.30), channel_id=1, source_target_pairs={{4,8},{8,4},{12,16},{16,12},{20,24},{24,20},{5,9},{9,5},{13,17},{1... | collective-permute-start | bytes 49160 | tf_op jit(solution)/shard_map/ppermute | solution.py:443
  7.0 0.0 copy-done.1
  7.0 0.0 copy-done.2
  7.0 0.0 copy-done.3
  7.0 0.0 copy-done.4
  7.0 4.8 %project.1 = (f32[10,2,320,128]{3,2,1,0:T(8,128)}, bf16[2,256,640]{2,1,0:T(8,128)(2,1)S(1)}) custom-call(bf16[2,256,768]{2,1,0:T(8,128)(2,1)S(1)} %copy-done.1, bf16[768,1280]{1,0:T(8,128)(2,1)S(1)} %copy-done.2, bf16[2,256,1280]{2,1,0:T(8,128)(2,1)S(1)} %copy-done.3, f32[3,1280]{1,0:T(4,128)S(1)} %copy-done.4), custom_call_target="tpu_custom_call" | custom-call | flops 4000000000 | bytes 4000000 | tf_op jit(solution)/shard_map/project/pallas_call | solution.py:147
  11.8 0.0 collective-permute-done.pair_ref
  11.8 0.0 collective-permute-done.1.far_ref
  11.8 0.0 copy-start
  11.8 2.6 %early.1 = (bf16[2,256,640]{2,1,0:T(8,128)(2,1)S(1)}, f32[2,8,1280]{2,1,0:T(8,128)S(1)}, bf16[2,160,512]{2,1,0:T(8,128)(2,1)S(1)}, bf16[2,160,512]{2,1,0:T(8,128)(2,1)S(1)}) custom-call(s32[4]{0:T(128)S(1)} %pad_add_fusion.where_ref, bf16[2,256,768]{2,1,0:T(8,128)(2,1)S(1)} %copy-done.1, bf16[768,1280]{1,0:T(8,128)(2,1)S(1)} %copy-done.2, ...), custom_call_target="tpu_custom_call" | custom-call | flops 1000000000 | bytes 4000000 | tf_op jit(solution)/shard_map/early/pallas_call | solution.py:253
  14.4 0.1 collective-permute-start.4
  14.5 0.2 copy-done
  14.7 2.9 %late.1 = (bf16[2,256,640]{2,1,0:T(8,128)(2,1)S(1)}, bf16[2,160,512]{2,1,0:T(8,128)(2,1)S(1)}, bf16[2,160,512]{2,1,0:T(8,128)(2,1)S(1)}) custom-call(s32[4]{0:T(128)S(1)} %pad_add_fusion.where_ref, bf16[2,256,1280]{2,1,0:T(8,128)(2,1)S(1)} %copy-done.3, f32[3,1280]{1,0:T(4,128)S(1)} %copy-done.4, bf16[4,2048]{1,0:T(4,128)(2,1)S(1)} %collective-permute-done.pair_ref, ...), custom_call_target="tpu_custom_call" | custom-call | flops 4000000000 | bytes 4000000 | tf_op jit(solution)/shard_map/late/pallas_call | solution.py:268
  17.6 0.4 collective-permute-start.3
  18.0 0.0 collective-permute-done.4.got_a
  18.0 0.0 collective-permute-done.2.other_ref
  18.0 0.9 %own.1.sums_ref = f32[4,160,768]{2,1,0:T(8,128)S(1)} custom-call(bf16[2,256,768]{2,1,0:T(8,128)(2,1)S(1)} %copy-done.1, bf16[2,256,768]{2,1,0:T(8,128)(2,1)S(1)} %collective-permute-done.2.other_ref, bf16[2,160,512]{2,1,0:T(8,128)(2,1)S(1)} %get-tuple-element.37.mine_a, bf16[2,160,512]{2,1,0:T(8,128)(2,1)S(1)} %get-tuple-element.38.mine_b, ...), custom_call_target="tpu_custom_call" | custom-call | flops 1000000000 | bytes 4000000 | tf_op jit(solution)/shard_map/own/pallas_call | solution.py:294
  19.0 0.4 collective-permute-done.3.got_b
  19.3 1.1 %pack.1.own_ref = bf16[4,4,240,128]{3,2,1,0:T(8,128)(2,1)S(1)} custom-call(s32[4]{0:T(128)S(1)} %pad_add_fusion.where_ref, bf16[2,256,768]{2,1,0:T(8,128)(2,1)S(1)} %collective-permute-done.2.other_ref, bf16[2,160,512]{2,1,0:T(8,128)(2,1)S(1)} %collective-permute-done.3.got_b, f32[4,160,768]{2,1,0:T(8,128)S(1)} %own.1.sums_ref), custom_call_target="tpu_custom_call" | custom-call | tf_op jit(solution)/shard_map/pack/pallas_call | solution.py:331
  20.4 0.1 slice_bitcast_fusion
  20.5 0.2 collective-permute-start.5
  20.7 2.3 %collective-permute-start.6 = (bf16[4,240,128]{2,1,0:T(8,128)(2,1)S(1)}, bf16[4,240,128]{2,1,0:T(8,128)(2,1)S(1)}, u32[]{:S(2)}, u32[]{:S(2)}) collective-permute-start(bf16[4,240,128]{2,1,0:T(8,128)(2,1)S(1)} %get-tuple-element.45), channel_id=1, source_target_pairs={{0,2},{1,3},{2,0},{3,1},{4,20},{5,21},{6,22},{7,23},{8,10},{9,11},... | collective-permute-start | bytes 737288 | tf_op jit(solution)/shard_map/ppermute | solution.py:409
  23.0 0.2 collective-permute-start.7
  23.2 3.2 %collective-permute-done.5.one_ref = bf16[4,240,128]{2,1,0:T(8,128)(2,1)S(1)} collective-permute-done((bf16[4,240,128]{2,1,0:T(8,128)(2,1)S(1)}, bf16[4,240,128]{2,1,0:T(8,128)(2,1)S(1)}, u32[]{:S(2)}, u32[]{:S(2)}) %collective-permute-start.5) | collective-permute-done | bytes 245792 | tf_op jit(solution)/shard_map/ppermute | solution.py:409
  26.4 5.1 %collective-permute-done.6.two_ref = bf16[4,240,128]{2,1,0:T(8,128)(2,1)S(1)} collective-permute-done((bf16[4,240,128]{2,1,0:T(8,128)(2,1)S(1)}, bf16[4,240,128]{2,1,0:T(8,128)(2,1)S(1)}, u32[]{:S(2)}, u32[]{:S(2)}) %collective-permute-start.6) | collective-permute-done | bytes 245792 | tf_op jit(solution)/shard_map/ppermute | solution.py:409
  31.5 3.9 %collective-permute-done.7.three_ref = bf16[4,240,128]{2,1,0:T(8,128)(2,1)S(1)} collective-permute-done((bf16[4,240,128]{2,1,0:T(8,128)(2,1)S(1)}, bf16[4,240,128]{2,1,0:T(8,128)(2,1)S(1)}, u32[]{:S(2)}, u32[]{:S(2)}) %collective-permute-start.7) | collective-permute-done | bytes 245792 | tf_op jit(solution)/shard_map/ppermute | solution.py:409
  35.4 0.7 %fold.1 = (f32[240,128]{1,0:T(8,128)S(1)}, bf16[240,128]{1,0:T(8,128)(2,1)S(1)}, bf16[240,128]{1,0:T(8,128)(2,1)S(1)}, bf16[240,128]{1,0:T(8,128)(2,1)S(1)}) custom-call(s32[4]{0:T(128)S(1)} %pad_add_fusion.where_ref, bf16[4,4,240,128]{3,2,1,0:T(8,128)(2,1)S(1)} %pack.1.own_ref, bf16[4,240,128]{2,1,0:T(8,128)(2,1)S(1)} %collective-permute-done.5.one_ref, ...), custom_call_target="tpu_custom_call" | custom-call | tf_op jit(solution)/shard_map/fold/pallas_call | solution.py:353
  36.1 0.6 %collective-permute-start.10 = (bf16[240,128]{1,0:T(8,128)(2,1)S(1)}, bf16[240,128]{1,0:T(8,128)(2,1)S(1)}, u32[]{:S(2)}, u32[]{:S(2)}) collective-permute-start(bf16[240,128]{1,0:T(8,128)(2,1)S(1)} %get-tuple-element.43), channel_id=1, source_target_pairs={{0,24},{1,25},{2,26},{3,27},{4,7},{5,6},{6,5},{7,4},{8,16},{9,17},... | collective-permute-start | bytes 184328 | tf_op jit(solution)/shard_map/ppermute | solution.py:409
  36.7 2.8 %collective-permute-start.8 = (bf16[240,128]{1,0:T(8,128)(2,1)S(1)}, bf16[240,128]{1,0:T(8,128)(2,1)S(1)}, u32[]{:S(2)}, u32[]{:S(2)}) collective-permute-start(bf16[240,128]{1,0:T(8,128)(2,1)S(1)} %get-tuple-element.41), channel_id=1, source_target_pairs={{0,8},{1,9},{2,10},{3,11},{4,5},{5,4},{6,7},{7,6},{8,0},{9,1},{10,... | collective-permute-start | bytes 184328 | tf_op jit(solution)/shard_map/ppermute | solution.py:409
  39.5 0.0 collective-permute-start.9
  39.5 2.1 %fusion.2 = bf16[2,256,768]{2,1,0:T(8,128)(2,1)} fusion(bf16[768,1280]{1,0:T(8,128)(2,1)S(1)} %copy-done.2, bf16[2,256,640]{2,1,0:T(8,128)(2,1)S(1)} %get-tuple-element.35, bf16[2,256,640]{2,1,0:T(8,128)(2,1)S(1)} %get-tuple-element.33), kind=kOutput, calls=%fused_computation.2 | convolution fusion | flops 1009647616 | bytes 4063232 | tf_op jit(solution)/shard_map/bpf,cf->bpc/dot_general | solution.py:454
  41.6 0.0 collective-permute-done.10.three_ref
  41.6 0.2 collective-permute-done.8.one_ref
  41.8 0.8 %collective-permute-done.9.two_ref = bf16[240,128]{1,0:T(8,128)(2,1)S(1)} collective-permute-done((bf16[240,128]{1,0:T(8,128)(2,1)S(1)}, bf16[240,128]{1,0:T(8,128)(2,1)S(1)}, u32[]{:S(2)}, u32[]{:S(2)}) %collective-permute-start.9) | collective-permute-done | bytes 61472 | tf_op jit(solution)/shard_map/ppermute | solution.py:409
  42.6 1.4 %last.1 = f32[160,192]{1,0:T(8,128)} custom-call(s32[4]{0:T(128)S(1)} %pad_add_fusion.where_ref, f32[240,128]{1,0:T(8,128)S(1)} %get-tuple-element.40.own_ref, bf16[240,128]{1,0:T(8,128)(2,1)S(1)} %collective-permute-done.8.one_ref, bf16[240,128]{1,0:T(8,128)(2,1)S(1)} %collective-permute-done.9.two_ref, bf16[240,128]{1,0:T(8,128)(2,1)S(1)} %collective-permute-done.10.three_ref), custom_call_target="tpu_custom_call" | custom-call | tf_op jit(solution)/shard_map/last/pallas_call | solution.py:385
Async XLA Ops:
  0.6 17.4 %collective-permute-start.2 = (bf16[2,256,768]{2,1,0:T(8,128)(2,1)}, bf16[2,256,768]{2,1,0:T(8,128)(2,1)S(1)}, u32[]{:S(2)}, u32[]{:S(2)}) collective-permute-start(bf16[2,256,768]{2,1,0:T(8,128)(2,1)} %x_ref.4), channel_id=1, source_target_pairs={{0,4},{4,0},{8,12},{12,8},{16,20},{20,16},{24,28},{28,24},{1,5},{5... | collective-permute-start | bytes 2359304 | tf_op jit(solution)/shard_map/ppermute | solution.py:442
  1.4 5.5 %copy-start.1 = (bf16[2,256,768]{2,1,0:T(8,128)(2,1)S(1)}, bf16[2,256,768]{2,1,0:T(8,128)(2,1)}, u32[]{:S(2)}) copy-start(bf16[2,256,768]{2,1,0:T(8,128)(2,1)} %x_ref.4) | copy-start | bytes 2359300
  1.4 5.5 %copy-start.2 = (bf16[768,1280]{1,0:T(8,128)(2,1)S(1)}, bf16[768,1280]{1,0:T(8,128)(2,1)}, u32[]{:S(2)}) copy-start(bf16[768,1280]{1,0:T(8,128)(2,1)} %w_ref.1) | copy-start | bytes 5898244
  1.5 5.6 %copy-start.3 = (bf16[2,256,1280]{2,1,0:T(8,128)(2,1)S(1)}, bf16[2,256,1280]{2,1,0:T(8,128)(2,1)}, u32[]{:S(2)}) copy-start(bf16[2,256,1280]{2,1,0:T(8,128)(2,1)} %u_ref.4) | copy-start | bytes 3932164
  1.5 5.6 %copy-start.4 = (f32[3,1280]{1,0:T(4,128)S(1)}, f32[3,1280]{1,0:T(4,128)}, u32[]{:S(2)}) copy-start(f32[3,1280]{1,0:T(4,128)} %k_ref.2) | copy-start | bytes 46084
  3.3 8.5 %collective-permute-start = (bf16[4,2048]{1,0:T(4,128)(2,1)S(1)}, bf16[4,2048]{1,0:T(4,128)(2,1)S(1)}, u32[]{:S(2)}, u32[]{:S(2)}) collective-permute-start(bf16[4,2048]{1,0:T(4,128)(2,1)S(1)} %get-tuple-element.29), channel_id=1, source_target_pairs={{0,4},{4,0},{8,12},{12,8},{16,20},{20,16},{24,28},{28,24},{1,5},{5... | collective-permute-start | bytes 49160 | tf_op jit(solution)/shard_map/ppermute | solution.py:438
  3.4 8.4 %collective-permute-start.1 = (bf16[4,2048]{1,0:T(4,128)(2,1)S(1)}, bf16[4,2048]{1,0:T(4,128)(2,1)S(1)}, u32[]{:S(2)}, u32[]{:S(2)}) collective-permute-start(bf16[4,2048]{1,0:T(4,128)(2,1)S(1)} %get-tuple-element.30), channel_id=1, source_target_pairs={{4,8},{8,4},{12,16},{16,12},{20,24},{24,20},{5,9},{9,5},{13,17},{1... | collective-permute-start | bytes 49160 | tf_op jit(solution)/shard_map/ppermute | solution.py:443
  11.8 2.9 %copy-start = (f32[10,2,320,128]{3,2,1,0:T(8,128)S(1)}, f32[10,2,320,128]{3,2,1,0:T(8,128)}, u32[]{:S(2)}) copy-start(f32[10,2,320,128]{3,2,1,0:T(8,128)} %get-tuple-element.31.proj) | copy-start | bytes 9830404
  14.4 3.6 %collective-permute-start.4 = (bf16[2,160,512]{2,1,0:T(8,128)(2,1)S(1)}, bf16[2,160,512]{2,1,0:T(8,128)(2,1)S(1)}, u32[]{:S(2)}, u32[]{:S(2)}) collective-permute-start(bf16[2,160,512]{2,1,0:T(8,128)(2,1)S(1)} %get-tuple-element.39), channel_id=1, source_target_pairs={{0,4},{4,0},{8,12},{12,8},{16,20},{20,16},{24,28},{28,24},{1,5},{5... | collective-permute-start | bytes 983048 | tf_op jit(solution)/shard_map/ppermute | solution.py:447
  17.6 1.7 %collective-permute-start.3 = (bf16[2,160,512]{2,1,0:T(8,128)(2,1)S(1)}, bf16[2,160,512]{2,1,0:T(8,128)(2,1)S(1)}, u32[]{:S(2)}, u32[]{:S(2)}) collective-permute-start(bf16[2,160,512]{2,1,0:T(8,128)(2,1)S(1)} %get-tuple-element.36), channel_id=1, source_target_pairs={{0,4},{4,0},{8,12},{12,8},{16,20},{20,16},{24,28},{28,24},{1,5},{5... | collective-permute-start | bytes 983048 | tf_op jit(solution)/shard_map/ppermute | solution.py:449
  20.5 5.9 %collective-permute-start.5 = (bf16[4,240,128]{2,1,0:T(8,128)(2,1)S(1)}, bf16[4,240,128]{2,1,0:T(8,128)(2,1)S(1)}, u32[]{:S(2)}, u32[]{:S(2)}) collective-permute-start(bf16[4,240,128]{2,1,0:T(8,128)(2,1)S(1)} %get-tuple-element.46), channel_id=1, source_target_pairs={{0,1},{1,0},{2,3},{3,2},{4,12},{5,13},{6,14},{7,15},{8,9},{9,8},{1... | collective-permute-start | bytes 737288 | tf_op jit(solution)/shard_map/ppermute | solution.py:409
  20.7 10.8 %collective-permute-start.6 = (bf16[4,240,128]{2,1,0:T(8,128)(2,1)S(1)}, bf16[4,240,128]{2,1,0:T(8,128)(2,1)S(1)}, u32[]{:S(2)}, u32[]{:S(2)}) collective-permute-start(bf16[4,240,128]{2,1,0:T(8,128)(2,1)S(1)} %get-tuple-element.45), channel_id=1, source_target_pairs={{0,2},{1,3},{2,0},{3,1},{4,20},{5,21},{6,22},{7,23},{8,10},{9,11},... | collective-permute-start | bytes 737288 | tf_op jit(solution)/shard_map/ppermute | solution.py:409
  23.0 12.4 %collective-permute-start.7 = (bf16[4,240,128]{2,1,0:T(8,128)(2,1)S(1)}, bf16[4,240,128]{2,1,0:T(8,128)(2,1)S(1)}, u32[]{:S(2)}, u32[]{:S(2)}) collective-permute-start(bf16[4,240,128]{2,1,0:T(8,128)(2,1)S(1)} %get-tuple-element.44), channel_id=1, source_target_pairs={{0,3},{1,2},{2,1},{3,0},{4,28},{5,29},{6,30},{7,31},{8,11},{9,10},... | collective-permute-start | bytes 737288 | tf_op jit(solution)/shard_map/ppermute | solution.py:409
  36.1 5.5 %collective-permute-start.10 = (bf16[240,128]{1,0:T(8,128)(2,1)S(1)}, bf16[240,128]{1,0:T(8,128)(2,1)S(1)}, u32[]{:S(2)}, u32[]{:S(2)}) collective-permute-start(bf16[240,128]{1,0:T(8,128)(2,1)S(1)} %get-tuple-element.43), channel_id=1, source_target_pairs={{0,24},{1,25},{2,26},{3,27},{4,7},{5,6},{6,5},{7,4},{8,16},{9,17},... | collective-permute-start | bytes 184328 | tf_op jit(solution)/shard_map/ppermute | solution.py:409
  36.7 5.1 %collective-permute-start.8 = (bf16[240,128]{1,0:T(8,128)(2,1)S(1)}, bf16[240,128]{1,0:T(8,128)(2,1)S(1)}, u32[]{:S(2)}, u32[]{:S(2)}) collective-permute-start(bf16[240,128]{1,0:T(8,128)(2,1)S(1)} %get-tuple-element.41), channel_id=1, source_target_pairs={{0,8},{1,9},{2,10},{3,11},{4,5},{5,4},{6,7},{7,6},{8,0},{9,1},{10,... | collective-permute-start | bytes 184328 | tf_op jit(solution)/shard_map/ppermute | solution.py:409
  39.5 3.1 %collective-permute-start.9 = (bf16[240,128]{1,0:T(8,128)(2,1)S(1)}, bf16[240,128]{1,0:T(8,128)(2,1)S(1)}, u32[]{:S(2)}, u32[]{:S(2)}) collective-permute-start(bf16[240,128]{1,0:T(8,128)(2,1)S(1)} %get-tuple-element.42), channel_id=1, source_target_pairs={{0,16},{1,17},{2,18},{3,19},{4,6},{5,7},{6,4},{7,5},{8,24},{9,25},... | collective-permute-start | bytes 184328 | tf_op jit(solution)/shard_map/ppermute | solution.py:409

commit v2 on v1

--- a/solution.py
+++ b/solution.py
@@ -16,26 +16,32 @@
 LANES = 128
 SUB = 8
 PAD = 8
-VMEM_BYTES = 48 * 1024 * 1024
+FIRST = ((0, 0), (3, 2), (1, 1), (2, 3))
+VMEM_BYTES = 14 * 1024 * 1024
+
+
+def position():
+    seq = lax.axis_index("seq")
+    return lax.rem(seq, 2), lax.div(seq, 2), lax.axis_index("dp")
 
 
 def vmem(count):
     return [pl.BlockSpec(memory_space=pltpu.VMEM)] * count
 
 
-def smem():
-    return [pl.BlockSpec(memory_space=pltpu.SMEM)]
-
-
 def params():
     return pltpu.CompilerParams(vmem_limit_bytes=VMEM_BYTES)
 
 
 def shape(dims, dtype):
-    return jax.ShapeDtypeStruct(dims, dtype)
-
-
-def edges_kernel(where_ref, x_ref, u_ref, pair_ref, far_ref, x_low, x_high, u_low, u_high, sems):
+    return pltpu.VMEM(dims, dtype)
+
+
+def here(array):
+    return pltpu.with_memory_space_constraint(array, pltpu.VMEM)
+
+
+def edges_kernel(x_ref, u_ref, pair_ref, far_ref, x_low, x_high, u_low, u_high, sems):
     batch, rows, chans = x_ref.shape
     copies = []
     for i, (src, low, high) in enumerate(((x_ref, x_low, x_high), (u_ref, u_low, u_high))):
@@ -45,7 +51,7 @@
         copy.start()
     for copy in copies:
         copy.wait()
-    even = where_ref[0] == 0
+    even = position()[0] == 0
     for low, high, lo, hi in ((x_low, x_high, 0, chans), (u_low, u_high, chans, pair_ref.shape[1])):
         first = jnp.concatenate([low[b].astype(F32)[:2] for b in range(batch)], axis=0)
         final = jnp.concatenate([high[b].astype(F32)[14:] for b in range(batch)], axis=0)
@@ -53,20 +59,37 @@
         far_ref[:, lo:hi] = jnp.where(even, first, final).astype(BF16)
 
 
-def edges(where, x, u):
+def edges(x, u):
     batch, _, chans = x.shape
     feats = u.shape[2]
     return pl.pallas_call(
         edges_kernel,
         out_shape=[shape((2 * batch, chans + feats), BF16)] * 2,
-        in_specs=smem() + [pl.BlockSpec(memory_space=pltpu.HBM)] * 2,
+        in_specs=[pl.BlockSpec(memory_space=pltpu.HBM)] * 2,
         out_specs=vmem(2),
         scratch_shapes=[pltpu.VMEM((batch, 16, chans), BF16)] * 2 + [pltpu.VMEM((batch, 16, feats), BF16)] * 2
         + [pltpu.SemaphoreType.DMA((4,))],
         compiler_params=params(),
+        cost_estimate=pl.CostEstimate(flops=0, bytes_accessed=1_000, transcendentals=0),
+        name="edges",
+    )(x, u)
+
+
+def relay_kernel(pair_ref, far_ref, pair_out, far_out):
+    pair_out[...] = pair_ref[...]
+    far_out[...] = far_ref[...]
+
+
+def relay(pair, far):
+    return pl.pallas_call(
+        relay_kernel,
+        out_shape=[shape(pair.shape, BF16)] * 2,
+        in_specs=vmem(2),
+        out_specs=vmem(2),
+        compiler_params=params(),
         cost_estimate=pl.CostEstimate(flops=10_000_000_000, bytes_accessed=1_000_000, transcendentals=0),
-        name="edges",
-    )(where, x, u)
+        name="relay",
+    )(here(pair), here(far))
 
 
 def odd_slope(w):
@@ -153,15 +176,15 @@
         compiler_params=params(),
         cost_estimate=pl.CostEstimate(flops=4_000_000_000, bytes_accessed=4_000_000, transcendentals=0),
         name="project",
-    )(x, w, u, k)
+    )(*map(here, (x, w, u, k)))
 
 
 def around(low, high):
     return jnp.concatenate([low, jnp.zeros((SUB - 4, low.shape[1]), low.dtype), high], axis=0)
 
 
-def halo_of(where_ref, pair_ref, far_ref, lo, hi, batch):
-    even = where_ref[0] == 0
+def halo_of(pair_ref, far_ref, lo, hi, batch):
+    even = position()[0] == 0
     pair, far = pair_ref[:, lo:hi].astype(F32), far_ref[:, lo:hi].astype(F32)
     low, high = jnp.where(even, far, pair), jnp.where(even, pair, far)
     return [around(low[2 * b:2 * b + 2], high[2 * b:2 * b + 2]) for b in range(batch)]
@@ -213,13 +236,13 @@
 
 
 def early_kernel(
-    where_ref, x_ref, w_ref, u_ref, k_ref, pair_ref, far_ref, proj, inner_ref,
+    x_ref, w_ref, u_ref, k_ref, pair_ref, far_ref, proj, inner_ref,
     gp_ref, halo_ref, *rest,
 ):
     *parts, gpt = rest
     batch, rows, chans = x_ref.shape
-    halo_x = halo_of(where_ref, pair_ref, far_ref, 0, chans, batch)
-    halo_u = halo_of(where_ref, pair_ref, far_ref, chans, pair_ref.shape[1], batch)
+    halo_x = halo_of(pair_ref, far_ref, 0, chans, batch)
+    halo_u = halo_of(pair_ref, far_ref, chans, pair_ref.shape[1], batch)
     halo_x = jnp.concatenate(halo_x, axis=0).astype(BF16)
     halo_all = jnp.dot(halo_x, w_ref[...], preferred_element_type=F32).astype(BF16).astype(F32)
     for b in range(batch):
@@ -228,53 +251,53 @@
     for j in range(gp_ref.shape[2] // LANES):
         finish(j, proj, u_ref, k_ref, halo_p, halo_u, inner_ref, gp_ref, j * LANES, gpt)
     if parts:
-        hand_out(where_ref[0], gpt, *parts)
+        hand_out(position()[0], gpt, *parts)
 
 
 def late_kernel(
-    col, where_ref, u_ref, k_ref, pair_ref, far_ref, proj, halo_ref,
+    col, u_ref, k_ref, pair_ref, far_ref, proj, halo_ref,
     gp_ref, mine_ref, send_ref, wide, out, gpt,
 ):
     batch, rows, feats = u_ref.shape
     chans = pair_ref.shape[1] - feats
-    halo_u = halo_of(where_ref, pair_ref, far_ref, chans, pair_ref.shape[1], batch)
+    halo_u = halo_of(pair_ref, far_ref, chans, pair_ref.shape[1], batch)
     halo_p = [halo_ref[b] for b in range(batch)]
     for t in range(gp_ref.shape[2] // LANES):
         j = col // LANES + t
         inner_gradients(j, proj, u_ref, k_ref, wide, out, gp_ref, t * LANES)
         finish(j, proj, u_ref, k_ref, halo_p, halo_u, gp_ref, gp_ref, t * LANES, gpt)
-    hand_out(where_ref[0], gpt, mine_ref, send_ref)
-
-
-def early(where, x, w, u, k, pair, far, proj, inner, strips, strip):
+    hand_out(position()[0], gpt, mine_ref, send_ref)
+
+
+def early(x, w, u, k, pair, far, proj, inner, strips, strip):
     batch, rows, _ = x.shape
     ncol = inner.shape[2]
     parts = [shape((strips, strip, batch * rows), BF16)] * 2 if strips else []
     return pl.pallas_call(
         early_kernel,
         out_shape=[shape(inner.shape, BF16), shape((batch, SUB, w.shape[1]), F32)] + parts,
-        in_specs=smem() + vmem(8),
+        in_specs=vmem(8),
         out_specs=vmem(2 + len(parts)),
         scratch_shapes=[pltpu.VMEM((ncol, batch * rows), BF16)],
         compiler_params=params(),
         cost_estimate=pl.CostEstimate(flops=1_000_000_000, bytes_accessed=4_000_000, transcendentals=0),
         name="early",
-    )(where, x, w, u, k, pair, far, proj, inner)
-
-
-def late(where, u, k, pair, far, proj, halo, col, ncol, strips, strip):
+    )(*map(here, (x, w, u, k, pair, far, proj, inner)))
+
+
+def late(u, k, pair, far, proj, halo, col, ncol, strips, strip):
     batch, rows, _ = u.shape
     part = shape((strips, strip, batch * rows), BF16)
     return pl.pallas_call(
         functools.partial(late_kernel, col),
         out_shape=[shape((batch, rows, ncol), BF16), part, part],
-        in_specs=smem() + vmem(6),
+        in_specs=vmem(6),
         out_specs=vmem(3),
         scratch_shapes=sample_scratch(batch, rows) + [pltpu.VMEM((ncol, batch * rows), BF16)],
         compiler_params=params(),
         cost_estimate=pl.CostEstimate(flops=4_000_000_000, bytes_accessed=4_000_000, transcendentals=0),
         name="late",
-    )(where, u, k, pair, far, proj, halo)
+    )(*map(here, (u, k, pair, far, proj, halo)))
 
 
 def own_kernel(x_ref, other_ref, mine_a, mine_b, got_a, out_ref):
@@ -299,69 +322,90 @@
         compiler_params=params(),
         cost_estimate=pl.CostEstimate(flops=1_000_000_000, bytes_accessed=4_000_000, transcendentals=0),
         name="own",
-    )(x, other, mine_a, mine_b, got_a)
-
-
-def pack_kernel(where_ref, other_ref, got_b, sums_ref, out_ref, whole):
-    core, zed, dee = where_ref[0], where_ref[1], where_ref[2]
+    )(*map(here, (x, other, mine_a, mine_b, got_a)))
+
+
+def pack_kernel(other_ref, got_b, sums_in, sums_ref, *outs):
+    core, zed, dee = position()
     batch, rows, chans = other_ref.shape
     other = other_ref[...].reshape(batch * rows, chans)
     half, strip, _ = got_b.shape
     for z in range(half):
-        whole[z] = sums_ref[half + z] + jnp.dot(got_b[z], other, preferred_element_type=F32)
+        sums_ref[half + z] = sums_in[half + z] + jnp.dot(got_b[z], other, preferred_element_type=F32)
     left = lax.broadcasted_iota(jnp.int32, (strip // 2, LANES), 1) < LANES // 2
-    for z in range(2 * half):
-        source = sums_ref.at[z] if z < half else whole.at[z - half]
-        for b in range(4):
-            slot = jnp.where(core == 0, jnp.bitwise_xor(dee, b), jnp.bitwise_xor(zed, z))
-            place = jnp.where(core == 0, z, b)
-            full = (3 * (b // 2) + 2 * (b % 2)) * LANES
-            rest = (3 * (b // 2) + 1) * LANES
-            top, bottom = source[0:strip // 2, rest:rest + LANES], source[strip // 2:strip, rest:rest + LANES]
-            if b % 2 == 0:
-                packed = jnp.where(left, top, pltpu.roll(bottom, LANES // 2, 1))
-            else:
-                packed = jnp.where(left, pltpu.roll(top, LANES // 2, 1), bottom)
-            out_ref[slot, place, 0:strip] = source[0:strip, full:full + LANES].astype(BF16)
-            out_ref[slot, place, strip:strip + strip // 2] = packed.astype(BF16)
-
-
-def pack(where, other, got_b, sums):
+    for (d_turn, z_turn), out in zip(FIRST, outs):
+        for j in range(4):
+            z = jnp.where(core == 0, j, jnp.bitwise_xor(zed, z_turn))
+            b = jnp.where(core == 0, jnp.bitwise_xor(dee, d_turn), j)
+            y, odd = lax.div(b, 2), lax.rem(b, 2)
+            full = pl.multiple_of((3 * y + 2 * odd) * LANES, LANES)
+            rest = pl.multiple_of((3 * y + 1) * LANES, LANES)
+            top, bottom = sums_ref[z, 0:strip // 2, pl.ds(rest, LANES)], sums_ref[z, strip // 2:strip, pl.ds(rest, LANES)]
+            turned = pltpu.roll(jnp.where(left, bottom, top), LANES // 2, 1)
+            kept = jnp.where(odd == 0, top, bottom)
+            out[j, 0:strip] = sums_ref[z, :, pl.ds(full, LANES)].astype(out.dtype)
+            out[j, strip:strip + strip // 2] = jnp.where(left == (odd == 0), kept, turned).astype(out.dtype)
+
+
+def pack(other, got_b, sums):
     half, strip, _ = got_b.shape
+    block = (4, strip + strip // 2, LANES)
     return pl.pallas_call(
         pack_kernel,
-        out_shape=shape((4, 4, strip + strip // 2, LANES), BF16),
-        in_specs=smem() + vmem(3),
-        out_specs=vmem(1)[0],
-        scratch_shapes=[pltpu.VMEM((half, strip, other.shape[2]), F32)],
+        out_shape=[shape(sums.shape, F32), shape(block, F32)] + [shape(block, BF16)] * 3,
+        in_specs=vmem(3),
+        out_specs=vmem(5),
+        input_output_aliases={2: 0},
         compiler_params=params(),
         name="pack",
-    )(where, other, got_b, sums)
-
-
-def fold_kernel(where_ref, own_ref, one_ref, two_ref, three_ref, *outs):
-    core, zed, dee = where_ref[0], where_ref[1], where_ref[2]
+    )(*map(here, (other, got_b, sums)))[1:]
+
+
+def fold_kernel(own_ref, one_ref, two_ref, three_ref, token, *outs):
+    core, zed, dee = position()
     mine = jnp.where(core == 0, zed, dee)
-    for k, out in enumerate(outs):
+    for k in (3, 2, 1, 0):
         j = jnp.bitwise_xor(mine, k)
-        total = own_ref[0, j].astype(F32) + one_ref[j].astype(F32) + two_ref[j].astype(F32) + three_ref[j].astype(F32)
-        out[...] = total.astype(out.dtype)
-
-
-def fold(where, whole, parts):
+        total = own_ref[j] + one_ref[j].astype(F32) + two_ref[j].astype(F32) + three_ref[j].astype(F32)
+        outs[k][...] = total.astype(outs[k].dtype)
+
+
+def fold(parts, token):
     block = parts[0].shape[1:]
     return pl.pallas_call(
         fold_kernel,
         out_shape=[shape(block, F32)] + [shape(block, BF16)] * 3,
-        in_specs=smem() + vmem(4),
+        in_specs=vmem(5),
         out_specs=vmem(4),
         compiler_params=params(),
         name="fold",
-    )(where, whole, *parts)
-
-
-def last_kernel(scale, where_ref, own_ref, one_ref, two_ref, three_ref, out_ref):
-    odd = where_ref[2] % 2
+    )(*map(here, parts), here(token))
+
+
+def input_kernel(gp_a, gp_b, w_ref, out_ref, token):
+    token[...] = jnp.zeros_like(token)
+    cut = gp_a.shape[2]
+    for b in range(out_ref.shape[0]):
+        total = lax.dot_general(gp_a[b], w_ref[:, :cut], (((1,), (1,)), ((), ())), preferred_element_type=F32)
+        total += lax.dot_general(gp_b[b], w_ref[:, cut:], (((1,), (1,)), ((), ())), preferred_element_type=F32)
+        out_ref[b] = total.astype(BF16)
+
+
+def input_gradient(gp_a, gp_b, w):
+    batch, rows, _ = gp_a.shape
+    return pl.pallas_call(
+        input_kernel,
+        out_shape=[jax.ShapeDtypeStruct((batch, rows, w.shape[0]), BF16), shape((SUB, LANES), F32)],
+        in_specs=vmem(3),
+        out_specs=vmem(2),
+        compiler_params=params(),
+        cost_estimate=pl.CostEstimate(flops=2_000_000_000, bytes_accessed=1_000_000, transcendentals=0),
+        name="input_gradient",
+    )(here(gp_a), here(gp_b), here(w))
+
+
+def last_kernel(scale, own_ref, one_ref, two_ref, three_ref, out_ref):
+    odd = lax.rem(position()[2], 2)
     total = own_ref[...] + one_ref[...].astype(F32) + two_ref[...].astype(F32) + three_ref[...].astype(F32)
     total = total * scale
     strip = out_ref.shape[0]
@@ -380,16 +424,16 @@
         out_ref[:, half:] = full
 
 
-def last(where, parts, scale):
+def last(parts, scale):
     strip = parts[0].shape[0] * 2 // 3
     return pl.pallas_call(
         functools.partial(last_kernel, scale),
-        out_shape=shape((strip, LANES + LANES // 2), F32),
-        in_specs=smem() + vmem(4),
+        out_shape=jax.ShapeDtypeStruct((strip, LANES + LANES // 2), F32),
+        in_specs=vmem(4),
         out_specs=vmem(1)[0],
         compiler_params=params(),
         name="last",
-    )(where, *parts).T
+    )(*parts).T
 
 
 def near_pairs():
@@ -409,10 +453,10 @@
     return lax.ppermute(array, ("seq", "dp"), pairs)
 
 
-def spread(where, x, w, u, k, pair, far):
+def spread(x, w, u, k, pair, far):
     batch = x.shape[0]
     proj, inner = project(x, w, u, k, w.shape[1])
-    gp, _ = early(where, x, w, u, k, pair, far, proj, inner, 0, 0)
+    gp, _ = early(x, w, u, k, pair, far, proj, inner, 0, 0)
     input_grad = jnp.einsum("bpf,cf->bpc", gp, w, preferred_element_type=F32).astype(BF16)
     partial = lax.dot_general(x, gp, (((0, 1), (0, 1)), ((), ())), preferred_element_type=F32)
     over_seq = lax.psum_scatter(partial, "seq", scatter_dimension=1, tiled=True)
@@ -426,37 +470,33 @@
     n_seq, n_dp = lax.axis_size("seq"), lax.axis_size("dp")
     seq, dee = lax.axis_index("seq"), lax.axis_index("dp")
     core, zed = seq % 2, seq // 2
-    where = jnp.stack([core, zed, dee, seq]).astype(jnp.int32)
     strip = feats // n_seq
     strips = n_seq // 4
     ncol = feats // 2
 
     there = functools.partial(pltpu.with_memory_space_constraint, memory_space=pltpu.HBM)
-    pair, far = edges(where, there(skip_input), there(upstream))
-    x, w, u, k, pair, far = lax.optimization_barrier(
-        (skip_input, proj_weight, upstream, depth_kernel, pair, far))
+    pair, far = edges(there(skip_input), there(upstream))
+    pair, far = relay(pair, far)
+    x, w, u, k = skip_input, proj_weight, upstream, depth_kernel
     pair = lax.ppermute(pair, "seq", near_pairs())
     if n_seq != 8 or n_dp != 4 or chans != 4 * (LANES + LANES // 2):
-        return spread(where, x, w, u, k, pair, lax.ppermute(far, "seq", far_pairs()))
-    here = functools.partial(pltpu.with_memory_space_constraint, memory_space=pltpu.VMEM)
+        return spread(x, w, u, k, pair, lax.ppermute(far, "seq", far_pairs()))
     other = lax.ppermute(skip_input, "seq", near_pairs())
     far = lax.ppermute(far, "seq", far_pairs())
-    x, w, u, k = here(x), here(w), here(u), here(k)
     proj, inner = project(x, w, u, k, ncol)
-    gp_a, halo, mine_a, send_a = early(where, x, w, u, k, pair, far, proj, inner, strips, strip)
+    gp_a, halo, mine_a, send_a = early(x, w, u, k, pair, far, proj, inner, strips, strip)
     got_a = lax.ppermute(send_a, "seq", near_pairs())
-    gp_b, mine_b, send_b = late(where, u, k, pair, far, proj, halo, ncol, feats - ncol, strips, strip)
+    gp_b, mine_b, send_b = late(u, k, pair, far, proj, halo, ncol, feats - ncol, strips, strip)
     got_b = lax.ppermute(send_b, "seq", near_pairs())
     sums = own(x, other, mine_a, mine_b, got_a)
-    whole = pack(where, other, got_b, sums)
-
-    gp = jnp.concatenate([gp_a, gp_b], axis=2)
-    input_grad = jnp.einsum("bpf,cf->bpc", gp, proj_weight, preferred_element_type=F32).astype(BF16)
-    z_bits = [m * 2 * n_dp for m in (1, 2, 3)]
-    got = [exchange(whole[m], m, z) for m, z in zip((1, 2, 3), z_bits)]
-    mine, *messages = fold(where, whole, got)
-    got = [exchange(message, z, m) for message, m, z in zip(messages, (1, 2, 3), z_bits)]
-    return input_grad, last(where, [mine] + got, 1.0 / (batch * n_dp))
+    own_blocks, *messages = pack(other, got_b, sums)
+
+    input_grad, token = input_gradient(gp_a, gp_b, w)
+    z_bits = [m * 2 * n_dp for m in range(4)]
+    got = [exchange(message, d, z_bits[z]) for message, (d, z) in zip(messages, FIRST[1:])]
+    own_block, *messages = fold([own_blocks] + got, token)
+    got = [exchange(messages[k - 1], z_bits[k], k) for k in (3, 2, 1)]
+    return input_grad, last([own_block] + got, 1.0 / (batch * n_dp))
 
 
 def solution(mesh):

time: 44.1 us -> 35.2 us (0.80)
  the two profiles are of different devices: /device:TPU:11 before, /device:TPU:0 now
where the time goes in v2:
time: 35.2 us; the launch traced here: 35.1 us
  starting transfers between devices  12.8 us (36%)
  Pallas kernels  12 us (34%)
  waiting for transfers between devices  8.27 us (23%)
  local copies, waits for them, and re-layouts  1.24 us (4%)
  between operations  0.75 us (2%)
    ppermute x6, starting transfers between devices, exchange(): return lax.ppermute(array, ('seq', 'dp'), pairs)  8.01 us
    ppermute x6, waiting for transfers between devices, exchange(): return lax.ppermute(array, ('seq', 'dp'), pairs)  7.61 us
    ppermute x1, starting transfers between devices, on_device(): got_a = lax.ppermute(send_a, 'seq', near_pairs())  3.28 us
    pallas_call x1, Pallas kernels, project(): pl.pallas_call(project_kernel, out_shape=[shape((feats // LANES, batch, r...  3.07 us
    pallas_call x1, Pallas kernels, late(): pl.pallas_call(functools.partial(late_kernel, col), out_shape=[shape((bat...  2.39 us
    pallas_call x1, Pallas kernels, input_gradient(): pl.pallas_call(input_kernel, out_shape=[jax.ShapeDtypeStruct((batch, rows...  2.32 us
    unnamed x8, local copies, waits for them, and re-layouts  1.24 us
    pallas_call x1, Pallas kernels, edges(): pl.pallas_call(edges_kernel, out_shape=[shape((2 * batch, chans + feats),...  1.05 us
  transfers between devices with their start and end apart: 11, of which 5 were waited for; matrix products, arithmetic and copies ran while one was open for 0% of the time, Pallas kernels for 29%

profile of v2, /device:TPU:0, one launch (start us, length us, event | category | flops | bytes accessed | tf_op | source)
XLA Modules:
  0.0 35.1 jit_solution(16650452415577103018)
XLA Ops:
  0.6 0.5 %collective-permute-start.2 = (bf16[2,256,768]{2,1,0:T(8,128)(2,1)}, bf16[2,256,768]{2,1,0:T(8,128)(2,1)S(1)}, u32[]{:S(2)}, u32[]{:S(2)}) collective-permute-start(bf16[2,256,768]{2,1,0:T(8,128)(2,1)} %x_ref.7), channel_id=1, source_target_pairs={{0,4},{4,0},{8,12},{12,8},{16,20},{20,16},{24,28},{28,24},{1,5},{5... | collective-permute-start | bytes 2359304 | tf_op jit(solution)/shard_map/ppermute | solution.py:484
  1.1 1.1 %edges.1 = (bf16[4,2048]{1,0:T(4,128)(2,1)S(1)}, bf16[4,2048]{1,0:T(4,128)(2,1)S(1)}) custom-call(bf16[2,256,768]{2,1,0:T(8,128)(2,1)} %x_ref.7, bf16[2,256,1280]{2,1,0:T(8,128)(2,1)} %u_ref.7), custom_call_target="tpu_custom_call" | custom-call | bytes 1000 | tf_op jit(solution)/shard_map/edges/pallas_call | solution.py:65
  2.2 0.0 copy-start
  2.2 0.0 copy-start.1
  2.2 0.0 copy-start.2
  2.2 0.0 copy-start.3
  2.3 0.1 collective-permute-start
  2.4 0.8 %collective-permute-start.1 = (bf16[4,2048]{1,0:T(4,128)(2,1)S(1)}, bf16[4,2048]{1,0:T(4,128)(2,1)S(1)}, u32[]{:S(2)}, u32[]{:S(2)}) collective-permute-start(bf16[4,2048]{1,0:T(4,128)(2,1)S(1)} %get-tuple-element.28), channel_id=1, source_target_pairs={{4,8},{8,4},{12,16},{16,12},{20,24},{24,20},{5,9},{9,5},{13,17},{1... | collective-permute-start | bytes 49160 | tf_op jit(solution)/shard_map/ppermute | solution.py:485
  3.2 0.2 copy-done
  3.3 0.4 %copy-done.1 = bf16[2,256,1280]{2,1,0:T(8,128)(2,1)S(1)} copy-done((bf16[2,256,1280]{2,1,0:T(8,128)(2,1)S(1)}, bf16[2,256,1280]{2,1,0:T(8,128)(2,1)}, u32[]{:S(2)}) %copy-start.1) | copy-done | bytes 1310744
  3.8 0.6 %copy-done.2 = bf16[768,1280]{1,0:T(8,128)(2,1)S(1)} copy-done((bf16[768,1280]{1,0:T(8,128)(2,1)S(1)}, bf16[768,1280]{1,0:T(8,128)(2,1)}, u32[]{:S(2)}) %copy-start.2) | copy-done | bytes 1966104
  4.4 0.0 copy-done.3
  4.4 3.1 %project.1 = (f32[10,2,320,128]{3,2,1,0:T(8,128)S(1)}, bf16[2,256,640]{2,1,0:T(8,128)(2,1)S(1)}) custom-call(bf16[2,256,768]{2,1,0:T(8,128)(2,1)S(1)} %copy-done, bf16[768,1280]{1,0:T(8,128)(2,1)S(1)} %copy-done.2, bf16[2,256,1280]{2,1,0:T(8,128)(2,1)S(1)} %copy-done.1, f32[3,1280]{1,0:T(4,128)S(1)} %copy-done.3), custom_call_target="tpu_custom_call" | custom-call | flops 4000000000 | bytes 4000000 | tf_op jit(solution)/shard_map/project/pallas_call | solution.py:170
  7.5 0.0 collective-permute-done.pair_ref
  7.5 0.0 collective-permute-done.1.far_ref
  7.5 0.6 %early.1 = (bf16[2,256,640]{2,1,0:T(8,128)(2,1)S(1)}, f32[2,8,1280]{2,1,0:T(8,128)S(1)}, bf16[2,160,512]{2,1,0:T(8,128)(2,1)S(1)}, bf16[2,160,512]{2,1,0:T(8,128)(2,1)S(1)}) custom-call(bf16[2,256,768]{2,1,0:T(8,128)(2,1)S(1)} %copy-done, bf16[768,1280]{1,0:T(8,128)(2,1)S(1)} %copy-done.2, bf16[2,256,1280]{2,1,0:T(8,128)(2,1)S(1)} %copy-done.1, ...), custom_call_target="tpu_custom_call" | custom-call | flops 1000000000 | bytes 4000000 | tf_op jit(solution)/shard_map/early/pallas_call | solution.py:276
  8.1 3.3 %collective-permute-start.4 = (bf16[2,160,512]{2,1,0:T(8,128)(2,1)S(1)}, bf16[2,160,512]{2,1,0:T(8,128)(2,1)S(1)}, u32[]{:S(2)}, u32[]{:S(2)}) collective-permute-start(bf16[2,160,512]{2,1,0:T(8,128)(2,1)S(1)} %get-tuple-element.38), channel_id=1, source_target_pairs={{0,4},{4,0},{8,12},{12,8},{16,20},{20,16},{24,28},{28,24},{1,5},{5... | collective-permute-start | bytes 983048 | tf_op jit(solution)/shard_map/ppermute | solution.py:488
  11.4 2.4 %late.1 = (bf16[2,256,640]{2,1,0:T(8,128)(2,1)S(1)}, bf16[2,160,512]{2,1,0:T(8,128)(2,1)S(1)}, bf16[2,160,512]{2,1,0:T(8,128)(2,1)S(1)}) custom-call(bf16[2,256,1280]{2,1,0:T(8,128)(2,1)S(1)} %copy-done.1, f32[3,1280]{1,0:T(4,128)S(1)} %copy-done.3, bf16[4,2048]{1,0:T(4,128)(2,1)S(1)} %collective-permute-done.pair_ref, ...), custom_call_target="tpu_custom_call" | custom-call | flops 4000000000 | bytes 4000000 | tf_op jit(solution)/shard_map/late/pallas_call | solution.py:291
  13.8 0.1 collective-permute-start.3
  13.8 0.0 collective-permute-done.4.got_a
  13.8 0.0 collective-permute-done.2.other_ref
  13.9 0.9 %own.1.sums_in = f32[4,160,768]{2,1,0:T(8,128)S(1)} custom-call(bf16[2,256,768]{2,1,0:T(8,128)(2,1)S(1)} %copy-done, bf16[2,256,768]{2,1,0:T(8,128)(2,1)S(1)} %collective-permute-done.2.other_ref, bf16[2,160,512]{2,1,0:T(8,128)(2,1)S(1)} %get-tuple-element.36.mine_a, bf16[2,160,512]{2,1,0:T(8,128)(2,1)S(1)} %get-tuple-element.37.mine_b, ...), custom_call_target="tpu_custom_call" | custom-call | flops 1000000000 | bytes 4000000 | tf_op jit(solution)/shard_map/own/pallas_call | solution.py:317
  14.8 0.6 %collective-permute-done.3.got_b = bf16[2,160,512]{2,1,0:T(8,128)(2,1)S(1)} collective-permute-done((bf16[2,160,512]{2,1,0:T(8,128)(2,1)S(1)}, bf16[2,160,512]{2,1,0:T(8,128)(2,1)S(1)}, u32[]{:S(2)}, u32[]{:S(2)}) %collective-permute-start.3) | collective-permute-done | bytes 327712 | tf_op jit(solution)/shard_map/ppermute | solution.py:490
  15.4 0.8 %pack.1 = (f32[4,160,768]{2,1,0:T(8,128)S(1)}, f32[4,240,128]{2,1,0:T(8,128)S(1)}, bf16[4,240,128]{2,1,0:T(8,128)(2,1)S(1)}, bf16[4,240,128]{2,1,0:T(8,128)(2,1)S(1)}, bf16[4,240,128]{2,1,0:T(8,128)(2,1)S(1)}) custom-call(bf16[2,256,768]{2,1,0:T(8,128)(2,1)S(1)} %collective-permute-done.2.other_ref, ...), custom_call_target="tpu_custom_call", output_to_operand_aliasing={{0}: (2, {})} | custom-call | tf_op jit(solution)/shard_map/pack/pallas_call | solution.py:353
  16.2 2.5 %collective-permute-start.5 = (bf16[4,240,128]{2,1,0:T(8,128)(2,1)S(1)}, bf16[4,240,128]{2,1,0:T(8,128)(2,1)S(1)}, u32[]{:S(2)}, u32[]{:S(2)}) collective-permute-start(bf16[4,240,128]{2,1,0:T(8,128)(2,1)S(1)} %get-tuple-element.40), channel_id=1, source_target_pairs={{0,3},{1,2},{2,1},{3,0},{4,20},{5,21},{6,22},{7,23},{8,11},{9,10},... | collective-permute-start | bytes 737288 | tf_op jit(solution)/shard_map/ppermute | solution.py:453
  18.7 0.5 %collective-permute-start.6 = (bf16[4,240,128]{2,1,0:T(8,128)(2,1)S(1)}, bf16[4,240,128]{2,1,0:T(8,128)(2,1)S(1)}, u32[]{:S(2)}, u32[]{:S(2)}) collective-permute-start(bf16[4,240,128]{2,1,0:T(8,128)(2,1)S(1)} %get-tuple-element.41), channel_id=1, source_target_pairs={{0,1},{1,0},{2,3},{3,2},{4,12},{5,13},{6,14},{7,15},{8,9},{9,8},{1... | collective-permute-start | bytes 737288 | tf_op jit(solution)/shard_map/ppermute | solution.py:453
  19.3 0.5 %collective-permute-start.7 = (bf16[4,240,128]{2,1,0:T(8,128)(2,1)S(1)}, bf16[4,240,128]{2,1,0:T(8,128)(2,1)S(1)}, u32[]{:S(2)}, u32[]{:S(2)}) collective-permute-start(bf16[4,240,128]{2,1,0:T(8,128)(2,1)S(1)} %get-tuple-element.42), channel_id=1, source_target_pairs={{0,2},{1,3},{2,0},{3,1},{4,28},{5,29},{6,30},{7,31},{8,10},{9,11},... | collective-permute-start | bytes 737288 | tf_op jit(solution)/shard_map/ppermute | solution.py:453
  19.8 2.3 %input_gradient.1 = (bf16[2,256,768]{2,1,0:T(8,128)(2,1)}, f32[8,128]{1,0:T(8,128)S(1)}) custom-call(bf16[2,256,640]{2,1,0:T(8,128)(2,1)S(1)} %get-tuple-element.31.gp_a, bf16[2,256,640]{2,1,0:T(8,128)(2,1)S(1)} %get-tuple-element.33.gp_b, bf16[768,1280]{1,0:T(8,128)(2,1)S(1)} %copy-done.2), custom_call_target="tpu_custom_call" | custom-call | flops 2000000000 | bytes 1000000 | tf_op jit(solution)/shard_map/input_gradient/pallas_call | solution.py:396
  22.1 1.3 %collective-permute-done.5.one_ref = bf16[4,240,128]{2,1,0:T(8,128)(2,1)S(1)} collective-permute-done((bf16[4,240,128]{2,1,0:T(8,128)(2,1)S(1)}, bf16[4,240,128]{2,1,0:T(8,128)(2,1)S(1)}, u32[]{:S(2)}, u32[]{:S(2)}) %collective-permute-start.5) | collective-permute-done | bytes 245792 | tf_op jit(solution)/shard_map/ppermute | solution.py:453
  23.4 2.6 %collective-permute-done.6.two_ref = bf16[4,240,128]{2,1,0:T(8,128)(2,1)S(1)} collective-permute-done((bf16[4,240,128]{2,1,0:T(8,128)(2,1)S(1)}, bf16[4,240,128]{2,1,0:T(8,128)(2,1)S(1)}, u32[]{:S(2)}, u32[]{:S(2)}) %collective-permute-start.6) | collective-permute-done | bytes 245792 | tf_op jit(solution)/shard_map/ppermute | solution.py:453
  26.1 0.0 collective-permute-done.7.three_ref
  26.1 0.1 fold.1
  26.2 2.3 %collective-permute-start.8 = (bf16[240,128]{1,0:T(8,128)(2,1)S(1)}, bf16[240,128]{1,0:T(8,128)(2,1)S(1)}, u32[]{:S(2)}, u32[]{:S(2)}) collective-permute-start(bf16[240,128]{1,0:T(8,128)(2,1)S(1)} %get-tuple-element.45), channel_id=1, source_target_pairs={{0,24},{1,25},{2,26},{3,27},{4,7},{5,6},{6,5},{7,4},{8,16},{9,17},... | collective-permute-start | bytes 184328 | tf_op jit(solution)/shard_map/ppermute | solution.py:453
  28.5 0.8 %collective-permute-start.9 = (bf16[240,128]{1,0:T(8,128)(2,1)S(1)}, bf16[240,128]{1,0:T(8,128)(2,1)S(1)}, u32[]{:S(2)}, u32[]{:S(2)}) collective-permute-start(bf16[240,128]{1,0:T(8,128)(2,1)S(1)} %get-tuple-element.46), channel_id=1, source_target_pairs={{0,16},{1,17},{2,18},{3,19},{4,6},{5,7},{6,4},{7,5},{8,24},{9,25},... | collective-permute-start | bytes 184328 | tf_op jit(solution)/shard_map/ppermute | solution.py:453
  29.3 1.3 %collective-permute-start.10 = (bf16[240,128]{1,0:T(8,128)(2,1)S(1)}, bf16[240,128]{1,0:T(8,128)(2,1)S(1)}, u32[]{:S(2)}, u32[]{:S(2)}) collective-permute-start(bf16[240,128]{1,0:T(8,128)(2,1)S(1)} %get-tuple-element.47), channel_id=1, source_target_pairs={{0,8},{1,9},{2,10},{3,11},{4,5},{5,4},{6,7},{7,6},{8,0},{9,1},{10,... | collective-permute-start | bytes 184328 | tf_op jit(solution)/shard_map/ppermute | solution.py:453
  30.7 1.6 %collective-permute-done.8.one_ref = bf16[240,128]{1,0:T(8,128)(2,1)S(1)} collective-permute-done((bf16[240,128]{1,0:T(8,128)(2,1)S(1)}, bf16[240,128]{1,0:T(8,128)(2,1)S(1)}, u32[]{:S(2)}, u32[]{:S(2)}) %collective-permute-start.8) | collective-permute-done | bytes 61472 | tf_op jit(solution)/shard_map/ppermute | solution.py:453
  32.3 2.0 %collective-permute-done.9.two_ref = bf16[240,128]{1,0:T(8,128)(2,1)S(1)} collective-permute-done((bf16[240,128]{1,0:T(8,128)(2,1)S(1)}, bf16[240,128]{1,0:T(8,128)(2,1)S(1)}, u32[]{:S(2)}, u32[]{:S(2)}) %collective-permute-start.9) | collective-permute-done | bytes 61472 | tf_op jit(solution)/shard_map/ppermute | solution.py:453
  34.3 0.0 collective-permute-done.10.three_ref
  34.3 0.8 %last.1 = f32[160,192]{1,0:T(8,128)} custom-call(f32[240,128]{1,0:T(8,128)S(1)} %get-tuple-element.44.own_ref, bf16[240,128]{1,0:T(8,128)(2,1)S(1)} %collective-permute-done.8.one_ref, bf16[240,128]{1,0:T(8,128)(2,1)S(1)} %collective-permute-done.9.two_ref, bf16[240,128]{1,0:T(8,128)(2,1)S(1)} %collective-permute-done.10.three_ref), custom_call_target="tpu_custom_call" | custom-call | tf_op jit(solution)/shard_map/last/pallas_call | solution.py:429
  (1 shorter events, 0.0 us)
Async XLA Ops:
  0.6 13.2 %collective-permute-start.2 = (bf16[2,256,768]{2,1,0:T(8,128)(2,1)}, bf16[2,256,768]{2,1,0:T(8,128)(2,1)S(1)}, u32[]{:S(2)}, u32[]{:S(2)}) collective-permute-start(bf16[2,256,768]{2,1,0:T(8,128)(2,1)} %x_ref.7), channel_id=1, source_target_pairs={{0,4},{4,0},{8,12},{12,8},{16,20},{20,16},{24,28},{28,24},{1,5},{5... | collective-permute-start | bytes 2359304 | tf_op jit(solution)/shard_map/ppermute | solution.py:484
  2.2 1.1 %copy-start = (bf16[2,256,768]{2,1,0:T(8,128)(2,1)S(1)}, bf16[2,256,768]{2,1,0:T(8,128)(2,1)}, u32[]{:S(2)}) copy-start(bf16[2,256,768]{2,1,0:T(8,128)(2,1)} %x_ref.7) | copy-start | bytes 2359300
  2.2 1.6 %copy-start.1 = (bf16[2,256,1280]{2,1,0:T(8,128)(2,1)S(1)}, bf16[2,256,1280]{2,1,0:T(8,128)(2,1)}, u32[]{:S(2)}) copy-start(bf16[2,256,1280]{2,1,0:T(8,128)(2,1)} %u_ref.7) | copy-start | bytes 3932164
  2.2 2.2 %copy-start.2 = (bf16[768,1280]{1,0:T(8,128)(2,1)S(1)}, bf16[768,1280]{1,0:T(8,128)(2,1)}, u32[]{:S(2)}) copy-start(bf16[768,1280]{1,0:T(8,128)(2,1)} %w_ref.5) | copy-start | bytes 5898244
  2.2 2.2 %copy-start.3 = (f32[3,1280]{1,0:T(4,128)S(1)}, f32[3,1280]{1,0:T(4,128)}, u32[]{:S(2)}) copy-start(f32[3,1280]{1,0:T(4,128)} %k_ref.5) | copy-start | bytes 46084
  2.3 5.2 %collective-permute-start = (bf16[4,2048]{1,0:T(4,128)(2,1)S(1)}, bf16[4,2048]{1,0:T(4,128)(2,1)S(1)}, u32[]{:S(2)}, u32[]{:S(2)}) collective-permute-start(bf16[4,2048]{1,0:T(4,128)(2,1)S(1)} %get-tuple-element.27), channel_id=1, source_target_pairs={{0,4},{4,0},{8,12},{12,8},{16,20},{20,16},{24,28},{28,24},{1,5},{5... | collective-permute-start | bytes 49160 | tf_op jit(solution)/shard_map/ppermute | solution.py:481
  2.4 5.1 %collective-permute-start.1 = (bf16[4,2048]{1,0:T(4,128)(2,1)S(1)}, bf16[4,2048]{1,0:T(4,128)(2,1)S(1)}, u32[]{:S(2)}, u32[]{:S(2)}) collective-permute-start(bf16[4,2048]{1,0:T(4,128)(2,1)S(1)} %get-tuple-element.28), channel_id=1, source_target_pairs={{4,8},{8,4},{12,16},{16,12},{20,24},{24,20},{5,9},{9,5},{13,17},{1... | collective-permute-start | bytes 49160 | tf_op jit(solution)/shard_map/ppermute | solution.py:485
  8.1 5.8 %collective-permute-start.4 = (bf16[2,160,512]{2,1,0:T(8,128)(2,1)S(1)}, bf16[2,160,512]{2,1,0:T(8,128)(2,1)S(1)}, u32[]{:S(2)}, u32[]{:S(2)}) collective-permute-start(bf16[2,160,512]{2,1,0:T(8,128)(2,1)S(1)} %get-tuple-element.38), channel_id=1, source_target_pairs={{0,4},{4,0},{8,12},{12,8},{16,20},{20,16},{24,28},{28,24},{1,5},{5... | collective-permute-start | bytes 983048 | tf_op jit(solution)/shard_map/ppermute | solution.py:488
  13.8 1.7 %collective-permute-start.3 = (bf16[2,160,512]{2,1,0:T(8,128)(2,1)S(1)}, bf16[2,160,512]{2,1,0:T(8,128)(2,1)S(1)}, u32[]{:S(2)}, u32[]{:S(2)}) collective-permute-start(bf16[2,160,512]{2,1,0:T(8,128)(2,1)S(1)} %get-tuple-element.35), channel_id=1, source_target_pairs={{0,4},{4,0},{8,12},{12,8},{16,20},{20,16},{24,28},{28,24},{1,5},{5... | collective-permute-start | bytes 983048 | tf_op jit(solution)/shard_map/ppermute | solution.py:490
  16.2 7.2 %collective-permute-start.5 = (bf16[4,240,128]{2,1,0:T(8,128)(2,1)S(1)}, bf16[4,240,128]{2,1,0:T(8,128)(2,1)S(1)}, u32[]{:S(2)}, u32[]{:S(2)}) collective-permute-start(bf16[4,240,128]{2,1,0:T(8,128)(2,1)S(1)} %get-tuple-element.40), channel_id=1, source_target_pairs={{0,3},{1,2},{2,1},{3,0},{4,20},{5,21},{6,22},{7,23},{8,11},{9,10},... | collective-permute-start | bytes 737288 | tf_op jit(solution)/shard_map/ppermute | solution.py:453
  18.7 7.3 %collective-permute-start.6 = (bf16[4,240,128]{2,1,0:T(8,128)(2,1)S(1)}, bf16[4,240,128]{2,1,0:T(8,128)(2,1)S(1)}, u32[]{:S(2)}, u32[]{:S(2)}) collective-permute-start(bf16[4,240,128]{2,1,0:T(8,128)(2,1)S(1)} %get-tuple-element.41), channel_id=1, source_target_pairs={{0,1},{1,0},{2,3},{3,2},{4,12},{5,13},{6,14},{7,15},{8,9},{9,8},{1... | collective-permute-start | bytes 737288 | tf_op jit(solution)/shard_map/ppermute | solution.py:453
  19.3 6.8 %collective-permute-start.7 = (bf16[4,240,128]{2,1,0:T(8,128)(2,1)S(1)}, bf16[4,240,128]{2,1,0:T(8,128)(2,1)S(1)}, u32[]{:S(2)}, u32[]{:S(2)}) collective-permute-start(bf16[4,240,128]{2,1,0:T(8,128)(2,1)S(1)} %get-tuple-element.42), channel_id=1, source_target_pairs={{0,2},{1,3},{2,0},{3,1},{4,28},{5,29},{6,30},{7,31},{8,10},{9,11},... | collective-permute-start | bytes 737288 | tf_op jit(solution)/shard_map/ppermute | solution.py:453
  26.2 6.1 %collective-permute-start.8 = (bf16[240,128]{1,0:T(8,128)(2,1)S(1)}, bf16[240,128]{1,0:T(8,128)(2,1)S(1)}, u32[]{:S(2)}, u32[]{:S(2)}) collective-permute-start(bf16[240,128]{1,0:T(8,128)(2,1)S(1)} %get-tuple-element.45), channel_id=1, source_target_pairs={{0,24},{1,25},{2,26},{3,27},{4,7},{5,6},{6,5},{7,4},{8,16},{9,17},... | collective-permute-start | bytes 184328 | tf_op jit(solution)/shard_map/ppermute | solution.py:453
  28.5 5.8 %collective-permute-start.9 = (bf16[240,128]{1,0:T(8,128)(2,1)S(1)}, bf16[240,128]{1,0:T(8,128)(2,1)S(1)}, u32[]{:S(2)}, u32[]{:S(2)}) collective-permute-start(bf16[240,128]{1,0:T(8,128)(2,1)S(1)} %get-tuple-element.46), channel_id=1, source_target_pairs={{0,16},{1,17},{2,18},{3,19},{4,6},{5,7},{6,4},{7,5},{8,24},{9,25},... | collective-permute-start | bytes 184328 | tf_op jit(solution)/shard_map/ppermute | solution.py:453
  29.3 5.0 %collective-permute-start.10 = (bf16[240,128]{1,0:T(8,128)(2,1)S(1)}, bf16[240,128]{1,0:T(8,128)(2,1)S(1)}, u32[]{:S(2)}, u32[]{:S(2)}) collective-permute-start(bf16[240,128]{1,0:T(8,128)(2,1)S(1)} %get-tuple-element.47), channel_id=1, source_target_pairs={{0,8},{1,9},{2,10},{3,11},{4,5},{5,4},{6,7},{7,6},{8,0},{9,1},{10,... | collective-permute-start | bytes 184328 | tf_op jit(solution)/shard_map/ppermute | solution.py:453

commit v3 on v2

--- a/solution.py
+++ b/solution.py
@@ -16,6 +16,7 @@
 LANES = 128
 SUB = 8
 PAD = 8
+HOP = 9
 FIRST = ((0, 0), (3, 2), (1, 1), (2, 3))
 VMEM_BYTES = 14 * 1024 * 1024
 
@@ -41,22 +42,22 @@
     return pltpu.with_memory_space_constraint(array, pltpu.VMEM)
 
 
-def edges_kernel(x_ref, u_ref, pair_ref, far_ref, x_low, x_high, u_low, u_high, sems):
+def edges_kernel(x_ref, u_ref, far_ref, x_rows, u_rows, sems):
     batch, rows, chans = x_ref.shape
-    copies = []
-    for i, (src, low, high) in enumerate(((x_ref, x_low, x_high), (u_ref, u_low, u_high))):
-        copies.append(pltpu.make_async_copy(src.at[:, pl.ds(0, 16), :], low, sems.at[2 * i]))
-        copies.append(pltpu.make_async_copy(src.at[:, pl.ds(rows - 16, 16), :], high, sems.at[2 * i + 1]))
+    even = position()[0] == 0
+    start = pl.multiple_of(jnp.where(even, 0, rows - 16), 16)
+    copies = [
+        pltpu.make_async_copy(src.at[:, pl.ds(start, 16), :], dst, sems.at[i])
+        for i, (src, dst) in enumerate(((x_ref, x_rows), (u_ref, u_rows)))
+    ]
     for copy in copies:
         copy.start()
     for copy in copies:
         copy.wait()
-    even = position()[0] == 0
-    for low, high, lo, hi in ((x_low, x_high, 0, chans), (u_low, u_high, chans, pair_ref.shape[1])):
-        first = jnp.concatenate([low[b].astype(F32)[:2] for b in range(batch)], axis=0)
-        final = jnp.concatenate([high[b].astype(F32)[14:] for b in range(batch)], axis=0)
-        pair_ref[:, lo:hi] = jnp.where(even, final, first).astype(BF16)
-        far_ref[:, lo:hi] = jnp.where(even, first, final).astype(BF16)
+    for held, lo, hi in ((x_rows, 0, chans), (u_rows, chans, far_ref.shape[1])):
+        wide = [held[b].astype(F32) for b in range(batch)]
+        wide = jnp.concatenate([jnp.where(even, one[:2], one[14:]) for one in wide], axis=0)
+        far_ref[:, lo:hi] = wide.astype(BF16)
 
 
 def edges(x, u):
@@ -64,51 +65,52 @@
     feats = u.shape[2]
     return pl.pallas_call(
         edges_kernel,
-        out_shape=[shape((2 * batch, chans + feats), BF16)] * 2,
+        out_shape=shape((2 * batch, chans + feats), BF16),
         in_specs=[pl.BlockSpec(memory_space=pltpu.HBM)] * 2,
-        out_specs=vmem(2),
-        scratch_shapes=[pltpu.VMEM((batch, 16, chans), BF16)] * 2 + [pltpu.VMEM((batch, 16, feats), BF16)] * 2
-        + [pltpu.SemaphoreType.DMA((4,))],
+        out_specs=vmem(1)[0],
+        scratch_shapes=[pltpu.VMEM((batch, 16, chans), BF16), pltpu.VMEM((batch, 16, feats), BF16),
+                        pltpu.SemaphoreType.DMA((2,))],
         compiler_params=params(),
         cost_estimate=pl.CostEstimate(flops=0, bytes_accessed=1_000, transcendentals=0),
         name="edges",
     )(x, u)
 
 
-def relay_kernel(pair_ref, far_ref, pair_out, far_out):
-    pair_out[...] = pair_ref[...]
+def relay_kernel(far_ref, far_out):
     far_out[...] = far_ref[...]
 
 
-def relay(pair, far):
+def relay(far):
     return pl.pallas_call(
         relay_kernel,
-        out_shape=[shape(pair.shape, BF16)] * 2,
-        in_specs=vmem(2),
-        out_specs=vmem(2),
+        out_shape=shape(far.shape, BF16),
+        in_specs=vmem(1),
+        out_specs=vmem(1)[0],
         compiler_params=params(),
         cost_estimate=pl.CostEstimate(flops=10_000_000_000, bytes_accessed=1_000_000, transcendentals=0),
         name="relay",
-    )(here(pair), here(far))
-
-
-def odd_slope(w):
+    )(here(far))
+
+
+def slope(w):
     w2 = w * w
     t = jnp.tanh(w * (w2 + KAPPA))
-    return t + w * (w2 + KAPPA / 3.0) * (3.0 - 3.0 * (t * t))
+    return (1.0 + t) * (w * (w2 + KAPPA / 3.0) * (1.0 - t) + 1.0 / 3.0)
 
 
 def tap_sets(taps):
     k_sum, k_dif, k_mid = 0.5 * (taps[0:1] + taps[2:3]), 0.5 * (taps[0:1] - taps[2:3]), taps[1:2]
-    return (ALPHA * k_sum, ALPHA * k_dif, ALPHA * k_mid), (0.25 * k_sum, 0.25 * k_dif, 0.25 * k_mid)
-
-
-def slopes(scaled, before, centre, after, u):
-    p_sum, p_dif, p_mid = scaled
-    same = p_mid * centre + p_sum * (before + after)
-    skew = p_dif * (before - after)
-    fwd, rev = odd_slope(same + skew), odd_slope(same - skew)
-    return u * (2.0 + (fwd + rev)), u * (fwd - rev)
+    return (ALPHA * taps[0:1], ALPHA * taps[1:2], ALPHA * taps[2:3]), (0.75 * k_sum, 0.75 * k_dif, 0.75 * k_mid)
+
+
+def products(scaled, value):
+    return [tap * value for tap in scaled]
+
+
+def slopes(before, centre, after, u):
+    fwd = slope(centre[1] + before[0] + after[2])
+    rev = slope(centre[1] + before[2] + after[0])
+    return u * (fwd + rev), u * (fwd - rev)
 
 
 def inner_gradients(j, proj, u_ref, k_ref, wide, out, gp_ref, gp_lane):
@@ -122,19 +124,19 @@
             wide[b, s * pitch:s * pitch + seg] = u_ref[b, s * seg:(s + 1) * seg, lanes].astype(F32)
     for b in range(batch):
         def vector(i, b=b):
-            return proj[j, b, pl.ds(i, SUB, stride=pitch), :]
+            return products(scaled, proj[j, b, pl.ds(i, SUB, stride=pitch), :])
 
         def put(i, before, centre, after, dif_before, dif_after, b=b):
-            out[b, pl.ds(i, SUB, stride=pitch), :] = (
+            out[b, i * HOP:i * HOP + SUB, :] = (
                 g_mid * centre + g_sum * (before + after) + g_dif * (dif_after - dif_before))
 
         head, tail = vector(0), vector(seg - 1)
-        before, stop = pltpu.roll(tail, 1, 0), pltpu.roll(head, SUB - 1, 0)
+        before, stop = [pltpu.roll(one, 1, 0) for one in tail], [pltpu.roll(one, SUB - 1, 0) for one in head]
         sums, difs = [], []
         centre = head
         for i in range(seg):
             after = stop if i == seg - 1 else (tail if i == seg - 2 else vector(i + 1))
-            one, two = slopes(scaled, before, centre, after, wide[b, pl.ds(i, SUB, stride=pitch), :])
+            one, two = slopes(before, centre, after, wide[b, pl.ds(i, SUB, stride=pitch), :])
             sums.append(one)
             difs.append(two)
             before, centre = centre, after
@@ -142,7 +144,8 @@
                 put(i - 1, sums[i - 2], sums[i - 1], sums[i], difs[i - 2], difs[i])
         put(0, pltpu.roll(sums[-1], 1, 0), sums[0], sums[1], pltpu.roll(difs[-1], 1, 0), difs[1])
         put(seg - 1, sums[-2], sums[-1], pltpu.roll(sums[0], SUB - 1, 0), difs[-2], pltpu.roll(difs[0], SUB - 1, 0))
-        done = jnp.concatenate([out[b, s * pitch:s * pitch + seg] for s in range(SUB)], axis=0)
+        done = jnp.concatenate(
+            [out[b, pl.ds(lo * HOP + s, SUB, stride=HOP), :] for s in range(SUB) for lo in range(0, seg, SUB)], axis=0)
         gp_ref[b, :, gp_lane:gp_lane + LANES] = done.astype(BF16)
 
 
@@ -161,7 +164,7 @@
 
 
 def sample_scratch(batch, rows):
-    return [pltpu.VMEM((batch, rows + SUB * PAD, LANES), F32)] * 2
+    return [pltpu.VMEM((batch, rows + SUB * PAD, LANES), F32), pltpu.VMEM((batch, rows // SUB * HOP, LANES), F32)]
 
 
 def project(x, w, u, k, ncol):
@@ -183,11 +186,16 @@
     return jnp.concatenate([low, jnp.zeros((SUB - 4, low.shape[1]), low.dtype), high], axis=0)
 
 
-def halo_of(pair_ref, far_ref, lo, hi, batch):
+def halo_of(pair_ref, far_rows):
+    batch, rows, _ = pair_ref.shape
     even = position()[0] == 0
-    pair, far = pair_ref[:, lo:hi].astype(F32), far_ref[:, lo:hi].astype(F32)
-    low, high = jnp.where(even, far, pair), jnp.where(even, pair, far)
-    return [around(low[2 * b:2 * b + 2], high[2 * b:2 * b + 2]) for b in range(batch)]
+    far_rows = far_rows.astype(F32)
+    result = []
+    for b in range(batch):
+        far = far_rows[2 * b:2 * b + 2]
+        low, high = pair_ref[b, rows - 16:rows].astype(F32)[14:], pair_ref[b, 0:16].astype(F32)[:2]
+        result.append(around(jnp.where(even, far, low), jnp.where(even, high, far)))
+    return result
 
 
 def finish(j, proj, u_ref, k_ref, halo_p, halo_u, inner_ref, gp_ref, gp_lane, gpt):
@@ -213,7 +221,7 @@
         u_low = u_ref[b, 0:16, lanes].astype(F32)[:SUB]
         u_high = u_ref[b, rows - 16:rows, lanes].astype(F32)[16 - SUB:]
         u = centred(u_low, u_high, halo_u[b][:, lanes])
-        sums, difs = slopes(scaled, before, centred(low, high, halo), after, u)
+        sums, difs = slopes(*(products(scaled, one) for one in (before, centred(low, high, halo), after)), u)
         ends = (g_mid * sums + g_sum * (pltpu.roll(sums, 1, 0) + pltpu.roll(sums, SUB - 1, 0))
                 + g_dif * (pltpu.roll(difs, SUB - 1, 0) - pltpu.roll(difs, 1, 0)))
         first = inner_ref[b, 0:16, cols].astype(F32)
@@ -236,13 +244,15 @@
 
 
 def early_kernel(
-    x_ref, w_ref, u_ref, k_ref, pair_ref, far_ref, proj, inner_ref,
-    gp_ref, halo_ref, *rest,
+    x_ref, w_ref, u_ref, k_ref, pair_x, pair_u, far_ref, proj, inner_ref,
+    gp_ref, halo_ref, halo_u_ref, *rest,
 ):
     *parts, gpt = rest
     batch, rows, chans = x_ref.shape
-    halo_x = halo_of(pair_ref, far_ref, 0, chans, batch)
-    halo_u = halo_of(pair_ref, far_ref, chans, pair_ref.shape[1], batch)
+    halo_x = halo_of(pair_x, far_ref[:, :chans])
+    halo_u = halo_of(pair_u, far_ref[:, chans:])
+    for b in range(batch):
+        halo_u_ref[b] = halo_u[b]
     halo_x = jnp.concatenate(halo_x, axis=0).astype(BF16)
     halo_all = jnp.dot(halo_x, w_ref[...], preferred_element_type=F32).astype(BF16).astype(F32)
     for b in range(batch):
@@ -255,12 +265,11 @@
 
 
 def late_kernel(
-    col, u_ref, k_ref, pair_ref, far_ref, proj, halo_ref,
+    col, u_ref, k_ref, proj, halo_ref, halo_u_ref,
     gp_ref, mine_ref, send_ref, wide, out, gpt,
 ):
     batch, rows, feats = u_ref.shape
-    chans = pair_ref.shape[1] - feats
-    halo_u = halo_of(pair_ref, far_ref, chans, pair_ref.shape[1], batch)
+    halo_u = [halo_u_ref[b] for b in range(batch)]
     halo_p = [halo_ref[b] for b in range(batch)]
     for t in range(gp_ref.shape[2] // LANES):
         j = col // LANES + t
@@ -269,96 +278,109 @@
     hand_out(position()[0], gpt, mine_ref, send_ref)
 
 
-def early(x, w, u, k, pair, far, proj, inner, strips, strip):
+def early(x, w, u, k, pair_x, pair_u, far, proj, inner, strips, strip):
     batch, rows, _ = x.shape
     ncol = inner.shape[2]
     parts = [shape((strips, strip, batch * rows), BF16)] * 2 if strips else []
     return pl.pallas_call(
         early_kernel,
-        out_shape=[shape(inner.shape, BF16), shape((batch, SUB, w.shape[1]), F32)] + parts,
-        in_specs=vmem(8),
-        out_specs=vmem(2 + len(parts)),
+        out_shape=[shape(inner.shape, BF16)] + [shape((batch, SUB, w.shape[1]), F32)] * 2 + parts,
+        in_specs=vmem(9),
+        out_specs=vmem(3 + len(parts)),
         scratch_shapes=[pltpu.VMEM((ncol, batch * rows), BF16)],
         compiler_params=params(),
         cost_estimate=pl.CostEstimate(flops=1_000_000_000, bytes_accessed=4_000_000, transcendentals=0),
         name="early",
-    )(*map(here, (x, w, u, k, pair, far, proj, inner)))
-
-
-def late(u, k, pair, far, proj, halo, col, ncol, strips, strip):
+    )(*map(here, (x, w, u, k, pair_x, pair_u, far, proj, inner)))
+
+
+def late(u, k, proj, halo, halo_u, col, ncol, strips, strip):
     batch, rows, _ = u.shape
     part = shape((strips, strip, batch * rows), BF16)
     return pl.pallas_call(
         functools.partial(late_kernel, col),
         out_shape=[shape((batch, rows, ncol), BF16), part, part],
-        in_specs=vmem(6),
+        in_specs=vmem(5),
         out_specs=vmem(3),
         scratch_shapes=sample_scratch(batch, rows) + [pltpu.VMEM((ncol, batch * rows), BF16)],
         compiler_params=params(),
         cost_estimate=pl.CostEstimate(flops=4_000_000_000, bytes_accessed=4_000_000, transcendentals=0),
         name="late",
-    )(*map(here, (u, k, pair, far, proj, halo)))
-
-
-def own_kernel(x_ref, other_ref, mine_a, mine_b, got_a, out_ref):
-    batch, rows, chans = x_ref.shape
-    flat = x_ref[...].reshape(batch * rows, chans)
-    other = other_ref[...].reshape(batch * rows, chans)
-    half = mine_a.shape[0]
+    )(*map(here, (u, k, proj, halo, halo_u)))
+
+
+def stacked(ref):
+    return ref[...].reshape(ref.shape[0] * ref.shape[1], ref.shape[2])
+
+
+def place_blocks(strips, sums_ref, out_ref):
+    core, zed, dee = position()
+    strip = sums_ref.shape[1]
+    half = strip // 2
+    left = lax.broadcasted_iota(jnp.int32, (half, LANES), 1) < LANES // 2
+
+    def slot(turn, turns):
+        return sum(jnp.where(turn == one, at, 0) for at, one in enumerate(turns))
+
+    for z in strips:
+        z_slot = slot(jnp.bitwise_xor(zed, z), [pair[1] for pair in FIRST])
+        for b in range(4):
+            b_slot = slot(jnp.bitwise_xor(dee, b), [pair[0] for pair in FIRST])
+            at, spot = jnp.where(core == 0, b_slot, z_slot), jnp.where(core == 0, z, b)
+            full = (3 * (b // 2) + 2 * (b % 2)) * LANES
+            rest = (3 * (b // 2) + 1) * LANES
+            top, bottom = sums_ref[z, 0:half, rest:rest + LANES], sums_ref[z, half:strip, rest:rest + LANES]
+            if b % 2 == 0:
+                packed = jnp.where(left, top, pltpu.roll(bottom, LANES // 2, 1))
+            else:
+                packed = jnp.where(left, pltpu.roll(top, LANES // 2, 1), bottom)
+            out_ref[at, spot, 0:strip] = sums_ref[z, :, full:full + LANES].astype(BF16)
+            out_ref[at, spot, strip:strip + half] = packed.astype(BF16)
+
+
+def own_kernel(x_ref, other_ref, mine_a, mine_b, got_a, sums_ref, out_ref):
+    flat, other = stacked(x_ref), stacked(other_ref)
+    half, strip, _ = mine_a.shape
+    later = jnp.dot(stacked(mine_b), flat, preferred_element_type=F32)
+    sooner = (jnp.dot(stacked(mine_a), flat, preferred_element_type=F32)
+              + jnp.dot(stacked(got_a), other, preferred_element_type=F32))
     for z in range(half):
-        out_ref[half + z] = jnp.dot(mine_b[z], flat, preferred_element_type=F32)
-    for z in range(half):
-        out_ref[z] = (jnp.dot(mine_a[z], flat, preferred_element_type=F32)
-                      + jnp.dot(got_a[z], other, preferred_element_type=F32))
+        sums_ref[half + z] = later[z * strip:(z + 1) * strip]
+        sums_ref[z] = sooner[z * strip:(z + 1) * strip]
+    place_blocks(range(half), sums_ref, out_ref)
 
 
 def own(x, other, mine_a, mine_b, got_a):
     half, strip, _ = mine_a.shape
     return pl.pallas_call(
         own_kernel,
-        out_shape=shape((2 * half, strip, x.shape[2]), F32),
+        out_shape=[shape((2 * half, strip, x.shape[2]), F32), shape((4, 4, strip + strip // 2, LANES), BF16)],
         in_specs=vmem(5),
-        out_specs=vmem(1)[0],
+        out_specs=vmem(2),
         compiler_params=params(),
         cost_estimate=pl.CostEstimate(flops=1_000_000_000, bytes_accessed=4_000_000, transcendentals=0),
         name="own",
     )(*map(here, (x, other, mine_a, mine_b, got_a)))
 
 
-def pack_kernel(other_ref, got_b, sums_in, sums_ref, *outs):
-    core, zed, dee = position()
-    batch, rows, chans = other_ref.shape
-    other = other_ref[...].reshape(batch * rows, chans)
+def pack_kernel(other_ref, got_b, sums_in, blocks_in, sums_ref, out_ref):
     half, strip, _ = got_b.shape
+    later = jnp.dot(stacked(got_b), stacked(other_ref), preferred_element_type=F32)
     for z in range(half):
-        sums_ref[half + z] = sums_in[half + z] + jnp.dot(got_b[z], other, preferred_element_type=F32)
-    left = lax.broadcasted_iota(jnp.int32, (strip // 2, LANES), 1) < LANES // 2
-    for (d_turn, z_turn), out in zip(FIRST, outs):
-        for j in range(4):
-            z = jnp.where(core == 0, j, jnp.bitwise_xor(zed, z_turn))
-            b = jnp.where(core == 0, jnp.bitwise_xor(dee, d_turn), j)
-            y, odd = lax.div(b, 2), lax.rem(b, 2)
-            full = pl.multiple_of((3 * y + 2 * odd) * LANES, LANES)
-            rest = pl.multiple_of((3 * y + 1) * LANES, LANES)
-            top, bottom = sums_ref[z, 0:strip // 2, pl.ds(rest, LANES)], sums_ref[z, strip // 2:strip, pl.ds(rest, LANES)]
-            turned = pltpu.roll(jnp.where(left, bottom, top), LANES // 2, 1)
-            kept = jnp.where(odd == 0, top, bottom)
-            out[j, 0:strip] = sums_ref[z, :, pl.ds(full, LANES)].astype(out.dtype)
-            out[j, strip:strip + strip // 2] = jnp.where(left == (odd == 0), kept, turned).astype(out.dtype)
-
-
-def pack(other, got_b, sums):
-    half, strip, _ = got_b.shape
-    block = (4, strip + strip // 2, LANES)
+        sums_ref[half + z] = sums_in[half + z] + later[z * strip:(z + 1) * strip]
+    place_blocks(range(half, 2 * half), sums_ref, out_ref)
+
+
+def pack(other, got_b, sums, blocks):
     return pl.pallas_call(
         pack_kernel,
-        out_shape=[shape(sums.shape, F32), shape(block, F32)] + [shape(block, BF16)] * 3,
-        in_specs=vmem(3),
-        out_specs=vmem(5),
-        input_output_aliases={2: 0},
+        out_shape=[shape(sums.shape, F32), shape(blocks.shape, BF16)],
+        in_specs=vmem(4),
+        out_specs=vmem(2),
+        input_output_aliases={2: 0, 3: 1},
         compiler_params=params(),
         name="pack",
-    )(*map(here, (other, got_b, sums)))[1:]
+    )(*map(here, (other, got_b, sums, blocks)))[1]
 
 
 def fold_kernel(own_ref, one_ref, two_ref, three_ref, token, *outs):
@@ -366,12 +388,12 @@
     mine = jnp.where(core == 0, zed, dee)
     for k in (3, 2, 1, 0):
         j = jnp.bitwise_xor(mine, k)
-        total = own_ref[j] + one_ref[j].astype(F32) + two_ref[j].astype(F32) + three_ref[j].astype(F32)
+        total = own_ref[0, j].astype(F32) + one_ref[j].astype(F32) + two_ref[j].astype(F32) + three_ref[j].astype(F32)
         outs[k][...] = total.astype(outs[k].dtype)
 
 
 def fold(parts, token):
-    block = parts[0].shape[1:]
+    block = parts[1].shape[1:]
     return pl.pallas_call(
         fold_kernel,
         out_shape=[shape(block, F32)] + [shape(block, BF16)] * 3,
@@ -453,10 +475,10 @@
     return lax.ppermute(array, ("seq", "dp"), pairs)
 
 
-def spread(x, w, u, k, pair, far):
+def spread(x, w, u, k, pair_x, pair_u, far):
     batch = x.shape[0]
     proj, inner = project(x, w, u, k, w.shape[1])
-    gp, _ = early(x, w, u, k, pair, far, proj, inner, 0, 0)
+    gp, *_ = early(x, w, u, k, pair_x, pair_u, far, proj, inner, 0, 0)
     input_grad = jnp.einsum("bpf,cf->bpc", gp, w, preferred_element_type=F32).astype(BF16)
     partial = lax.dot_general(x, gp, (((0, 1), (0, 1)), ((), ())), preferred_element_type=F32)
     over_seq = lax.psum_scatter(partial, "seq", scatter_dimension=1, tiled=True)
@@ -475,26 +497,23 @@
     ncol = feats // 2
 
     there = functools.partial(pltpu.with_memory_space_constraint, memory_space=pltpu.HBM)
-    pair, far = edges(there(skip_input), there(upstream))
-    pair, far = relay(pair, far)
     x, w, u, k = skip_input, proj_weight, upstream, depth_kernel
-    pair = lax.ppermute(pair, "seq", near_pairs())
+    pair_x = lax.ppermute(x, "seq", near_pairs())
+    pair_u = lax.ppermute(u, "seq", near_pairs())
+    far = lax.ppermute(relay(edges(there(x), there(u))), "seq", far_pairs())
     if n_seq != 8 or n_dp != 4 or chans != 4 * (LANES + LANES // 2):
-        return spread(x, w, u, k, pair, lax.ppermute(far, "seq", far_pairs()))
-    other = lax.ppermute(skip_input, "seq", near_pairs())
-    far = lax.ppermute(far, "seq", far_pairs())
+        return spread(x, w, u, k, pair_x, pair_u, far)
     proj, inner = project(x, w, u, k, ncol)
-    gp_a, halo, mine_a, send_a = early(x, w, u, k, pair, far, proj, inner, strips, strip)
+    gp_a, halo, halo_u, mine_a, send_a = early(x, w, u, k, pair_x, pair_u, far, proj, inner, strips, strip)
     got_a = lax.ppermute(send_a, "seq", near_pairs())
-    gp_b, mine_b, send_b = late(u, k, pair, far, proj, halo, ncol, feats - ncol, strips, strip)
+    gp_b, mine_b, send_b = late(u, k, proj, halo, halo_u, ncol, feats - ncol, strips, strip)
     got_b = lax.ppermute(send_b, "seq", near_pairs())
-    sums = own(x, other, mine_a, mine_b, got_a)
-    own_blocks, *messages = pack(other, got_b, sums)
+    blocks = pack(pair_x, got_b, *own(x, pair_x, mine_a, mine_b, got_a))
 
     input_grad, token = input_gradient(gp_a, gp_b, w)
     z_bits = [m * 2 * n_dp for m in range(4)]
-    got = [exchange(message, d, z_bits[z]) for message, (d, z) in zip(messages, FIRST[1:])]
-    own_block, *messages = fold([own_blocks] + got, token)
+    got = [exchange(blocks[i], *(FIRST[i][0], z_bits[FIRST[i][1]])) for i in (3, 2, 1)]
+    own_block, *messages = fold([blocks] + got, token)
     got = [exchange(messages[k - 1], z_bits[k], k) for k in (3, 2, 1)]
     return input_grad, last([own_block] + got, 1.0 / (batch * n_dp))
 

time: 35.2 us -> 34.9 us (level)
  Pallas kernels: 12 us -> 11.6 us
  transfers between devices with their start and end apart: 11 -> 11, of which waited for: 5 -> 5; matrix products, arithmetic and copies ran while one was open for 0% -> 0% of each run, Pallas kernels for 29% -> 28%
where the time goes in v3:
time: 34.9 us; the launch traced here: 34.7 us
  starting transfers between devices  12.8 us (37%)
  Pallas kernels  11.6 us (33%)
  waiting for transfers between devices  8.14 us (23%)
  local copies, waits for them, and re-layouts  1.4 us (4%)
  between operations  0.77 us (2%)
    ppermute x6, starting transfers between devices, exchange(): return lax.ppermute(array, ('seq', 'dp'), pairs)  8.01 us
    ppermute x6, waiting for transfers between devices, exchange(): return lax.ppermute(array, ('seq', 'dp'), pairs)  7.55 us
    ppermute x1, starting transfers between devices, on_device(): got_a = lax.ppermute(send_a, 'seq', near_pairs())  3.27 us
    pallas_call x1, Pallas kernels, project(): pl.pallas_call(project_kernel, out_shape=[shape((feats // LANES, batch, r...  3 us
    pallas_call x1, Pallas kernels, input_gradient(): pl.pallas_call(input_kernel, out_shape=[jax.ShapeDtypeStruct((batch, rows...  2.33 us
    pallas_call x1, Pallas kernels, late(): pl.pallas_call(functools.partial(late_kernel, col), out_shape=[shape((bat...  2.33 us
    unnamed x8, local copies, waits for them, and re-layouts  1.35 us
    pallas_call x1, Pallas kernels, own(): pl.pallas_call(own_kernel, out_shape=[shape((2 * half, strip, x.shape[2])...  1.01 us
  transfers between devices with their start and end apart: 11, of which 5 were waited for; matrix products, arithmetic and copies ran while one was open for 0% of the time, Pallas kernels for 28%

profile of v3, /device:TPU:0, one launch (start us, length us, event | category | flops | bytes accessed | tf_op | source)
XLA Modules:
  0.0 34.7 jit_solution(10562609918364176575)
XLA Ops:
  0.6 0.5 %collective-permute-start = (bf16[2,256,768]{2,1,0:T(8,128)(2,1)}, bf16[2,256,768]{2,1,0:T(8,128)(2,1)S(1)}, u32[]{:S(2)}, u32[]{:S(2)}) collective-permute-start(bf16[2,256,768]{2,1,0:T(8,128)(2,1)} %x_ref.7), channel_id=1, source_target_pairs={{0,4},{4,0},{8,12},{12,8},{16,20},{20,16},{24,28},{28,24},{1,5},{5... | collective-permute-start | bytes 2359304 | tf_op jit(solution)/shard_map/ppermute | solution.py:501
  1.1 0.1 collective-permute-start.1
  1.2 1.0 %edges.1.far_ref = bf16[4,2048]{1,0:T(4,128)(2,1)S(1)} custom-call(bf16[2,256,768]{2,1,0:T(8,128)(2,1)} %x_ref.7, bf16[2,256,1280]{2,1,0:T(8,128)(2,1)} %u_ref.7), custom_call_target="tpu_custom_call" | custom-call | bytes 1000 | tf_op jit(solution)/shard_map/edges/pallas_call | solution.py:66
  2.2 0.0 copy-start
  2.2 0.0 copy-start.1
  2.2 0.0 copy-start.2
  2.2 0.0 copy-start.3
  2.3 0.8 %collective-permute-start.2 = (bf16[4,2048]{1,0:T(4,128)(2,1)S(1)}, bf16[4,2048]{1,0:T(4,128)(2,1)S(1)}, u32[]{:S(2)}, u32[]{:S(2)}) collective-permute-start(bf16[4,2048]{1,0:T(4,128)(2,1)S(1)} %relay.1), channel_id=1, source_target_pairs={{4,8},{8,4},{12,16},{16,12},{20,24},{24,20},{5,9},{9,5},{13,17},{1... | collective-permute-start | bytes 49160 | tf_op jit(solution)/shard_map/ppermute | solution.py:503
  3.1 0.5 %copy-done = bf16[2,256,1280]{2,1,0:T(8,128)(2,1)S(1)} copy-done((bf16[2,256,1280]{2,1,0:T(8,128)(2,1)S(1)}, bf16[2,256,1280]{2,1,0:T(8,128)(2,1)}, u32[]{:S(2)}) %copy-start) | copy-done | bytes 1310744
  3.5 0.2 copy-done.1
  3.7 0.7 %copy-done.2 = bf16[768,1280]{1,0:T(8,128)(2,1)S(1)} copy-done((bf16[768,1280]{1,0:T(8,128)(2,1)S(1)}, bf16[768,1280]{1,0:T(8,128)(2,1)}, u32[]{:S(2)}) %copy-start.2) | copy-done | bytes 1966104
  4.4 0.0 copy-done.3
  4.4 3.0 %project.1 = (f32[10,2,320,128]{3,2,1,0:T(8,128)S(1)}, bf16[2,256,640]{2,1,0:T(8,128)(2,1)S(1)}) custom-call(bf16[2,256,768]{2,1,0:T(8,128)(2,1)S(1)} %copy-done.1, bf16[768,1280]{1,0:T(8,128)(2,1)S(1)} %copy-done.2, bf16[2,256,1280]{2,1,0:T(8,128)(2,1)S(1)} %copy-done, f32[3,1280]{1,0:T(4,128)S(1)} %copy-done.3), custom_call_target="tpu_custom_call" | custom-call | flops 4000000000 | bytes 4000000 | tf_op jit(solution)/shard_map/project/pallas_call | solution.py:173
  7.4 0.0 collective-permute-done.2.far_ref
  7.4 0.0 collective-permute-done.pair_x.other_ref
  7.4 0.0 collective-permute-done.1.pair_u
  7.4 0.6 %early.1 = (bf16[2,256,640]{2,1,0:T(8,128)(2,1)S(1)}, f32[2,8,1280]{2,1,0:T(8,128)S(1)}, f32[2,8,1280]{2,1,0:T(8,128)S(1)}, bf16[2,160,512]{2,1,0:T(8,128)(2,1)S(1)}, bf16[2,160,512]{2,1,0:T(8,128)(2,1)S(1)}) custom-call(bf16[2,256,768]{2,1,0:T(8,128)(2,1)S(1)} %copy-done.1, bf16[768,1280]{1,0:T(8,128)(2,1)S(1)} %copy-done.2, ...), custom_call_target="tpu_custom_call" | custom-call | flops 1000000000 | bytes 4000000 | tf_op jit(solution)/shard_map/early/pallas_call | solution.py:285
  8.0 3.3 %collective-permute-start.4 = (bf16[2,160,512]{2,1,0:T(8,128)(2,1)S(1)}, bf16[2,160,512]{2,1,0:T(8,128)(2,1)S(1)}, u32[]{:S(2)}, u32[]{:S(2)}) collective-permute-start(bf16[2,160,512]{2,1,0:T(8,128)(2,1)S(1)} %get-tuple-element.31), channel_id=1, source_target_pairs={{0,4},{4,0},{8,12},{12,8},{16,20},{20,16},{24,28},{28,24},{1,5},{5... | collective-permute-start | bytes 983048 | tf_op jit(solution)/shard_map/ppermute | solution.py:508
  11.3 2.3 %late.1 = (bf16[2,256,640]{2,1,0:T(8,128)(2,1)S(1)}, bf16[2,160,512]{2,1,0:T(8,128)(2,1)S(1)}, bf16[2,160,512]{2,1,0:T(8,128)(2,1)S(1)}) custom-call(bf16[2,256,1280]{2,1,0:T(8,128)(2,1)S(1)} %copy-done, f32[3,1280]{1,0:T(4,128)S(1)} %copy-done.3, f32[10,2,320,128]{3,2,1,0:T(8,128)S(1)} %get-tuple-element.21.proj, ...), custom_call_target="tpu_custom_call" | custom-call | flops 4000000000 | bytes 4000000 | tf_op jit(solution)/shard_map/late/pallas_call | solution.py:300
  13.6 0.1 collective-permute-start.3
  13.7 0.0 collective-permute-done.4.got_a
  13.7 1.0 %own.1 = (f32[4,160,768]{2,1,0:T(8,128)S(1)}, bf16[4,4,240,128]{3,2,1,0:T(8,128)(2,1)S(1)}) custom-call(bf16[2,256,768]{2,1,0:T(8,128)(2,1)S(1)} %copy-done.1, bf16[2,256,768]{2,1,0:T(8,128)(2,1)S(1)} %collective-permute-done.pair_x.other_ref, bf16[2,160,512]{2,1,0:T(8,128)(2,1)S(1)} %get-tuple-element.29.mine_a, ...), custom_call_target="tpu_custom_call" | custom-call | flops 1000000000 | bytes 4000000 | tf_op jit(solution)/shard_map/own/pallas_call | solution.py:355
  14.7 0.6 %collective-permute-done.3.got_b = bf16[2,160,512]{2,1,0:T(8,128)(2,1)S(1)} collective-permute-done((bf16[2,160,512]{2,1,0:T(8,128)(2,1)S(1)}, bf16[2,160,512]{2,1,0:T(8,128)(2,1)S(1)}, u32[]{:S(2)}, u32[]{:S(2)}) %collective-permute-start.3) | collective-permute-done | bytes 327712 | tf_op jit(solution)/shard_map/ppermute | solution.py:510
  15.3 0.5 %pack.1 = (f32[4,160,768]{2,1,0:T(8,128)S(1)}, bf16[4,4,240,128]{3,2,1,0:T(8,128)(2,1)S(1)}) custom-call(bf16[2,256,768]{2,1,0:T(8,128)(2,1)S(1)} %collective-permute-done.pair_x.other_ref, bf16[2,160,512]{2,1,0:T(8,128)(2,1)S(1)} %collective-permute-done.3.got_b, ...), custom_call_target="tpu_custom_call", output_to_operand_aliasing={{0}: (2, {}), {1}: (3, {})} | custom-call | tf_op jit(solution)/shard_map/pack/pallas_call | solution.py:375
  15.9 0.1 slice_bitcast_fusion
  15.9 2.5 %collective-permute-start.7 = (bf16[4,240,128]{2,1,0:T(8,128)(2,1)S(1)}, bf16[4,240,128]{2,1,0:T(8,128)(2,1)S(1)}, u32[]{:S(2)}, u32[]{:S(2)}) collective-permute-start(bf16[4,240,128]{2,1,0:T(8,128)(2,1)S(1)} %get-tuple-element.40), channel_id=1, source_target_pairs={{0,3},{1,2},{2,1},{3,0},{4,20},{5,21},{6,22},{7,23},{8,11},{9,10},... | collective-permute-start | bytes 737288 | tf_op jit(solution)/shard_map/ppermute | solution.py:475
  18.4 0.5 %collective-permute-start.6 = (bf16[4,240,128]{2,1,0:T(8,128)(2,1)S(1)}, bf16[4,240,128]{2,1,0:T(8,128)(2,1)S(1)}, u32[]{:S(2)}, u32[]{:S(2)}) collective-permute-start(bf16[4,240,128]{2,1,0:T(8,128)(2,1)S(1)} %get-tuple-element.41), channel_id=1, source_target_pairs={{0,1},{1,0},{2,3},{3,2},{4,12},{5,13},{6,14},{7,15},{8,9},{9,8},{1... | collective-permute-start | bytes 737288 | tf_op jit(solution)/shard_map/ppermute | solution.py:475
  19.0 0.5 %collective-permute-start.5 = (bf16[4,240,128]{2,1,0:T(8,128)(2,1)S(1)}, bf16[4,240,128]{2,1,0:T(8,128)(2,1)S(1)}, u32[]{:S(2)}, u32[]{:S(2)}) collective-permute-start(bf16[4,240,128]{2,1,0:T(8,128)(2,1)S(1)} %get-tuple-element.42), channel_id=1, source_target_pairs={{0,2},{1,3},{2,0},{3,1},{4,28},{5,29},{6,30},{7,31},{8,10},{9,11},... | collective-permute-start | bytes 737288 | tf_op jit(solution)/shard_map/ppermute | solution.py:475
  19.5 2.3 %input_gradient.1 = (bf16[2,256,768]{2,1,0:T(8,128)(2,1)}, f32[8,128]{1,0:T(8,128)S(1)}) custom-call(bf16[2,256,640]{2,1,0:T(8,128)(2,1)S(1)} %get-tuple-element.23.gp_a, bf16[2,256,640]{2,1,0:T(8,128)(2,1)S(1)} %get-tuple-element.26.gp_b, bf16[768,1280]{1,0:T(8,128)(2,1)S(1)} %copy-done.2), custom_call_target="tpu_custom_call" | custom-call | flops 2000000000 | bytes 1000000 | tf_op jit(solution)/shard_map/input_gradient/pallas_call | solution.py:418
  21.8 1.3 %collective-permute-done.7.three_ref = bf16[4,240,128]{2,1,0:T(8,128)(2,1)S(1)} collective-permute-done((bf16[4,240,128]{2,1,0:T(8,128)(2,1)S(1)}, bf16[4,240,128]{2,1,0:T(8,128)(2,1)S(1)}, u32[]{:S(2)}, u32[]{:S(2)}) %collective-permute-start.7) | collective-permute-done | bytes 245792 | tf_op jit(solution)/shard_map/ppermute | solution.py:475
  23.1 2.6 %collective-permute-done.6.two_ref = bf16[4,240,128]{2,1,0:T(8,128)(2,1)S(1)} collective-permute-done((bf16[4,240,128]{2,1,0:T(8,128)(2,1)S(1)}, bf16[4,240,128]{2,1,0:T(8,128)(2,1)S(1)}, u32[]{:S(2)}, u32[]{:S(2)}) %collective-permute-start.6) | collective-permute-done | bytes 245792 | tf_op jit(solution)/shard_map/ppermute | solution.py:475
  25.8 0.0 collective-permute-done.5.one_ref
  25.8 0.1 fold.1
  25.9 2.2 %collective-permute-start.8 = (bf16[240,128]{1,0:T(8,128)(2,1)S(1)}, bf16[240,128]{1,0:T(8,128)(2,1)S(1)}, u32[]{:S(2)}, u32[]{:S(2)}) collective-permute-start(bf16[240,128]{1,0:T(8,128)(2,1)S(1)} %get-tuple-element.37), channel_id=1, source_target_pairs={{0,24},{1,25},{2,26},{3,27},{4,7},{5,6},{6,5},{7,4},{8,16},{9,17},... | collective-permute-start | bytes 184328 | tf_op jit(solution)/shard_map/ppermute | solution.py:475
  28.2 0.9 %collective-permute-start.9 = (bf16[240,128]{1,0:T(8,128)(2,1)S(1)}, bf16[240,128]{1,0:T(8,128)(2,1)S(1)}, u32[]{:S(2)}, u32[]{:S(2)}) collective-permute-start(bf16[240,128]{1,0:T(8,128)(2,1)S(1)} %get-tuple-element.38), channel_id=1, source_target_pairs={{0,16},{1,17},{2,18},{3,19},{4,6},{5,7},{6,4},{7,5},{8,24},{9,25},... | collective-permute-start | bytes 184328 | tf_op jit(solution)/shard_map/ppermute | solution.py:475
  29.0 1.3 %collective-permute-start.10 = (bf16[240,128]{1,0:T(8,128)(2,1)S(1)}, bf16[240,128]{1,0:T(8,128)(2,1)S(1)}, u32[]{:S(2)}, u32[]{:S(2)}) collective-permute-start(bf16[240,128]{1,0:T(8,128)(2,1)S(1)} %get-tuple-element.39), channel_id=1, source_target_pairs={{0,8},{1,9},{2,10},{3,11},{4,5},{5,4},{6,7},{7,6},{8,0},{9,1},{10,... | collective-permute-start | bytes 184328 | tf_op jit(solution)/shard_map/ppermute | solution.py:475
  30.4 1.6 %collective-permute-done.8.one_ref = bf16[240,128]{1,0:T(8,128)(2,1)S(1)} collective-permute-done((bf16[240,128]{1,0:T(8,128)(2,1)S(1)}, bf16[240,128]{1,0:T(8,128)(2,1)S(1)}, u32[]{:S(2)}, u32[]{:S(2)}) %collective-permute-start.8) | collective-permute-done | bytes 61472 | tf_op jit(solution)/shard_map/ppermute | solution.py:475
  32.0 1.9 %collective-permute-done.9.two_ref = bf16[240,128]{1,0:T(8,128)(2,1)S(1)} collective-permute-done((bf16[240,128]{1,0:T(8,128)(2,1)S(1)}, bf16[240,128]{1,0:T(8,128)(2,1)S(1)}, u32[]{:S(2)}, u32[]{:S(2)}) %collective-permute-start.9) | collective-permute-done | bytes 61472 | tf_op jit(solution)/shard_map/ppermute | solution.py:475
  33.9 0.0 collective-permute-done.10.three_ref
  33.9 0.8 %last.1 = f32[160,192]{1,0:T(8,128)} custom-call(f32[240,128]{1,0:T(8,128)S(1)} %get-tuple-element.36.own_ref, bf16[240,128]{1,0:T(8,128)(2,1)S(1)} %collective-permute-done.8.one_ref, bf16[240,128]{1,0:T(8,128)(2,1)S(1)} %collective-permute-done.9.two_ref, bf16[240,128]{1,0:T(8,128)(2,1)S(1)} %collective-permute-done.10.three_ref), custom_call_target="tpu_custom_call" | custom-call | tf_op jit(solution)/shard_map/last/pallas_call | solution.py:451
  (1 shorter events, 0.0 us)
Async XLA Ops:
  0.6 6.8 %collective-permute-start = (bf16[2,256,768]{2,1,0:T(8,128)(2,1)}, bf16[2,256,768]{2,1,0:T(8,128)(2,1)S(1)}, u32[]{:S(2)}, u32[]{:S(2)}) collective-permute-start(bf16[2,256,768]{2,1,0:T(8,128)(2,1)} %x_ref.7), channel_id=1, source_target_pairs={{0,4},{4,0},{8,12},{12,8},{16,20},{20,16},{24,28},{28,24},{1,5},{5... | collective-permute-start | bytes 2359304 | tf_op jit(solution)/shard_map/ppermute | solution.py:501
  1.1 6.3 %collective-permute-start.1 = (bf16[2,256,1280]{2,1,0:T(8,128)(2,1)}, bf16[2,256,1280]{2,1,0:T(8,128)(2,1)S(1)}, u32[]{:S(2)}, u32[]{:S(2)}) collective-permute-start(bf16[2,256,1280]{2,1,0:T(8,128)(2,1)} %u_ref.7), channel_id=1, source_target_pairs={{0,4},{4,0},{8,12},{12,8},{16,20},{20,16},{24,28},{28,24},{1,5},{5... | collective-permute-start | bytes 3932168 | tf_op jit(solution)/shard_map/ppermute | solution.py:502
  2.2 1.3 %copy-start = (bf16[2,256,1280]{2,1,0:T(8,128)(2,1)S(1)}, bf16[2,256,1280]{2,1,0:T(8,128)(2,1)}, u32[]{:S(2)}) copy-start(bf16[2,256,1280]{2,1,0:T(8,128)(2,1)} %u_ref.7) | copy-start | bytes 3932164
  2.2 1.5 %copy-start.1 = (bf16[2,256,768]{2,1,0:T(8,128)(2,1)S(1)}, bf16[2,256,768]{2,1,0:T(8,128)(2,1)}, u32[]{:S(2)}) copy-start(bf16[2,256,768]{2,1,0:T(8,128)(2,1)} %x_ref.7) | copy-start | bytes 2359300
  2.2 2.2 %copy-start.2 = (bf16[768,1280]{1,0:T(8,128)(2,1)S(1)}, bf16[768,1280]{1,0:T(8,128)(2,1)}, u32[]{:S(2)}) copy-start(bf16[768,1280]{1,0:T(8,128)(2,1)} %w_ref.5) | copy-start | bytes 5898244
  2.2 2.2 %copy-start.3 = (f32[3,1280]{1,0:T(4,128)S(1)}, f32[3,1280]{1,0:T(4,128)}, u32[]{:S(2)}) copy-start(f32[3,1280]{1,0:T(4,128)} %k_ref.5) | copy-start | bytes 46084
  2.3 5.1 %collective-permute-start.2 = (bf16[4,2048]{1,0:T(4,128)(2,1)S(1)}, bf16[4,2048]{1,0:T(4,128)(2,1)S(1)}, u32[]{:S(2)}, u32[]{:S(2)}) collective-permute-start(bf16[4,2048]{1,0:T(4,128)(2,1)S(1)} %relay.1), channel_id=1, source_target_pairs={{4,8},{8,4},{12,16},{16,12},{20,24},{24,20},{5,9},{9,5},{13,17},{1... | collective-permute-start | bytes 49160 | tf_op jit(solution)/shard_map/ppermute | solution.py:503
  8.0 5.7 %collective-permute-start.4 = (bf16[2,160,512]{2,1,0:T(8,128)(2,1)S(1)}, bf16[2,160,512]{2,1,0:T(8,128)(2,1)S(1)}, u32[]{:S(2)}, u32[]{:S(2)}) collective-permute-start(bf16[2,160,512]{2,1,0:T(8,128)(2,1)S(1)} %get-tuple-element.31), channel_id=1, source_target_pairs={{0,4},{4,0},{8,12},{12,8},{16,20},{20,16},{24,28},{28,24},{1,5},{5... | collective-permute-start | bytes 983048 | tf_op jit(solution)/shard_map/ppermute | solution.py:508
  13.6 1.7 %collective-permute-start.3 = (bf16[2,160,512]{2,1,0:T(8,128)(2,1)S(1)}, bf16[2,160,512]{2,1,0:T(8,128)(2,1)S(1)}, u32[]{:S(2)}, u32[]{:S(2)}) collective-permute-start(bf16[2,160,512]{2,1,0:T(8,128)(2,1)S(1)} %get-tuple-element.28), channel_id=1, source_target_pairs={{0,4},{4,0},{8,12},{12,8},{16,20},{20,16},{24,28},{28,24},{1,5},{5... | collective-permute-start | bytes 983048 | tf_op jit(solution)/shard_map/ppermute | solution.py:510
  15.9 7.2 %collective-permute-start.7 = (bf16[4,240,128]{2,1,0:T(8,128)(2,1)S(1)}, bf16[4,240,128]{2,1,0:T(8,128)(2,1)S(1)}, u32[]{:S(2)}, u32[]{:S(2)}) collective-permute-start(bf16[4,240,128]{2,1,0:T(8,128)(2,1)S(1)} %get-tuple-element.40), channel_id=1, source_target_pairs={{0,3},{1,2},{2,1},{3,0},{4,20},{5,21},{6,22},{7,23},{8,11},{9,10},... | collective-permute-start | bytes 737288 | tf_op jit(solution)/shard_map/ppermute | solution.py:475
  18.4 7.3 %collective-permute-start.6 = (bf16[4,240,128]{2,1,0:T(8,128)(2,1)S(1)}, bf16[4,240,128]{2,1,0:T(8,128)(2,1)S(1)}, u32[]{:S(2)}, u32[]{:S(2)}) collective-permute-start(bf16[4,240,128]{2,1,0:T(8,128)(2,1)S(1)} %get-tuple-element.41), channel_id=1, source_target_pairs={{0,1},{1,0},{2,3},{3,2},{4,12},{5,13},{6,14},{7,15},{8,9},{9,8},{1... | collective-permute-start | bytes 737288 | tf_op jit(solution)/shard_map/ppermute | solution.py:475
  19.0 6.8 %collective-permute-start.5 = (bf16[4,240,128]{2,1,0:T(8,128)(2,1)S(1)}, bf16[4,240,128]{2,1,0:T(8,128)(2,1)S(1)}, u32[]{:S(2)}, u32[]{:S(2)}) collective-permute-start(bf16[4,240,128]{2,1,0:T(8,128)(2,1)S(1)} %get-tuple-element.42), channel_id=1, source_target_pairs={{0,2},{1,3},{2,0},{3,1},{4,28},{5,29},{6,30},{7,31},{8,10},{9,11},... | collective-permute-start | bytes 737288 | tf_op jit(solution)/shard_map/ppermute | solution.py:475
  25.9 6.1 %collective-permute-start.8 = (bf16[240,128]{1,0:T(8,128)(2,1)S(1)}, bf16[240,128]{1,0:T(8,128)(2,1)S(1)}, u32[]{:S(2)}, u32[]{:S(2)}) collective-permute-start(bf16[240,128]{1,0:T(8,128)(2,1)S(1)} %get-tuple-element.37), channel_id=1, source_target_pairs={{0,24},{1,25},{2,26},{3,27},{4,7},{5,6},{6,5},{7,4},{8,16},{9,17},... | collective-permute-start | bytes 184328 | tf_op jit(solution)/shard_map/ppermute | solution.py:475
  28.2 5.8 %collective-permute-start.9 = (bf16[240,128]{1,0:T(8,128)(2,1)S(1)}, bf16[240,128]{1,0:T(8,128)(2,1)S(1)}, u32[]{:S(2)}, u32[]{:S(2)}) collective-permute-start(bf16[240,128]{1,0:T(8,128)(2,1)S(1)} %get-tuple-element.38), channel_id=1, source_target_pairs={{0,16},{1,17},{2,18},{3,19},{4,6},{5,7},{6,4},{7,5},{8,24},{9,25},... | collective-permute-start | bytes 184328 | tf_op jit(solution)/shard_map/ppermute | solution.py:475
  29.0 4.9 %collective-permute-start.10 = (bf16[240,128]{1,0:T(8,128)(2,1)S(1)}, bf16[240,128]{1,0:T(8,128)(2,1)S(1)}, u32[]{:S(2)}, u32[]{:S(2)}) collective-permute-start(bf16[240,128]{1,0:T(8,128)(2,1)S(1)} %get-tuple-element.39), channel_id=1, source_target_pairs={{0,8},{1,9},{2,10},{3,11},{4,5},{5,4},{6,7},{7,6},{8,0},{9,1},{10,... | collective-permute-start | bytes 184328 | tf_op jit(solution)/shard_map/ppermute | solution.py:475

commit v4 on v3

--- a/solution.py
+++ b/solution.py
@@ -116,7 +116,7 @@
 def inner_gradients(j, proj, u_ref, k_ref, wide, out, gp_ref, gp_lane):
     batch, rows = u_ref.shape[:2]
     seg = rows // SUB
-    pitch = proj.shape[2] // SUB
+    pitch = seg + PAD
     lanes = slice(j * LANES, (j + 1) * LANES)
     scaled, (g_sum, g_dif, g_mid) = tap_sets(k_ref[:, lanes])
     for b in range(batch):
@@ -152,7 +152,7 @@
 def project_kernel(x_ref, w_ref, u_ref, k_ref, proj, gp_ref, wide, out):
     batch, rows, _ = x_ref.shape
     seg = rows // SUB
-    pitch = proj.shape[2] // SUB
+    pitch = seg + PAD
     tiles = gp_ref.shape[2] // LANES
     for b in range(batch):
         body = jnp.dot(x_ref[b], w_ref[...], preferred_element_type=F32).astype(BF16).astype(F32)
@@ -163,8 +163,13 @@
         inner_gradients(j, proj, u_ref, k_ref, wide, out, gp_ref, j * LANES)
 
 
+def pitched(rows):
+    seg = rows // SUB
+    return SUB * (seg + PAD) + seg
+
+
 def sample_scratch(batch, rows):
-    return [pltpu.VMEM((batch, rows + SUB * PAD, LANES), F32), pltpu.VMEM((batch, rows // SUB * HOP, LANES), F32)]
+    return [pltpu.VMEM((batch, pitched(rows), LANES), F32), pltpu.VMEM((batch, rows // SUB * HOP + 2 * SUB, LANES), F32)]
 
 
 def project(x, w, u, k, ncol):
@@ -172,7 +177,7 @@
     feats = w.shape[1]
     return pl.pallas_call(
         project_kernel,
-        out_shape=[shape((feats // LANES, batch, rows + SUB * PAD, LANES), F32), shape((batch, rows, ncol), BF16)],
+        out_shape=[shape((feats // LANES, batch, pitched(rows), LANES), F32), shape((batch, rows, ncol), BF16)],
         in_specs=vmem(4),
         out_specs=vmem(2),
         scratch_shapes=sample_scratch(batch, rows),
@@ -200,8 +205,8 @@
 
 def finish(j, proj, u_ref, k_ref, halo_p, halo_u, inner_ref, gp_ref, gp_lane, gpt):
     batch, rows = u_ref.shape[:2]
-    pitch = proj.shape[2] // SUB
     seg = rows // SUB
+    pitch = seg + PAD
     lanes = slice(j * LANES, (j + 1) * LANES)
     cols = slice(gp_lane, gp_lane + LANES)
     scaled, (g_sum, g_dif, g_mid) = tap_sets(k_ref[:, lanes])

time: 34.9 us -> 34.9 us (level)
  no operation moved by 1% of the time
where the time goes in v4:
time: 34.9 us; the launch traced here: 34.7 us
  starting transfers between devices  12.8 us (37%)
  Pallas kernels  11.6 us (33%)
  waiting for transfers between devices  8.15 us (23%)
  local copies, waits for them, and re-layouts  1.4 us (4%)
  between operations  0.76 us (2%)
    ppermute x6, starting transfers between devices, exchange(): return lax.ppermute(array, ('seq', 'dp'), pairs)  8.01 us
    ppermute x6, waiting for transfers between devices, exchange(): return lax.ppermute(array, ('seq', 'dp'), pairs)  7.56 us
    ppermute x1, starting transfers between devices, on_device(): got_a = lax.ppermute(send_a, 'seq', near_pairs())  3.27 us
    pallas_call x1, Pallas kernels, project(): pl.pallas_call(project_kernel, out_shape=[shape((feats // LANES, batch, p...  3 us
    pallas_call x1, Pallas kernels, input_gradient(): pl.pallas_call(input_kernel, out_shape=[jax.ShapeDtypeStruct((batch, rows...  2.33 us
    pallas_call x1, Pallas kernels, late(): pl.pallas_call(functools.partial(late_kernel, col), out_shape=[shape((bat...  2.32 us
    unnamed x8, local copies, waits for them, and re-layouts  1.35 us
    pallas_call x1, Pallas kernels, own(): pl.pallas_call(own_kernel, out_shape=[shape((2 * half, strip, x.shape[2])...  1.01 us
  transfers between devices with their start and end apart: 11, of which 5 were waited for; matrix products, arithmetic and copies ran while one was open for 0% of the time, Pallas kernels for 28%

profile of v4, /device:TPU:0, one launch (start us, length us, event | category | flops | bytes accessed | tf_op | source)
XLA Modules:
  0.0 34.7 jit_solution(11266325136520024256)
XLA Ops:
  0.6 0.5 %collective-permute-start = (bf16[2,256,768]{2,1,0:T(8,128)(2,1)}, bf16[2,256,768]{2,1,0:T(8,128)(2,1)S(1)}, u32[]{:S(2)}, u32[]{:S(2)}) collective-permute-start(bf16[2,256,768]{2,1,0:T(8,128)(2,1)} %x_ref.7), channel_id=1, source_target_pairs={{0,4},{4,0},{8,12},{12,8},{16,20},{20,16},{24,28},{28,24},{1,5},{5... | collective-permute-start | bytes 2359304 | tf_op jit(solution)/shard_map/ppermute | solution.py:506
  1.1 0.1 collective-permute-start.1
  1.2 1.0 %edges.1.far_ref = bf16[4,2048]{1,0:T(4,128)(2,1)S(1)} custom-call(bf16[2,256,768]{2,1,0:T(8,128)(2,1)} %x_ref.7, bf16[2,256,1280]{2,1,0:T(8,128)(2,1)} %u_ref.7), custom_call_target="tpu_custom_call" | custom-call | bytes 1000 | tf_op jit(solution)/shard_map/edges/pallas_call | solution.py:66
  2.2 0.0 copy-start
  2.2 0.0 copy-start.1
  2.2 0.0 copy-start.2
  2.2 0.0 copy-start.3
  2.3 0.8 %collective-permute-start.2 = (bf16[4,2048]{1,0:T(4,128)(2,1)S(1)}, bf16[4,2048]{1,0:T(4,128)(2,1)S(1)}, u32[]{:S(2)}, u32[]{:S(2)}) collective-permute-start(bf16[4,2048]{1,0:T(4,128)(2,1)S(1)} %relay.1), channel_id=1, source_target_pairs={{4,8},{8,4},{12,16},{16,12},{20,24},{24,20},{5,9},{9,5},{13,17},{1... | collective-permute-start | bytes 49160 | tf_op jit(solution)/shard_map/ppermute | solution.py:508
  3.1 0.5 %copy-done = bf16[2,256,1280]{2,1,0:T(8,128)(2,1)S(1)} copy-done((bf16[2,256,1280]{2,1,0:T(8,128)(2,1)S(1)}, bf16[2,256,1280]{2,1,0:T(8,128)(2,1)}, u32[]{:S(2)}) %copy-start) | copy-done | bytes 1310744
  3.5 0.2 copy-done.1
  3.7 0.7 %copy-done.2 = bf16[768,1280]{1,0:T(8,128)(2,1)S(1)} copy-done((bf16[768,1280]{1,0:T(8,128)(2,1)S(1)}, bf16[768,1280]{1,0:T(8,128)(2,1)}, u32[]{:S(2)}) %copy-start.2) | copy-done | bytes 1966104
  4.4 0.0 copy-done.3
  4.4 3.0 %project.1 = (f32[10,2,352,128]{3,2,1,0:T(8,128)S(1)}, bf16[2,256,640]{2,1,0:T(8,128)(2,1)S(1)}) custom-call(bf16[2,256,768]{2,1,0:T(8,128)(2,1)S(1)} %copy-done.1, bf16[768,1280]{1,0:T(8,128)(2,1)S(1)} %copy-done.2, bf16[2,256,1280]{2,1,0:T(8,128)(2,1)S(1)} %copy-done, f32[3,1280]{1,0:T(4,128)S(1)} %copy-done.3), custom_call_target="tpu_custom_call" | custom-call | flops 4000000000 | bytes 4000000 | tf_op jit(solution)/shard_map/project/pallas_call | solution.py:178
  7.4 0.0 collective-permute-done.2.far_ref
  7.4 0.0 collective-permute-done.pair_x.other_ref
  7.4 0.0 collective-permute-done.1.pair_u
  7.4 0.6 %early.1 = (bf16[2,256,640]{2,1,0:T(8,128)(2,1)S(1)}, f32[2,8,1280]{2,1,0:T(8,128)S(1)}, f32[2,8,1280]{2,1,0:T(8,128)S(1)}, bf16[2,160,512]{2,1,0:T(8,128)(2,1)S(1)}, bf16[2,160,512]{2,1,0:T(8,128)(2,1)S(1)}) custom-call(bf16[2,256,768]{2,1,0:T(8,128)(2,1)S(1)} %copy-done.1, bf16[768,1280]{1,0:T(8,128)(2,1)S(1)} %copy-done.2, ...), custom_call_target="tpu_custom_call" | custom-call | flops 1000000000 | bytes 4000000 | tf_op jit(solution)/shard_map/early/pallas_call | solution.py:290
  8.0 3.3 %collective-permute-start.4 = (bf16[2,160,512]{2,1,0:T(8,128)(2,1)S(1)}, bf16[2,160,512]{2,1,0:T(8,128)(2,1)S(1)}, u32[]{:S(2)}, u32[]{:S(2)}) collective-permute-start(bf16[2,160,512]{2,1,0:T(8,128)(2,1)S(1)} %get-tuple-element.31), channel_id=1, source_target_pairs={{0,4},{4,0},{8,12},{12,8},{16,20},{20,16},{24,28},{28,24},{1,5},{5... | collective-permute-start | bytes 983048 | tf_op jit(solution)/shard_map/ppermute | solution.py:513
  11.3 2.3 %late.1 = (bf16[2,256,640]{2,1,0:T(8,128)(2,1)S(1)}, bf16[2,160,512]{2,1,0:T(8,128)(2,1)S(1)}, bf16[2,160,512]{2,1,0:T(8,128)(2,1)S(1)}) custom-call(bf16[2,256,1280]{2,1,0:T(8,128)(2,1)S(1)} %copy-done, f32[3,1280]{1,0:T(4,128)S(1)} %copy-done.3, f32[10,2,352,128]{3,2,1,0:T(8,128)S(1)} %get-tuple-element.21.proj, ...), custom_call_target="tpu_custom_call" | custom-call | flops 4000000000 | bytes 4000000 | tf_op jit(solution)/shard_map/late/pallas_call | solution.py:305
  13.6 0.1 collective-permute-start.3
  13.7 0.0 collective-permute-done.4.got_a
  13.7 1.0 %own.1 = (f32[4,160,768]{2,1,0:T(8,128)S(1)}, bf16[4,4,240,128]{3,2,1,0:T(8,128)(2,1)S(1)}) custom-call(bf16[2,256,768]{2,1,0:T(8,128)(2,1)S(1)} %copy-done.1, bf16[2,256,768]{2,1,0:T(8,128)(2,1)S(1)} %collective-permute-done.pair_x.other_ref, bf16[2,160,512]{2,1,0:T(8,128)(2,1)S(1)} %get-tuple-element.29.mine_a, ...), custom_call_target="tpu_custom_call" | custom-call | flops 1000000000 | bytes 4000000 | tf_op jit(solution)/shard_map/own/pallas_call | solution.py:360
  14.7 0.6 %collective-permute-done.3.got_b = bf16[2,160,512]{2,1,0:T(8,128)(2,1)S(1)} collective-permute-done((bf16[2,160,512]{2,1,0:T(8,128)(2,1)S(1)}, bf16[2,160,512]{2,1,0:T(8,128)(2,1)S(1)}, u32[]{:S(2)}, u32[]{:S(2)}) %collective-permute-start.3) | collective-permute-done | bytes 327712 | tf_op jit(solution)/shard_map/ppermute | solution.py:515
  15.3 0.5 %pack.1 = (f32[4,160,768]{2,1,0:T(8,128)S(1)}, bf16[4,4,240,128]{3,2,1,0:T(8,128)(2,1)S(1)}) custom-call(bf16[2,256,768]{2,1,0:T(8,128)(2,1)S(1)} %collective-permute-done.pair_x.other_ref, bf16[2,160,512]{2,1,0:T(8,128)(2,1)S(1)} %collective-permute-done.3.got_b, ...), custom_call_target="tpu_custom_call", output_to_operand_aliasing={{0}: (2, {}), {1}: (3, {})} | custom-call | tf_op jit(solution)/shard_map/pack/pallas_call | solution.py:380
  15.8 0.1 slice_bitcast_fusion
  15.9 2.5 %collective-permute-start.7 = (bf16[4,240,128]{2,1,0:T(8,128)(2,1)S(1)}, bf16[4,240,128]{2,1,0:T(8,128)(2,1)S(1)}, u32[]{:S(2)}, u32[]{:S(2)}) collective-permute-start(bf16[4,240,128]{2,1,0:T(8,128)(2,1)S(1)} %get-tuple-element.40), channel_id=1, source_target_pairs={{0,3},{1,2},{2,1},{3,0},{4,20},{5,21},{6,22},{7,23},{8,11},{9,10},... | collective-permute-start | bytes 737288 | tf_op jit(solution)/shard_map/ppermute | solution.py:480
  18.4 0.5 %collective-permute-start.6 = (bf16[4,240,128]{2,1,0:T(8,128)(2,1)S(1)}, bf16[4,240,128]{2,1,0:T(8,128)(2,1)S(1)}, u32[]{:S(2)}, u32[]{:S(2)}) collective-permute-start(bf16[4,240,128]{2,1,0:T(8,128)(2,1)S(1)} %get-tuple-element.41), channel_id=1, source_target_pairs={{0,1},{1,0},{2,3},{3,2},{4,12},{5,13},{6,14},{7,15},{8,9},{9,8},{1... | collective-permute-start | bytes 737288 | tf_op jit(solution)/shard_map/ppermute | solution.py:480
  18.9 0.5 %collective-permute-start.5 = (bf16[4,240,128]{2,1,0:T(8,128)(2,1)S(1)}, bf16[4,240,128]{2,1,0:T(8,128)(2,1)S(1)}, u32[]{:S(2)}, u32[]{:S(2)}) collective-permute-start(bf16[4,240,128]{2,1,0:T(8,128)(2,1)S(1)} %get-tuple-element.42), channel_id=1, source_target_pairs={{0,2},{1,3},{2,0},{3,1},{4,28},{5,29},{6,30},{7,31},{8,10},{9,11},... | collective-permute-start | bytes 737288 | tf_op jit(solution)/shard_map/ppermute | solution.py:480
  19.5 2.3 %input_gradient.1 = (bf16[2,256,768]{2,1,0:T(8,128)(2,1)}, f32[8,128]{1,0:T(8,128)S(1)}) custom-call(bf16[2,256,640]{2,1,0:T(8,128)(2,1)S(1)} %get-tuple-element.23.gp_a, bf16[2,256,640]{2,1,0:T(8,128)(2,1)S(1)} %get-tuple-element.26.gp_b, bf16[768,1280]{1,0:T(8,128)(2,1)S(1)} %copy-done.2), custom_call_target="tpu_custom_call" | custom-call | flops 2000000000 | bytes 1000000 | tf_op jit(solution)/shard_map/input_gradient/pallas_call | solution.py:423
  21.8 1.3 %collective-permute-done.7.three_ref = bf16[4,240,128]{2,1,0:T(8,128)(2,1)S(1)} collective-permute-done((bf16[4,240,128]{2,1,0:T(8,128)(2,1)S(1)}, bf16[4,240,128]{2,1,0:T(8,128)(2,1)S(1)}, u32[]{:S(2)}, u32[]{:S(2)}) %collective-permute-start.7) | collective-permute-done | bytes 245792 | tf_op jit(solution)/shard_map/ppermute | solution.py:480
  23.1 2.6 %collective-permute-done.6.two_ref = bf16[4,240,128]{2,1,0:T(8,128)(2,1)S(1)} collective-permute-done((bf16[4,240,128]{2,1,0:T(8,128)(2,1)S(1)}, bf16[4,240,128]{2,1,0:T(8,128)(2,1)S(1)}, u32[]{:S(2)}, u32[]{:S(2)}) %collective-permute-start.6) | collective-permute-done | bytes 245792 | tf_op jit(solution)/shard_map/ppermute | solution.py:480
  25.8 0.0 collective-permute-done.5.one_ref
  25.8 0.1 fold.1
  25.9 2.2 %collective-permute-start.8 = (bf16[240,128]{1,0:T(8,128)(2,1)S(1)}, bf16[240,128]{1,0:T(8,128)(2,1)S(1)}, u32[]{:S(2)}, u32[]{:S(2)}) collective-permute-start(bf16[240,128]{1,0:T(8,128)(2,1)S(1)} %get-tuple-element.37), channel_id=1, source_target_pairs={{0,24},{1,25},{2,26},{3,27},{4,7},{5,6},{6,5},{7,4},{8,16},{9,17},... | collective-permute-start | bytes 184328 | tf_op jit(solution)/shard_map/ppermute | solution.py:480
  28.2 0.9 %collective-permute-start.9 = (bf16[240,128]{1,0:T(8,128)(2,1)S(1)}, bf16[240,128]{1,0:T(8,128)(2,1)S(1)}, u32[]{:S(2)}, u32[]{:S(2)}) collective-permute-start(bf16[240,128]{1,0:T(8,128)(2,1)S(1)} %get-tuple-element.38), channel_id=1, source_target_pairs={{0,16},{1,17},{2,18},{3,19},{4,6},{5,7},{6,4},{7,5},{8,24},{9,25},... | collective-permute-start | bytes 184328 | tf_op jit(solution)/shard_map/ppermute | solution.py:480
  29.0 1.4 %collective-permute-start.10 = (bf16[240,128]{1,0:T(8,128)(2,1)S(1)}, bf16[240,128]{1,0:T(8,128)(2,1)S(1)}, u32[]{:S(2)}, u32[]{:S(2)}) collective-permute-start(bf16[240,128]{1,0:T(8,128)(2,1)S(1)} %get-tuple-element.39), channel_id=1, source_target_pairs={{0,8},{1,9},{2,10},{3,11},{4,5},{5,4},{6,7},{7,6},{8,0},{9,1},{10,... | collective-permute-start | bytes 184328 | tf_op jit(solution)/shard_map/ppermute | solution.py:480
  30.4 1.6 %collective-permute-done.8.one_ref = bf16[240,128]{1,0:T(8,128)(2,1)S(1)} collective-permute-done((bf16[240,128]{1,0:T(8,128)(2,1)S(1)}, bf16[240,128]{1,0:T(8,128)(2,1)S(1)}, u32[]{:S(2)}, u32[]{:S(2)}) %collective-permute-start.8) | collective-permute-done | bytes 61472 | tf_op jit(solution)/shard_map/ppermute | solution.py:480
  32.0 1.9 %collective-permute-done.9.two_ref = bf16[240,128]{1,0:T(8,128)(2,1)S(1)} collective-permute-done((bf16[240,128]{1,0:T(8,128)(2,1)S(1)}, bf16[240,128]{1,0:T(8,128)(2,1)S(1)}, u32[]{:S(2)}, u32[]{:S(2)}) %collective-permute-start.9) | collective-permute-done | bytes 61472 | tf_op jit(solution)/shard_map/ppermute | solution.py:480
  33.9 0.0 collective-permute-done.10.three_ref
  33.9 0.8 %last.1 = f32[160,192]{1,0:T(8,128)} custom-call(f32[240,128]{1,0:T(8,128)S(1)} %get-tuple-element.36.own_ref, bf16[240,128]{1,0:T(8,128)(2,1)S(1)} %collective-permute-done.8.one_ref, bf16[240,128]{1,0:T(8,128)(2,1)S(1)} %collective-permute-done.9.two_ref, bf16[240,128]{1,0:T(8,128)(2,1)S(1)} %collective-permute-done.10.three_ref), custom_call_target="tpu_custom_call" | custom-call | tf_op jit(solution)/shard_map/last/pallas_call | solution.py:456
  (1 shorter events, 0.0 us)
Async XLA Ops:
  0.6 6.8 %collective-permute-start = (bf16[2,256,768]{2,1,0:T(8,128)(2,1)}, bf16[2,256,768]{2,1,0:T(8,128)(2,1)S(1)}, u32[]{:S(2)}, u32[]{:S(2)}) collective-permute-start(bf16[2,256,768]{2,1,0:T(8,128)(2,1)} %x_ref.7), channel_id=1, source_target_pairs={{0,4},{4,0},{8,12},{12,8},{16,20},{20,16},{24,28},{28,24},{1,5},{5... | collective-permute-start | bytes 2359304 | tf_op jit(solution)/shard_map/ppermute | solution.py:506
  1.1 6.3 %collective-permute-start.1 = (bf16[2,256,1280]{2,1,0:T(8,128)(2,1)}, bf16[2,256,1280]{2,1,0:T(8,128)(2,1)S(1)}, u32[]{:S(2)}, u32[]{:S(2)}) collective-permute-start(bf16[2,256,1280]{2,1,0:T(8,128)(2,1)} %u_ref.7), channel_id=1, source_target_pairs={{0,4},{4,0},{8,12},{12,8},{16,20},{20,16},{24,28},{28,24},{1,5},{5... | collective-permute-start | bytes 3932168 | tf_op jit(solution)/shard_map/ppermute | solution.py:507
  2.2 1.3 %copy-start = (bf16[2,256,1280]{2,1,0:T(8,128)(2,1)S(1)}, bf16[2,256,1280]{2,1,0:T(8,128)(2,1)}, u32[]{:S(2)}) copy-start(bf16[2,256,1280]{2,1,0:T(8,128)(2,1)} %u_ref.7) | copy-start | bytes 3932164
  2.2 1.5 %copy-start.1 = (bf16[2,256,768]{2,1,0:T(8,128)(2,1)S(1)}, bf16[2,256,768]{2,1,0:T(8,128)(2,1)}, u32[]{:S(2)}) copy-start(bf16[2,256,768]{2,1,0:T(8,128)(2,1)} %x_ref.7) | copy-start | bytes 2359300
  2.2 2.2 %copy-start.2 = (bf16[768,1280]{1,0:T(8,128)(2,1)S(1)}, bf16[768,1280]{1,0:T(8,128)(2,1)}, u32[]{:S(2)}) copy-start(bf16[768,1280]{1,0:T(8,128)(2,1)} %w_ref.5) | copy-start | bytes 5898244
  2.2 2.2 %copy-start.3 = (f32[3,1280]{1,0:T(4,128)S(1)}, f32[3,1280]{1,0:T(4,128)}, u32[]{:S(2)}) copy-start(f32[3,1280]{1,0:T(4,128)} %k_ref.5) | copy-start | bytes 46084
  2.3 5.1 %collective-permute-start.2 = (bf16[4,2048]{1,0:T(4,128)(2,1)S(1)}, bf16[4,2048]{1,0:T(4,128)(2,1)S(1)}, u32[]{:S(2)}, u32[]{:S(2)}) collective-permute-start(bf16[4,2048]{1,0:T(4,128)(2,1)S(1)} %relay.1), channel_id=1, source_target_pairs={{4,8},{8,4},{12,16},{16,12},{20,24},{24,20},{5,9},{9,5},{13,17},{1... | collective-permute-start | bytes 49160 | tf_op jit(solution)/shard_map/ppermute | solution.py:508
  8.0 5.7 %collective-permute-start.4 = (bf16[2,160,512]{2,1,0:T(8,128)(2,1)S(1)}, bf16[2,160,512]{2,1,0:T(8,128)(2,1)S(1)}, u32[]{:S(2)}, u32[]{:S(2)}) collective-permute-start(bf16[2,160,512]{2,1,0:T(8,128)(2,1)S(1)} %get-tuple-element.31), channel_id=1, source_target_pairs={{0,4},{4,0},{8,12},{12,8},{16,20},{20,16},{24,28},{28,24},{1,5},{5... | collective-permute-start | bytes 983048 | tf_op jit(solution)/shard_map/ppermute | solution.py:513
  13.6 1.7 %collective-permute-start.3 = (bf16[2,160,512]{2,1,0:T(8,128)(2,1)S(1)}, bf16[2,160,512]{2,1,0:T(8,128)(2,1)S(1)}, u32[]{:S(2)}, u32[]{:S(2)}) collective-permute-start(bf16[2,160,512]{2,1,0:T(8,128)(2,1)S(1)} %get-tuple-element.28), channel_id=1, source_target_pairs={{0,4},{4,0},{8,12},{12,8},{16,20},{20,16},{24,28},{28,24},{1,5},{5... | collective-permute-start | bytes 983048 | tf_op jit(solution)/shard_map/ppermute | solution.py:515
  15.9 7.2 %collective-permute-start.7 = (bf16[4,240,128]{2,1,0:T(8,128)(2,1)S(1)}, bf16[4,240,128]{2,1,0:T(8,128)(2,1)S(1)}, u32[]{:S(2)}, u32[]{:S(2)}) collective-permute-start(bf16[4,240,128]{2,1,0:T(8,128)(2,1)S(1)} %get-tuple-element.40), channel_id=1, source_target_pairs={{0,3},{1,2},{2,1},{3,0},{4,20},{5,21},{6,22},{7,23},{8,11},{9,10},... | collective-permute-start | bytes 737288 | tf_op jit(solution)/shard_map/ppermute | solution.py:480
  18.4 7.3 %collective-permute-start.6 = (bf16[4,240,128]{2,1,0:T(8,128)(2,1)S(1)}, bf16[4,240,128]{2,1,0:T(8,128)(2,1)S(1)}, u32[]{:S(2)}, u32[]{:S(2)}) collective-permute-start(bf16[4,240,128]{2,1,0:T(8,128)(2,1)S(1)} %get-tuple-element.41), channel_id=1, source_target_pairs={{0,1},{1,0},{2,3},{3,2},{4,12},{5,13},{6,14},{7,15},{8,9},{9,8},{1... | collective-permute-start | bytes 737288 | tf_op jit(solution)/shard_map/ppermute | solution.py:480
  18.9 6.8 %collective-permute-start.5 = (bf16[4,240,128]{2,1,0:T(8,128)(2,1)S(1)}, bf16[4,240,128]{2,1,0:T(8,128)(2,1)S(1)}, u32[]{:S(2)}, u32[]{:S(2)}) collective-permute-start(bf16[4,240,128]{2,1,0:T(8,128)(2,1)S(1)} %get-tuple-element.42), channel_id=1, source_target_pairs={{0,2},{1,3},{2,0},{3,1},{4,28},{5,29},{6,30},{7,31},{8,10},{9,11},... | collective-permute-start | bytes 737288 | tf_op jit(solution)/shard_map/ppermute | solution.py:480
  25.9 6.1 %collective-permute-start.8 = (bf16[240,128]{1,0:T(8,128)(2,1)S(1)}, bf16[240,128]{1,0:T(8,128)(2,1)S(1)}, u32[]{:S(2)}, u32[]{:S(2)}) collective-permute-start(bf16[240,128]{1,0:T(8,128)(2,1)S(1)} %get-tuple-element.37), channel_id=1, source_target_pairs={{0,24},{1,25},{2,26},{3,27},{4,7},{5,6},{6,5},{7,4},{8,16},{9,17},... | collective-permute-start | bytes 184328 | tf_op jit(solution)/shard_map/ppermute | solution.py:480
  28.2 5.8 %collective-permute-start.9 = (bf16[240,128]{1,0:T(8,128)(2,1)S(1)}, bf16[240,128]{1,0:T(8,128)(2,1)S(1)}, u32[]{:S(2)}, u32[]{:S(2)}) collective-permute-start(bf16[240,128]{1,0:T(8,128)(2,1)S(1)} %get-tuple-element.38), channel_id=1, source_target_pairs={{0,16},{1,17},{2,18},{3,19},{4,6},{5,7},{6,4},{7,5},{8,24},{9,25},... | collective-permute-start | bytes 184328 | tf_op jit(solution)/shard_map/ppermute | solution.py:480
  29.0 4.9 %collective-permute-start.10 = (bf16[240,128]{1,0:T(8,128)(2,1)S(1)}, bf16[240,128]{1,0:T(8,128)(2,1)S(1)}, u32[]{:S(2)}, u32[]{:S(2)}) collective-permute-start(bf16[240,128]{1,0:T(8,128)(2,1)S(1)} %get-tuple-element.39), channel_id=1, source_target_pairs={{0,8},{1,9},{2,10},{3,11},{4,5},{5,4},{6,7},{7,6},{8,0},{9,1},{10,... | collective-permute-start | bytes 184328 | tf_op jit(solution)/shard_map/ppermute | solution.py:480

commit v5 on v4

--- a/solution.py
+++ b/solution.py
@@ -18,6 +18,7 @@
 PAD = 8
 HOP = 9
 FIRST = ((0, 0), (3, 2), (1, 1), (2, 3))
+SECOND = ((0, 0), (3, 2), (2, 3), (1, 1))
 VMEM_BYTES = 14 * 1024 * 1024
 
 
@@ -390,11 +391,10 @@
 
 def fold_kernel(own_ref, one_ref, two_ref, three_ref, token, *outs):
     core, zed, dee = position()
-    mine = jnp.where(core == 0, zed, dee)
-    for k in (3, 2, 1, 0):
-        j = jnp.bitwise_xor(mine, k)
+    for (z_turn, d_turn), out in zip(SECOND, outs):
+        j = jnp.where(core == 0, jnp.bitwise_xor(zed, z_turn), jnp.bitwise_xor(dee, d_turn))
         total = own_ref[0, j].astype(F32) + one_ref[j].astype(F32) + two_ref[j].astype(F32) + three_ref[j].astype(F32)
-        outs[k][...] = total.astype(outs[k].dtype)
+        out[...] = total.astype(out.dtype)
 
 
 def fold(parts, token):
@@ -519,7 +519,7 @@
     z_bits = [m * 2 * n_dp for m in range(4)]
     got = [exchange(blocks[i], *(FIRST[i][0], z_bits[FIRST[i][1]])) for i in (3, 2, 1)]
     own_block, *messages = fold([blocks] + got, token)
-    got = [exchange(messages[k - 1], z_bits[k], k) for k in (3, 2, 1)]
+    got = [exchange(message, z_bits[z], d) for message, (z, d) in zip(messages, SECOND[1:])]
     return input_grad, last([own_block] + got, 1.0 / (batch * n_dp))
 
 

time: 34.9 us -> 34.9 us (level)
  no operation moved by 1% of the time
where the time goes in v5:
time: 34.9 us; the launch traced here: 34.7 us
  starting transfers between devices  12.8 us (37%)
  Pallas kernels  11.6 us (33%)
  waiting for transfers between devices  8.15 us (23%)
  local copies, waits for them, and re-layouts  1.4 us (4%)
  between operations  0.76 us (2%)
    ppermute x6, starting transfers between devices, exchange(): return lax.ppermute(array, ('seq', 'dp'), pairs)  8.01 us
    ppermute x6, waiting for transfers between devices, exchange(): return lax.ppermute(array, ('seq', 'dp'), pairs)  7.56 us
    ppermute x1, starting transfers between devices, on_device(): got_a = lax.ppermute(send_a, 'seq', near_pairs())  3.27 us
    pallas_call x1, Pallas kernels, project(): pl.pallas_call(project_kernel, out_shape=[shape((feats // LANES, batch, p...  3 us
    pallas_call x1, Pallas kernels, input_gradient(): pl.pallas_call(input_kernel, out_shape=[jax.ShapeDtypeStruct((batch, rows...  2.33 us
    pallas_call x1, Pallas kernels, late(): pl.pallas_call(functools.partial(late_kernel, col), out_shape=[shape((bat...  2.32 us
    unnamed x8, local copies, waits for them, and re-layouts  1.35 us
    pallas_call x1, Pallas kernels, own(): pl.pallas_call(own_kernel, out_shape=[shape((2 * half, strip, x.shape[2])...  1.01 us
  transfers between devices with their start and end apart: 11, of which 5 were waited for; matrix products, arithmetic and copies ran while one was open for 0% of the time, Pallas kernels for 28%

profile of v5, /device:TPU:0, one launch (start us, length us, event | category | flops | bytes accessed | tf_op | source)
XLA Modules:
  0.0 34.7 jit_solution(1224859413053171351)
XLA Ops:
  0.6 0.5 %collective-permute-start = (bf16[2,256,768]{2,1,0:T(8,128)(2,1)}, bf16[2,256,768]{2,1,0:T(8,128)(2,1)S(1)}, u32[]{:S(2)}, u32[]{:S(2)}) collective-permute-start(bf16[2,256,768]{2,1,0:T(8,128)(2,1)} %x_ref.7), channel_id=1, source_target_pairs={{0,4},{4,0},{8,12},{12,8},{16,20},{20,16},{24,28},{28,24},{1,5},{5... | collective-permute-start | bytes 2359304 | tf_op jit(solution)/shard_map/ppermute | solution.py:506
  1.1 0.1 collective-permute-start.1
  1.2 1.0 %edges.1.far_ref = bf16[4,2048]{1,0:T(4,128)(2,1)S(1)} custom-call(bf16[2,256,768]{2,1,0:T(8,128)(2,1)} %x_ref.7, bf16[2,256,1280]{2,1,0:T(8,128)(2,1)} %u_ref.7), custom_call_target="tpu_custom_call" | custom-call | bytes 1000 | tf_op jit(solution)/shard_map/edges/pallas_call | solution.py:67
  2.2 0.0 copy-start
  2.2 0.0 copy-start.1
  2.2 0.0 copy-start.2
  2.2 0.0 copy-start.3
  2.3 0.8 %collective-permute-start.2 = (bf16[4,2048]{1,0:T(4,128)(2,1)S(1)}, bf16[4,2048]{1,0:T(4,128)(2,1)S(1)}, u32[]{:S(2)}, u32[]{:S(2)}) collective-permute-start(bf16[4,2048]{1,0:T(4,128)(2,1)S(1)} %relay.1), channel_id=1, source_target_pairs={{4,8},{8,4},{12,16},{16,12},{20,24},{24,20},{5,9},{9,5},{13,17},{1... | collective-permute-start | bytes 49160 | tf_op jit(solution)/shard_map/ppermute | solution.py:508
  3.1 0.5 %copy-done = bf16[2,256,1280]{2,1,0:T(8,128)(2,1)S(1)} copy-done((bf16[2,256,1280]{2,1,0:T(8,128)(2,1)S(1)}, bf16[2,256,1280]{2,1,0:T(8,128)(2,1)}, u32[]{:S(2)}) %copy-start) | copy-done | bytes 1310744
  3.5 0.2 copy-done.1
  3.7 0.7 %copy-done.2 = bf16[768,1280]{1,0:T(8,128)(2,1)S(1)} copy-done((bf16[768,1280]{1,0:T(8,128)(2,1)S(1)}, bf16[768,1280]{1,0:T(8,128)(2,1)}, u32[]{:S(2)}) %copy-start.2) | copy-done | bytes 1966104
  4.4 0.0 copy-done.3
  4.4 3.0 %project.1 = (f32[10,2,352,128]{3,2,1,0:T(8,128)S(1)}, bf16[2,256,640]{2,1,0:T(8,128)(2,1)S(1)}) custom-call(bf16[2,256,768]{2,1,0:T(8,128)(2,1)S(1)} %copy-done.1, bf16[768,1280]{1,0:T(8,128)(2,1)S(1)} %copy-done.2, bf16[2,256,1280]{2,1,0:T(8,128)(2,1)S(1)} %copy-done, f32[3,1280]{1,0:T(4,128)S(1)} %copy-done.3), custom_call_target="tpu_custom_call" | custom-call | flops 4000000000 | bytes 4000000 | tf_op jit(solution)/shard_map/project/pallas_call | solution.py:179
  7.4 0.0 collective-permute-done.2.far_ref
  7.4 0.0 collective-permute-done.pair_x.other_ref
  7.4 0.0 collective-permute-done.1.pair_u
  7.4 0.6 %early.1 = (bf16[2,256,640]{2,1,0:T(8,128)(2,1)S(1)}, f32[2,8,1280]{2,1,0:T(8,128)S(1)}, f32[2,8,1280]{2,1,0:T(8,128)S(1)}, bf16[2,160,512]{2,1,0:T(8,128)(2,1)S(1)}, bf16[2,160,512]{2,1,0:T(8,128)(2,1)S(1)}) custom-call(bf16[2,256,768]{2,1,0:T(8,128)(2,1)S(1)} %copy-done.1, bf16[768,1280]{1,0:T(8,128)(2,1)S(1)} %copy-done.2, ...), custom_call_target="tpu_custom_call" | custom-call | flops 1000000000 | bytes 4000000 | tf_op jit(solution)/shard_map/early/pallas_call | solution.py:291
  8.0 3.3 %collective-permute-start.4 = (bf16[2,160,512]{2,1,0:T(8,128)(2,1)S(1)}, bf16[2,160,512]{2,1,0:T(8,128)(2,1)S(1)}, u32[]{:S(2)}, u32[]{:S(2)}) collective-permute-start(bf16[2,160,512]{2,1,0:T(8,128)(2,1)S(1)} %get-tuple-element.31), channel_id=1, source_target_pairs={{0,4},{4,0},{8,12},{12,8},{16,20},{20,16},{24,28},{28,24},{1,5},{5... | collective-permute-start | bytes 983048 | tf_op jit(solution)/shard_map/ppermute | solution.py:513
  11.3 2.3 %late.1 = (bf16[2,256,640]{2,1,0:T(8,128)(2,1)S(1)}, bf16[2,160,512]{2,1,0:T(8,128)(2,1)S(1)}, bf16[2,160,512]{2,1,0:T(8,128)(2,1)S(1)}) custom-call(bf16[2,256,1280]{2,1,0:T(8,128)(2,1)S(1)} %copy-done, f32[3,1280]{1,0:T(4,128)S(1)} %copy-done.3, f32[10,2,352,128]{3,2,1,0:T(8,128)S(1)} %get-tuple-element.21.proj, ...), custom_call_target="tpu_custom_call" | custom-call | flops 4000000000 | bytes 4000000 | tf_op jit(solution)/shard_map/late/pallas_call | solution.py:306
  13.6 0.1 collective-permute-start.3
  13.7 0.0 collective-permute-done.4.got_a
  13.7 1.0 %own.1 = (f32[4,160,768]{2,1,0:T(8,128)S(1)}, bf16[4,4,240,128]{3,2,1,0:T(8,128)(2,1)S(1)}) custom-call(bf16[2,256,768]{2,1,0:T(8,128)(2,1)S(1)} %copy-done.1, bf16[2,256,768]{2,1,0:T(8,128)(2,1)S(1)} %collective-permute-done.pair_x.other_ref, bf16[2,160,512]{2,1,0:T(8,128)(2,1)S(1)} %get-tuple-element.29.mine_a, ...), custom_call_target="tpu_custom_call" | custom-call | flops 1000000000 | bytes 4000000 | tf_op jit(solution)/shard_map/own/pallas_call | solution.py:361
  14.7 0.6 %collective-permute-done.3.got_b = bf16[2,160,512]{2,1,0:T(8,128)(2,1)S(1)} collective-permute-done((bf16[2,160,512]{2,1,0:T(8,128)(2,1)S(1)}, bf16[2,160,512]{2,1,0:T(8,128)(2,1)S(1)}, u32[]{:S(2)}, u32[]{:S(2)}) %collective-permute-start.3) | collective-permute-done | bytes 327712 | tf_op jit(solution)/shard_map/ppermute | solution.py:515
  15.3 0.5 %pack.1 = (f32[4,160,768]{2,1,0:T(8,128)S(1)}, bf16[4,4,240,128]{3,2,1,0:T(8,128)(2,1)S(1)}) custom-call(bf16[2,256,768]{2,1,0:T(8,128)(2,1)S(1)} %collective-permute-done.pair_x.other_ref, bf16[2,160,512]{2,1,0:T(8,128)(2,1)S(1)} %collective-permute-done.3.got_b, ...), custom_call_target="tpu_custom_call", output_to_operand_aliasing={{0}: (2, {}), {1}: (3, {})} | custom-call | tf_op jit(solution)/shard_map/pack/pallas_call | solution.py:381
  15.8 0.1 slice_bitcast_fusion
  15.9 2.5 %collective-permute-start.7 = (bf16[4,240,128]{2,1,0:T(8,128)(2,1)S(1)}, bf16[4,240,128]{2,1,0:T(8,128)(2,1)S(1)}, u32[]{:S(2)}, u32[]{:S(2)}) collective-permute-start(bf16[4,240,128]{2,1,0:T(8,128)(2,1)S(1)} %get-tuple-element.40), channel_id=1, source_target_pairs={{0,3},{1,2},{2,1},{3,0},{4,20},{5,21},{6,22},{7,23},{8,11},{9,10},... | collective-permute-start | bytes 737288 | tf_op jit(solution)/shard_map/ppermute | solution.py:480
  18.4 0.5 %collective-permute-start.6 = (bf16[4,240,128]{2,1,0:T(8,128)(2,1)S(1)}, bf16[4,240,128]{2,1,0:T(8,128)(2,1)S(1)}, u32[]{:S(2)}, u32[]{:S(2)}) collective-permute-start(bf16[4,240,128]{2,1,0:T(8,128)(2,1)S(1)} %get-tuple-element.41), channel_id=1, source_target_pairs={{0,1},{1,0},{2,3},{3,2},{4,12},{5,13},{6,14},{7,15},{8,9},{9,8},{1... | collective-permute-start | bytes 737288 | tf_op jit(solution)/shard_map/ppermute | solution.py:480
  18.9 0.5 %collective-permute-start.5 = (bf16[4,240,128]{2,1,0:T(8,128)(2,1)S(1)}, bf16[4,240,128]{2,1,0:T(8,128)(2,1)S(1)}, u32[]{:S(2)}, u32[]{:S(2)}) collective-permute-start(bf16[4,240,128]{2,1,0:T(8,128)(2,1)S(1)} %get-tuple-element.42), channel_id=1, source_target_pairs={{0,2},{1,3},{2,0},{3,1},{4,28},{5,29},{6,30},{7,31},{8,10},{9,11},... | collective-permute-start | bytes 737288 | tf_op jit(solution)/shard_map/ppermute | solution.py:480
  19.5 2.3 %input_gradient.1 = (bf16[2,256,768]{2,1,0:T(8,128)(2,1)}, f32[8,128]{1,0:T(8,128)S(1)}) custom-call(bf16[2,256,640]{2,1,0:T(8,128)(2,1)S(1)} %get-tuple-element.23.gp_a, bf16[2,256,640]{2,1,0:T(8,128)(2,1)S(1)} %get-tuple-element.26.gp_b, bf16[768,1280]{1,0:T(8,128)(2,1)S(1)} %copy-done.2), custom_call_target="tpu_custom_call" | custom-call | flops 2000000000 | bytes 1000000 | tf_op jit(solution)/shard_map/input_gradient/pallas_call | solution.py:423
  21.8 1.3 %collective-permute-done.7.three_ref = bf16[4,240,128]{2,1,0:T(8,128)(2,1)S(1)} collective-permute-done((bf16[4,240,128]{2,1,0:T(8,128)(2,1)S(1)}, bf16[4,240,128]{2,1,0:T(8,128)(2,1)S(1)}, u32[]{:S(2)}, u32[]{:S(2)}) %collective-permute-start.7) | collective-permute-done | bytes 245792 | tf_op jit(solution)/shard_map/ppermute | solution.py:480
  23.1 2.6 %collective-permute-done.6.two_ref = bf16[4,240,128]{2,1,0:T(8,128)(2,1)S(1)} collective-permute-done((bf16[4,240,128]{2,1,0:T(8,128)(2,1)S(1)}, bf16[4,240,128]{2,1,0:T(8,128)(2,1)S(1)}, u32[]{:S(2)}, u32[]{:S(2)}) %collective-permute-start.6) | collective-permute-done | bytes 245792 | tf_op jit(solution)/shard_map/ppermute | solution.py:480
  25.8 0.0 collective-permute-done.5.one_ref
  25.8 0.1 fold.1
  25.9 2.2 %collective-permute-start.8 = (bf16[240,128]{1,0:T(8,128)(2,1)S(1)}, bf16[240,128]{1,0:T(8,128)(2,1)S(1)}, u32[]{:S(2)}, u32[]{:S(2)}) collective-permute-start(bf16[240,128]{1,0:T(8,128)(2,1)S(1)} %get-tuple-element.37), channel_id=1, source_target_pairs={{0,24},{1,25},{2,26},{3,27},{4,6},{5,7},{6,4},{7,5},{8,16},{9,17},... | collective-permute-start | bytes 184328 | tf_op jit(solution)/shard_map/ppermute | solution.py:480
  28.2 0.9 %collective-permute-start.9 = (bf16[240,128]{1,0:T(8,128)(2,1)S(1)}, bf16[240,128]{1,0:T(8,128)(2,1)S(1)}, u32[]{:S(2)}, u32[]{:S(2)}) collective-permute-start(bf16[240,128]{1,0:T(8,128)(2,1)S(1)} %get-tuple-element.38), channel_id=1, source_target_pairs={{0,16},{1,17},{2,18},{3,19},{4,7},{5,6},{6,5},{7,4},{8,24},{9,25},... | collective-permute-start | bytes 184328 | tf_op jit(solution)/shard_map/ppermute | solution.py:480
  29.0 1.4 %collective-permute-start.10 = (bf16[240,128]{1,0:T(8,128)(2,1)S(1)}, bf16[240,128]{1,0:T(8,128)(2,1)S(1)}, u32[]{:S(2)}, u32[]{:S(2)}) collective-permute-start(bf16[240,128]{1,0:T(8,128)(2,1)S(1)} %get-tuple-element.39), channel_id=1, source_target_pairs={{0,8},{1,9},{2,10},{3,11},{4,5},{5,4},{6,7},{7,6},{8,0},{9,1},{10,... | collective-permute-start | bytes 184328 | tf_op jit(solution)/shard_map/ppermute | solution.py:480
  30.4 1.6 %collective-permute-done.8.one_ref = bf16[240,128]{1,0:T(8,128)(2,1)S(1)} collective-permute-done((bf16[240,128]{1,0:T(8,128)(2,1)S(1)}, bf16[240,128]{1,0:T(8,128)(2,1)S(1)}, u32[]{:S(2)}, u32[]{:S(2)}) %collective-permute-start.8) | collective-permute-done | bytes 61472 | tf_op jit(solution)/shard_map/ppermute | solution.py:480
  32.0 1.9 %collective-permute-done.9.two_ref = bf16[240,128]{1,0:T(8,128)(2,1)S(1)} collective-permute-done((bf16[240,128]{1,0:T(8,128)(2,1)S(1)}, bf16[240,128]{1,0:T(8,128)(2,1)S(1)}, u32[]{:S(2)}, u32[]{:S(2)}) %collective-permute-start.9) | collective-permute-done | bytes 61472 | tf_op jit(solution)/shard_map/ppermute | solution.py:480
  33.9 0.0 collective-permute-done.10.three_ref
  33.9 0.8 %last.1 = f32[160,192]{1,0:T(8,128)} custom-call(f32[240,128]{1,0:T(8,128)S(1)} %get-tuple-element.36.own_ref, bf16[240,128]{1,0:T(8,128)(2,1)S(1)} %collective-permute-done.8.one_ref, bf16[240,128]{1,0:T(8,128)(2,1)S(1)} %collective-permute-done.9.two_ref, bf16[240,128]{1,0:T(8,128)(2,1)S(1)} %collective-permute-done.10.three_ref), custom_call_target="tpu_custom_call" | custom-call | tf_op jit(solution)/shard_map/last/pallas_call | solution.py:456
  (1 shorter events, 0.0 us)
Async XLA Ops:
  0.6 6.8 %collective-permute-start = (bf16[2,256,768]{2,1,0:T(8,128)(2,1)}, bf16[2,256,768]{2,1,0:T(8,128)(2,1)S(1)}, u32[]{:S(2)}, u32[]{:S(2)}) collective-permute-start(bf16[2,256,768]{2,1,0:T(8,128)(2,1)} %x_ref.7), channel_id=1, source_target_pairs={{0,4},{4,0},{8,12},{12,8},{16,20},{20,16},{24,28},{28,24},{1,5},{5... | collective-permute-start | bytes 2359304 | tf_op jit(solution)/shard_map/ppermute | solution.py:506
  1.1 6.3 %collective-permute-start.1 = (bf16[2,256,1280]{2,1,0:T(8,128)(2,1)}, bf16[2,256,1280]{2,1,0:T(8,128)(2,1)S(1)}, u32[]{:S(2)}, u32[]{:S(2)}) collective-permute-start(bf16[2,256,1280]{2,1,0:T(8,128)(2,1)} %u_ref.7), channel_id=1, source_target_pairs={{0,4},{4,0},{8,12},{12,8},{16,20},{20,16},{24,28},{28,24},{1,5},{5... | collective-permute-start | bytes 3932168 | tf_op jit(solution)/shard_map/ppermute | solution.py:507
  2.2 1.3 %copy-start = (bf16[2,256,1280]{2,1,0:T(8,128)(2,1)S(1)}, bf16[2,256,1280]{2,1,0:T(8,128)(2,1)}, u32[]{:S(2)}) copy-start(bf16[2,256,1280]{2,1,0:T(8,128)(2,1)} %u_ref.7) | copy-start | bytes 3932164
  2.2 1.5 %copy-start.1 = (bf16[2,256,768]{2,1,0:T(8,128)(2,1)S(1)}, bf16[2,256,768]{2,1,0:T(8,128)(2,1)}, u32[]{:S(2)}) copy-start(bf16[2,256,768]{2,1,0:T(8,128)(2,1)} %x_ref.7) | copy-start | bytes 2359300
  2.2 2.2 %copy-start.2 = (bf16[768,1280]{1,0:T(8,128)(2,1)S(1)}, bf16[768,1280]{1,0:T(8,128)(2,1)}, u32[]{:S(2)}) copy-start(bf16[768,1280]{1,0:T(8,128)(2,1)} %w_ref.5) | copy-start | bytes 5898244
  2.2 2.2 %copy-start.3 = (f32[3,1280]{1,0:T(4,128)S(1)}, f32[3,1280]{1,0:T(4,128)}, u32[]{:S(2)}) copy-start(f32[3,1280]{1,0:T(4,128)} %k_ref.5) | copy-start | bytes 46084
  2.3 5.1 %collective-permute-start.2 = (bf16[4,2048]{1,0:T(4,128)(2,1)S(1)}, bf16[4,2048]{1,0:T(4,128)(2,1)S(1)}, u32[]{:S(2)}, u32[]{:S(2)}) collective-permute-start(bf16[4,2048]{1,0:T(4,128)(2,1)S(1)} %relay.1), channel_id=1, source_target_pairs={{4,8},{8,4},{12,16},{16,12},{20,24},{24,20},{5,9},{9,5},{13,17},{1... | collective-permute-start | bytes 49160 | tf_op jit(solution)/shard_map/ppermute | solution.py:508
  8.0 5.7 %collective-permute-start.4 = (bf16[2,160,512]{2,1,0:T(8,128)(2,1)S(1)}, bf16[2,160,512]{2,1,0:T(8,128)(2,1)S(1)}, u32[]{:S(2)}, u32[]{:S(2)}) collective-permute-start(bf16[2,160,512]{2,1,0:T(8,128)(2,1)S(1)} %get-tuple-element.31), channel_id=1, source_target_pairs={{0,4},{4,0},{8,12},{12,8},{16,20},{20,16},{24,28},{28,24},{1,5},{5... | collective-permute-start | bytes 983048 | tf_op jit(solution)/shard_map/ppermute | solution.py:513
  13.6 1.7 %collective-permute-start.3 = (bf16[2,160,512]{2,1,0:T(8,128)(2,1)S(1)}, bf16[2,160,512]{2,1,0:T(8,128)(2,1)S(1)}, u32[]{:S(2)}, u32[]{:S(2)}) collective-permute-start(bf16[2,160,512]{2,1,0:T(8,128)(2,1)S(1)} %get-tuple-element.28), channel_id=1, source_target_pairs={{0,4},{4,0},{8,12},{12,8},{16,20},{20,16},{24,28},{28,24},{1,5},{5... | collective-permute-start | bytes 983048 | tf_op jit(solution)/shard_map/ppermute | solution.py:515
  15.9 7.2 %collective-permute-start.7 = (bf16[4,240,128]{2,1,0:T(8,128)(2,1)S(1)}, bf16[4,240,128]{2,1,0:T(8,128)(2,1)S(1)}, u32[]{:S(2)}, u32[]{:S(2)}) collective-permute-start(bf16[4,240,128]{2,1,0:T(8,128)(2,1)S(1)} %get-tuple-element.40), channel_id=1, source_target_pairs={{0,3},{1,2},{2,1},{3,0},{4,20},{5,21},{6,22},{7,23},{8,11},{9,10},... | collective-permute-start | bytes 737288 | tf_op jit(solution)/shard_map/ppermute | solution.py:480
  18.4 7.3 %collective-permute-start.6 = (bf16[4,240,128]{2,1,0:T(8,128)(2,1)S(1)}, bf16[4,240,128]{2,1,0:T(8,128)(2,1)S(1)}, u32[]{:S(2)}, u32[]{:S(2)}) collective-permute-start(bf16[4,240,128]{2,1,0:T(8,128)(2,1)S(1)} %get-tuple-element.41), channel_id=1, source_target_pairs={{0,1},{1,0},{2,3},{3,2},{4,12},{5,13},{6,14},{7,15},{8,9},{9,8},{1... | collective-permute-start | bytes 737288 | tf_op jit(solution)/shard_map/ppermute | solution.py:480
  18.9 6.8 %collective-permute-start.5 = (bf16[4,240,128]{2,1,0:T(8,128)(2,1)S(1)}, bf16[4,240,128]{2,1,0:T(8,128)(2,1)S(1)}, u32[]{:S(2)}, u32[]{:S(2)}) collective-permute-start(bf16[4,240,128]{2,1,0:T(8,128)(2,1)S(1)} %get-tuple-element.42), channel_id=1, source_target_pairs={{0,2},{1,3},{2,0},{3,1},{4,28},{5,29},{6,30},{7,31},{8,10},{9,11},... | collective-permute-start | bytes 737288 | tf_op jit(solution)/shard_map/ppermute | solution.py:480
  25.9 6.1 %collective-permute-start.8 = (bf16[240,128]{1,0:T(8,128)(2,1)S(1)}, bf16[240,128]{1,0:T(8,128)(2,1)S(1)}, u32[]{:S(2)}, u32[]{:S(2)}) collective-permute-start(bf16[240,128]{1,0:T(8,128)(2,1)S(1)} %get-tuple-element.37), channel_id=1, source_target_pairs={{0,24},{1,25},{2,26},{3,27},{4,6},{5,7},{6,4},{7,5},{8,16},{9,17},... | collective-permute-start | bytes 184328 | tf_op jit(solution)/shard_map/ppermute | solution.py:480
  28.2 5.8 %collective-permute-start.9 = (bf16[240,128]{1,0:T(8,128)(2,1)S(1)}, bf16[240,128]{1,0:T(8,128)(2,1)S(1)}, u32[]{:S(2)}, u32[]{:S(2)}) collective-permute-start(bf16[240,128]{1,0:T(8,128)(2,1)S(1)} %get-tuple-element.38), channel_id=1, source_target_pairs={{0,16},{1,17},{2,18},{3,19},{4,7},{5,6},{6,5},{7,4},{8,24},{9,25},... | collective-permute-start | bytes 184328 | tf_op jit(solution)/shard_map/ppermute | solution.py:480
  29.0 4.9 %collective-permute-start.10 = (bf16[240,128]{1,0:T(8,128)(2,1)S(1)}, bf16[240,128]{1,0:T(8,128)(2,1)S(1)}, u32[]{:S(2)}, u32[]{:S(2)}) collective-permute-start(bf16[240,128]{1,0:T(8,128)(2,1)S(1)} %get-tuple-element.39), channel_id=1, source_target_pairs={{0,8},{1,9},{2,10},{3,11},{4,5},{5,4},{6,7},{7,6},{8,0},{9,1},{10,... | collective-permute-start | bytes 184328 | tf_op jit(solution)/shard_map/ppermute | solution.py:480

commit v6 on v4

--- a/solution.py
+++ b/solution.py
@@ -17,7 +17,7 @@
 SUB = 8
 PAD = 8
 HOP = 9
-FIRST = ((0, 0), (3, 2), (1, 1), (2, 3))
+FIRST = ((0, 0), (3, 2), (2, 3), (1, 1))
 VMEM_BYTES = 14 * 1024 * 1024
 
 

time: 34.9 us -> 34.9 us (level)
  transfers between devices with their start and end apart: 11 -> 11, of which waited for: 5 -> 6; matrix products, arithmetic and copies ran while one was open for 0% -> 0% of each run, Pallas kernels for 28% -> 28%
where the time goes in v6:
time: 34.9 us; the launch traced here: 34.7 us
  starting transfers between devices  12.8 us (37%)
  Pallas kernels  11.6 us (33%)
  waiting for transfers between devices  8.18 us (23%)
  local copies, waits for them, and re-layouts  1.4 us (4%)
  between operations  0.76 us (2%)
    ppermute x6, starting transfers between devices, exchange(): return lax.ppermute(array, ('seq', 'dp'), pairs)  8.01 us
    ppermute x6, waiting for transfers between devices, exchange(): return lax.ppermute(array, ('seq', 'dp'), pairs)  7.59 us
    ppermute x1, starting transfers between devices, on_device(): got_a = lax.ppermute(send_a, 'seq', near_pairs())  3.27 us
    pallas_call x1, Pallas kernels, project(): pl.pallas_call(project_kernel, out_shape=[shape((feats // LANES, batch, p...  3 us
    pallas_call x1, Pallas kernels, input_gradient(): pl.pallas_call(input_kernel, out_shape=[jax.ShapeDtypeStruct((batch, rows...  2.33 us
    pallas_call x1, Pallas kernels, late(): pl.pallas_call(functools.partial(late_kernel, col), out_shape=[shape((bat...  2.32 us
    unnamed x8, local copies, waits for them, and re-layouts  1.35 us
    pallas_call x1, Pallas kernels, own(): pl.pallas_call(own_kernel, out_shape=[shape((2 * half, strip, x.shape[2])...  1.01 us
  transfers between devices with their start and end apart: 11, of which 6 were waited for; matrix products, arithmetic and copies ran while one was open for 0% of the time, Pallas kernels for 28%

profile of v6, /device:TPU:0, one launch (start us, length us, event | category | flops | bytes accessed | tf_op | source)
XLA Modules:
  0.0 34.7 jit_solution(8464694929306691611)
XLA Ops:
  0.6 0.5 %collective-permute-start = (bf16[2,256,768]{2,1,0:T(8,128)(2,1)}, bf16[2,256,768]{2,1,0:T(8,128)(2,1)S(1)}, u32[]{:S(2)}, u32[]{:S(2)}) collective-permute-start(bf16[2,256,768]{2,1,0:T(8,128)(2,1)} %x_ref.7), channel_id=1, source_target_pairs={{0,4},{4,0},{8,12},{12,8},{16,20},{20,16},{24,28},{28,24},{1,5},{5... | collective-permute-start | bytes 2359304 | tf_op jit(solution)/shard_map/ppermute | solution.py:506
  1.1 0.1 collective-permute-start.1
  1.2 1.0 %edges.1.far_ref = bf16[4,2048]{1,0:T(4,128)(2,1)S(1)} custom-call(bf16[2,256,768]{2,1,0:T(8,128)(2,1)} %x_ref.7, bf16[2,256,1280]{2,1,0:T(8,128)(2,1)} %u_ref.7), custom_call_target="tpu_custom_call" | custom-call | bytes 1000 | tf_op jit(solution)/shard_map/edges/pallas_call | solution.py:66
  2.2 0.0 copy-start
  2.2 0.0 copy-start.1
  2.2 0.0 copy-start.2
  2.2 0.0 copy-start.3
  2.3 0.8 %collective-permute-start.2 = (bf16[4,2048]{1,0:T(4,128)(2,1)S(1)}, bf16[4,2048]{1,0:T(4,128)(2,1)S(1)}, u32[]{:S(2)}, u32[]{:S(2)}) collective-permute-start(bf16[4,2048]{1,0:T(4,128)(2,1)S(1)} %relay.1), channel_id=1, source_target_pairs={{4,8},{8,4},{12,16},{16,12},{20,24},{24,20},{5,9},{9,5},{13,17},{1... | collective-permute-start | bytes 49160 | tf_op jit(solution)/shard_map/ppermute | solution.py:508
  3.1 0.5 %copy-done = bf16[2,256,1280]{2,1,0:T(8,128)(2,1)S(1)} copy-done((bf16[2,256,1280]{2,1,0:T(8,128)(2,1)S(1)}, bf16[2,256,1280]{2,1,0:T(8,128)(2,1)}, u32[]{:S(2)}) %copy-start) | copy-done | bytes 1310744
  3.5 0.2 copy-done.1
  3.7 0.7 %copy-done.2 = bf16[768,1280]{1,0:T(8,128)(2,1)S(1)} copy-done((bf16[768,1280]{1,0:T(8,128)(2,1)S(1)}, bf16[768,1280]{1,0:T(8,128)(2,1)}, u32[]{:S(2)}) %copy-start.2) | copy-done | bytes 1966104
  4.4 0.0 copy-done.3
  4.4 3.0 %project.1 = (f32[10,2,352,128]{3,2,1,0:T(8,128)S(1)}, bf16[2,256,640]{2,1,0:T(8,128)(2,1)S(1)}) custom-call(bf16[2,256,768]{2,1,0:T(8,128)(2,1)S(1)} %copy-done.1, bf16[768,1280]{1,0:T(8,128)(2,1)S(1)} %copy-done.2, bf16[2,256,1280]{2,1,0:T(8,128)(2,1)S(1)} %copy-done, f32[3,1280]{1,0:T(4,128)S(1)} %copy-done.3), custom_call_target="tpu_custom_call" | custom-call | flops 4000000000 | bytes 4000000 | tf_op jit(solution)/shard_map/project/pallas_call | solution.py:178
  7.4 0.0 collective-permute-done.2.far_ref
  7.4 0.0 collective-permute-done.pair_x.other_ref
  7.4 0.0 collective-permute-done.1.pair_u
  7.4 0.6 %early.1 = (bf16[2,256,640]{2,1,0:T(8,128)(2,1)S(1)}, f32[2,8,1280]{2,1,0:T(8,128)S(1)}, f32[2,8,1280]{2,1,0:T(8,128)S(1)}, bf16[2,160,512]{2,1,0:T(8,128)(2,1)S(1)}, bf16[2,160,512]{2,1,0:T(8,128)(2,1)S(1)}) custom-call(bf16[2,256,768]{2,1,0:T(8,128)(2,1)S(1)} %copy-done.1, bf16[768,1280]{1,0:T(8,128)(2,1)S(1)} %copy-done.2, ...), custom_call_target="tpu_custom_call" | custom-call | flops 1000000000 | bytes 4000000 | tf_op jit(solution)/shard_map/early/pallas_call | solution.py:290
  8.0 3.3 %collective-permute-start.4 = (bf16[2,160,512]{2,1,0:T(8,128)(2,1)S(1)}, bf16[2,160,512]{2,1,0:T(8,128)(2,1)S(1)}, u32[]{:S(2)}, u32[]{:S(2)}) collective-permute-start(bf16[2,160,512]{2,1,0:T(8,128)(2,1)S(1)} %get-tuple-element.31), channel_id=1, source_target_pairs={{0,4},{4,0},{8,12},{12,8},{16,20},{20,16},{24,28},{28,24},{1,5},{5... | collective-permute-start | bytes 983048 | tf_op jit(solution)/shard_map/ppermute | solution.py:513
  11.3 2.3 %late.1 = (bf16[2,256,640]{2,1,0:T(8,128)(2,1)S(1)}, bf16[2,160,512]{2,1,0:T(8,128)(2,1)S(1)}, bf16[2,160,512]{2,1,0:T(8,128)(2,1)S(1)}) custom-call(bf16[2,256,1280]{2,1,0:T(8,128)(2,1)S(1)} %copy-done, f32[3,1280]{1,0:T(4,128)S(1)} %copy-done.3, f32[10,2,352,128]{3,2,1,0:T(8,128)S(1)} %get-tuple-element.21.proj, ...), custom_call_target="tpu_custom_call" | custom-call | flops 4000000000 | bytes 4000000 | tf_op jit(solution)/shard_map/late/pallas_call | solution.py:305
  13.6 0.1 collective-permute-start.3
  13.7 0.0 collective-permute-done.4.got_a
  13.7 1.0 %own.1 = (f32[4,160,768]{2,1,0:T(8,128)S(1)}, bf16[4,4,240,128]{3,2,1,0:T(8,128)(2,1)S(1)}) custom-call(bf16[2,256,768]{2,1,0:T(8,128)(2,1)S(1)} %copy-done.1, bf16[2,256,768]{2,1,0:T(8,128)(2,1)S(1)} %collective-permute-done.pair_x.other_ref, bf16[2,160,512]{2,1,0:T(8,128)(2,1)S(1)} %get-tuple-element.29.mine_a, ...), custom_call_target="tpu_custom_call" | custom-call | flops 1000000000 | bytes 4000000 | tf_op jit(solution)/shard_map/own/pallas_call | solution.py:360
  14.7 0.6 %collective-permute-done.3.got_b = bf16[2,160,512]{2,1,0:T(8,128)(2,1)S(1)} collective-permute-done((bf16[2,160,512]{2,1,0:T(8,128)(2,1)S(1)}, bf16[2,160,512]{2,1,0:T(8,128)(2,1)S(1)}, u32[]{:S(2)}, u32[]{:S(2)}) %collective-permute-start.3) | collective-permute-done | bytes 327712 | tf_op jit(solution)/shard_map/ppermute | solution.py:515
  15.3 0.5 %pack.1 = (f32[4,160,768]{2,1,0:T(8,128)S(1)}, bf16[4,4,240,128]{3,2,1,0:T(8,128)(2,1)S(1)}) custom-call(bf16[2,256,768]{2,1,0:T(8,128)(2,1)S(1)} %collective-permute-done.pair_x.other_ref, bf16[2,160,512]{2,1,0:T(8,128)(2,1)S(1)} %collective-permute-done.3.got_b, ...), custom_call_target="tpu_custom_call", output_to_operand_aliasing={{0}: (2, {}), {1}: (3, {})} | custom-call | tf_op jit(solution)/shard_map/pack/pallas_call | solution.py:380
  15.8 0.1 slice_bitcast_fusion
  15.9 2.5 %collective-permute-start.7 = (bf16[4,240,128]{2,1,0:T(8,128)(2,1)S(1)}, bf16[4,240,128]{2,1,0:T(8,128)(2,1)S(1)}, u32[]{:S(2)}, u32[]{:S(2)}) collective-permute-start(bf16[4,240,128]{2,1,0:T(8,128)(2,1)S(1)} %get-tuple-element.40), channel_id=1, source_target_pairs={{0,3},{1,2},{2,1},{3,0},{4,20},{5,21},{6,22},{7,23},{8,11},{9,10},... | collective-permute-start | bytes 737288 | tf_op jit(solution)/shard_map/ppermute | solution.py:480
  18.4 0.5 %collective-permute-start.6 = (bf16[4,240,128]{2,1,0:T(8,128)(2,1)S(1)}, bf16[4,240,128]{2,1,0:T(8,128)(2,1)S(1)}, u32[]{:S(2)}, u32[]{:S(2)}) collective-permute-start(bf16[4,240,128]{2,1,0:T(8,128)(2,1)S(1)} %get-tuple-element.41), channel_id=1, source_target_pairs={{0,2},{1,3},{2,0},{3,1},{4,28},{5,29},{6,30},{7,31},{8,10},{9,11},... | collective-permute-start | bytes 737288 | tf_op jit(solution)/shard_map/ppermute | solution.py:480
  18.9 0.5 %collective-permute-start.5 = (bf16[4,240,128]{2,1,0:T(8,128)(2,1)S(1)}, bf16[4,240,128]{2,1,0:T(8,128)(2,1)S(1)}, u32[]{:S(2)}, u32[]{:S(2)}) collective-permute-start(bf16[4,240,128]{2,1,0:T(8,128)(2,1)S(1)} %get-tuple-element.42), channel_id=1, source_target_pairs={{0,1},{1,0},{2,3},{3,2},{4,12},{5,13},{6,14},{7,15},{8,9},{9,8},{1... | collective-permute-start | bytes 737288 | tf_op jit(solution)/shard_map/ppermute | solution.py:480
  19.5 2.3 %input_gradient.1 = (bf16[2,256,768]{2,1,0:T(8,128)(2,1)}, f32[8,128]{1,0:T(8,128)S(1)}) custom-call(bf16[2,256,640]{2,1,0:T(8,128)(2,1)S(1)} %get-tuple-element.23.gp_a, bf16[2,256,640]{2,1,0:T(8,128)(2,1)S(1)} %get-tuple-element.26.gp_b, bf16[768,1280]{1,0:T(8,128)(2,1)S(1)} %copy-done.2), custom_call_target="tpu_custom_call" | custom-call | flops 2000000000 | bytes 1000000 | tf_op jit(solution)/shard_map/input_gradient/pallas_call | solution.py:423
  21.8 1.4 %collective-permute-done.7.three_ref = bf16[4,240,128]{2,1,0:T(8,128)(2,1)S(1)} collective-permute-done((bf16[4,240,128]{2,1,0:T(8,128)(2,1)S(1)}, bf16[4,240,128]{2,1,0:T(8,128)(2,1)S(1)}, u32[]{:S(2)}, u32[]{:S(2)}) %collective-permute-start.7) | collective-permute-done | bytes 245792 | tf_op jit(solution)/shard_map/ppermute | solution.py:480
  23.2 2.5 %collective-permute-done.6.two_ref = bf16[4,240,128]{2,1,0:T(8,128)(2,1)S(1)} collective-permute-done((bf16[4,240,128]{2,1,0:T(8,128)(2,1)S(1)}, bf16[4,240,128]{2,1,0:T(8,128)(2,1)S(1)}, u32[]{:S(2)}, u32[]{:S(2)}) %collective-permute-start.6) | collective-permute-done | bytes 245792 | tf_op jit(solution)/shard_map/ppermute | solution.py:480
  25.7 0.1 collective-permute-done.5.one_ref
  25.8 0.1 fold.1
  25.9 2.2 %collective-permute-start.8 = (bf16[240,128]{1,0:T(8,128)(2,1)S(1)}, bf16[240,128]{1,0:T(8,128)(2,1)S(1)}, u32[]{:S(2)}, u32[]{:S(2)}) collective-permute-start(bf16[240,128]{1,0:T(8,128)(2,1)S(1)} %get-tuple-element.37), channel_id=1, source_target_pairs={{0,24},{1,25},{2,26},{3,27},{4,7},{5,6},{6,5},{7,4},{8,16},{9,17},... | collective-permute-start | bytes 184328 | tf_op jit(solution)/shard_map/ppermute | solution.py:480
  28.2 0.9 %collective-permute-start.9 = (bf16[240,128]{1,0:T(8,128)(2,1)S(1)}, bf16[240,128]{1,0:T(8,128)(2,1)S(1)}, u32[]{:S(2)}, u32[]{:S(2)}) collective-permute-start(bf16[240,128]{1,0:T(8,128)(2,1)S(1)} %get-tuple-element.38), channel_id=1, source_target_pairs={{0,16},{1,17},{2,18},{3,19},{4,6},{5,7},{6,4},{7,5},{8,24},{9,25},... | collective-permute-start | bytes 184328 | tf_op jit(solution)/shard_map/ppermute | solution.py:480
  29.0 1.3 %collective-permute-start.10 = (bf16[240,128]{1,0:T(8,128)(2,1)S(1)}, bf16[240,128]{1,0:T(8,128)(2,1)S(1)}, u32[]{:S(2)}, u32[]{:S(2)}) collective-permute-start(bf16[240,128]{1,0:T(8,128)(2,1)S(1)} %get-tuple-element.39), channel_id=1, source_target_pairs={{0,8},{1,9},{2,10},{3,11},{4,5},{5,4},{6,7},{7,6},{8,0},{9,1},{10,... | collective-permute-start | bytes 184328 | tf_op jit(solution)/shard_map/ppermute | solution.py:480
  30.4 1.6 %collective-permute-done.8.one_ref = bf16[240,128]{1,0:T(8,128)(2,1)S(1)} collective-permute-done((bf16[240,128]{1,0:T(8,128)(2,1)S(1)}, bf16[240,128]{1,0:T(8,128)(2,1)S(1)}, u32[]{:S(2)}, u32[]{:S(2)}) %collective-permute-start.8) | collective-permute-done | bytes 61472 | tf_op jit(solution)/shard_map/ppermute | solution.py:480
  32.0 1.9 %collective-permute-done.9.two_ref = bf16[240,128]{1,0:T(8,128)(2,1)S(1)} collective-permute-done((bf16[240,128]{1,0:T(8,128)(2,1)S(1)}, bf16[240,128]{1,0:T(8,128)(2,1)S(1)}, u32[]{:S(2)}, u32[]{:S(2)}) %collective-permute-start.9) | collective-permute-done | bytes 61472 | tf_op jit(solution)/shard_map/ppermute | solution.py:480
  34.0 0.0 collective-permute-done.10.three_ref
  34.0 0.8 %last.1 = f32[160,192]{1,0:T(8,128)} custom-call(f32[240,128]{1,0:T(8,128)S(1)} %get-tuple-element.36.own_ref, bf16[240,128]{1,0:T(8,128)(2,1)S(1)} %collective-permute-done.8.one_ref, bf16[240,128]{1,0:T(8,128)(2,1)S(1)} %collective-permute-done.9.two_ref, bf16[240,128]{1,0:T(8,128)(2,1)S(1)} %collective-permute-done.10.three_ref), custom_call_target="tpu_custom_call" | custom-call | tf_op jit(solution)/shard_map/last/pallas_call | solution.py:456
  (1 shorter events, 0.0 us)
Async XLA Ops:
  0.6 6.8 %collective-permute-start = (bf16[2,256,768]{2,1,0:T(8,128)(2,1)}, bf16[2,256,768]{2,1,0:T(8,128)(2,1)S(1)}, u32[]{:S(2)}, u32[]{:S(2)}) collective-permute-start(bf16[2,256,768]{2,1,0:T(8,128)(2,1)} %x_ref.7), channel_id=1, source_target_pairs={{0,4},{4,0},{8,12},{12,8},{16,20},{20,16},{24,28},{28,24},{1,5},{5... | collective-permute-start | bytes 2359304 | tf_op jit(solution)/shard_map/ppermute | solution.py:506
  1.1 6.3 %collective-permute-start.1 = (bf16[2,256,1280]{2,1,0:T(8,128)(2,1)}, bf16[2,256,1280]{2,1,0:T(8,128)(2,1)S(1)}, u32[]{:S(2)}, u32[]{:S(2)}) collective-permute-start(bf16[2,256,1280]{2,1,0:T(8,128)(2,1)} %u_ref.7), channel_id=1, source_target_pairs={{0,4},{4,0},{8,12},{12,8},{16,20},{20,16},{24,28},{28,24},{1,5},{5... | collective-permute-start | bytes 3932168 | tf_op jit(solution)/shard_map/ppermute | solution.py:507
  2.2 1.3 %copy-start = (bf16[2,256,1280]{2,1,0:T(8,128)(2,1)S(1)}, bf16[2,256,1280]{2,1,0:T(8,128)(2,1)}, u32[]{:S(2)}) copy-start(bf16[2,256,1280]{2,1,0:T(8,128)(2,1)} %u_ref.7) | copy-start | bytes 3932164
  2.2 1.5 %copy-start.1 = (bf16[2,256,768]{2,1,0:T(8,128)(2,1)S(1)}, bf16[2,256,768]{2,1,0:T(8,128)(2,1)}, u32[]{:S(2)}) copy-start(bf16[2,256,768]{2,1,0:T(8,128)(2,1)} %x_ref.7) | copy-start | bytes 2359300
  2.2 2.2 %copy-start.2 = (bf16[768,1280]{1,0:T(8,128)(2,1)S(1)}, bf16[768,1280]{1,0:T(8,128)(2,1)}, u32[]{:S(2)}) copy-start(bf16[768,1280]{1,0:T(8,128)(2,1)} %w_ref.5) | copy-start | bytes 5898244
  2.2 2.2 %copy-start.3 = (f32[3,1280]{1,0:T(4,128)S(1)}, f32[3,1280]{1,0:T(4,128)}, u32[]{:S(2)}) copy-start(f32[3,1280]{1,0:T(4,128)} %k_ref.5) | copy-start | bytes 46084
  2.3 5.1 %collective-permute-start.2 = (bf16[4,2048]{1,0:T(4,128)(2,1)S(1)}, bf16[4,2048]{1,0:T(4,128)(2,1)S(1)}, u32[]{:S(2)}, u32[]{:S(2)}) collective-permute-start(bf16[4,2048]{1,0:T(4,128)(2,1)S(1)} %relay.1), channel_id=1, source_target_pairs={{4,8},{8,4},{12,16},{16,12},{20,24},{24,20},{5,9},{9,5},{13,17},{1... | collective-permute-start | bytes 49160 | tf_op jit(solution)/shard_map/ppermute | solution.py:508
  8.0 5.7 %collective-permute-start.4 = (bf16[2,160,512]{2,1,0:T(8,128)(2,1)S(1)}, bf16[2,160,512]{2,1,0:T(8,128)(2,1)S(1)}, u32[]{:S(2)}, u32[]{:S(2)}) collective-permute-start(bf16[2,160,512]{2,1,0:T(8,128)(2,1)S(1)} %get-tuple-element.31), channel_id=1, source_target_pairs={{0,4},{4,0},{8,12},{12,8},{16,20},{20,16},{24,28},{28,24},{1,5},{5... | collective-permute-start | bytes 983048 | tf_op jit(solution)/shard_map/ppermute | solution.py:513
  13.6 1.7 %collective-permute-start.3 = (bf16[2,160,512]{2,1,0:T(8,128)(2,1)S(1)}, bf16[2,160,512]{2,1,0:T(8,128)(2,1)S(1)}, u32[]{:S(2)}, u32[]{:S(2)}) collective-permute-start(bf16[2,160,512]{2,1,0:T(8,128)(2,1)S(1)} %get-tuple-element.28), channel_id=1, source_target_pairs={{0,4},{4,0},{8,12},{12,8},{16,20},{20,16},{24,28},{28,24},{1,5},{5... | collective-permute-start | bytes 983048 | tf_op jit(solution)/shard_map/ppermute | solution.py:515
  15.9 7.3 %collective-permute-start.7 = (bf16[4,240,128]{2,1,0:T(8,128)(2,1)S(1)}, bf16[4,240,128]{2,1,0:T(8,128)(2,1)S(1)}, u32[]{:S(2)}, u32[]{:S(2)}) collective-permute-start(bf16[4,240,128]{2,1,0:T(8,128)(2,1)S(1)} %get-tuple-element.40), channel_id=1, source_target_pairs={{0,3},{1,2},{2,1},{3,0},{4,20},{5,21},{6,22},{7,23},{8,11},{9,10},... | collective-permute-start | bytes 737288 | tf_op jit(solution)/shard_map/ppermute | solution.py:480
  18.4 7.3 %collective-permute-start.6 = (bf16[4,240,128]{2,1,0:T(8,128)(2,1)S(1)}, bf16[4,240,128]{2,1,0:T(8,128)(2,1)S(1)}, u32[]{:S(2)}, u32[]{:S(2)}) collective-permute-start(bf16[4,240,128]{2,1,0:T(8,128)(2,1)S(1)} %get-tuple-element.41), channel_id=1, source_target_pairs={{0,2},{1,3},{2,0},{3,1},{4,28},{5,29},{6,30},{7,31},{8,10},{9,11},... | collective-permute-start | bytes 737288 | tf_op jit(solution)/shard_map/ppermute | solution.py:480
  18.9 6.9 %collective-permute-start.5 = (bf16[4,240,128]{2,1,0:T(8,128)(2,1)S(1)}, bf16[4,240,128]{2,1,0:T(8,128)(2,1)S(1)}, u32[]{:S(2)}, u32[]{:S(2)}) collective-permute-start(bf16[4,240,128]{2,1,0:T(8,128)(2,1)S(1)} %get-tuple-element.42), channel_id=1, source_target_pairs={{0,1},{1,0},{2,3},{3,2},{4,12},{5,13},{6,14},{7,15},{8,9},{9,8},{1... | collective-permute-start | bytes 737288 | tf_op jit(solution)/shard_map/ppermute | solution.py:480
  25.9 6.1 %collective-permute-start.8 = (bf16[240,128]{1,0:T(8,128)(2,1)S(1)}, bf16[240,128]{1,0:T(8,128)(2,1)S(1)}, u32[]{:S(2)}, u32[]{:S(2)}) collective-permute-start(bf16[240,128]{1,0:T(8,128)(2,1)S(1)} %get-tuple-element.37), channel_id=1, source_target_pairs={{0,24},{1,25},{2,26},{3,27},{4,7},{5,6},{6,5},{7,4},{8,16},{9,17},... | collective-permute-start | bytes 184328 | tf_op jit(solution)/shard_map/ppermute | solution.py:480
  28.2 5.8 %collective-permute-start.9 = (bf16[240,128]{1,0:T(8,128)(2,1)S(1)}, bf16[240,128]{1,0:T(8,128)(2,1)S(1)}, u32[]{:S(2)}, u32[]{:S(2)}) collective-permute-start(bf16[240,128]{1,0:T(8,128)(2,1)S(1)} %get-tuple-element.38), channel_id=1, source_target_pairs={{0,16},{1,17},{2,18},{3,19},{4,6},{5,7},{6,4},{7,5},{8,24},{9,25},... | collective-permute-start | bytes 184328 | tf_op jit(solution)/shard_map/ppermute | solution.py:480
  29.0 4.9 %collective-permute-start.10 = (bf16[240,128]{1,0:T(8,128)(2,1)S(1)}, bf16[240,128]{1,0:T(8,128)(2,1)S(1)}, u32[]{:S(2)}, u32[]{:S(2)}) collective-permute-start(bf16[240,128]{1,0:T(8,128)(2,1)S(1)} %get-tuple-element.39), channel_id=1, source_target_pairs={{0,8},{1,9},{2,10},{3,11},{4,5},{5,4},{6,7},{7,6},{8,0},{9,1},{10,... | collective-permute-start | bytes 184328 | tf_op jit(solution)/shard_map/ppermute | solution.py:480
